TPU v7x, 32 devices: a whole 2x2x4 slice. The times are simulated.
32 devices in a mesh: fact: 4 (over x, core), dim: 8 (over z, y).
Axes of the slice: x: 2, y: 2, z: 4, core: 2. Of those that a mesh axis runs over, the one named last changes fastest.
Arguments:
- queries: bfloat16 [8192, 1024], P(('fact', 'dim')), may hold values from -6 to 6
- key_rows: bfloat16 [8192, 1024], P('dim'), may hold values from -6 to 6
- value_rows: bfloat16 [8192, 1024], P('dim'), may hold values from -6 to 6
- cotangent: bfloat16 [8192, 1024], P(('fact', 'dim')), may hold values from -6 to 6
- block_lists: int32 [64, 8], P(('fact', 'dim')), may hold values from 0 to 63, as said below
- tile_lengths: int32 [64], P(('fact', 'dim')), may hold values from 1 to 8, as said below
Outputs:
- attended: bfloat16 [8192, 1024], P(('fact', 'dim'))
- query_grad: bfloat16 [8192, 1024], P(('fact', 'dim'))
- key_grad: bfloat16 [8192, 1024], P('dim', 'fact')
- value_grad: bfloat16 [8192, 1024], P('dim', 'fact')
Inputs may be any that keep to these rules, and one draw needn't show every extreme that they name: Rows of block_lists come in aligned groups of 2 rows. The entries of one row lie in different ranges [o * 8, (o + 1) * 8). Within one group, all entries that lie in one such range are the same block. Within each aligned run of 8 groups, the first entries of all rows lie in one common range. Only the first tile_lengths[t] entries of row t of block_lists are used.
All inputs are finite; a program needn't handle non-finite values.
Results may differ from a plain program's by a relative error of at most 0.0056.
Values may be sent and summed in bfloat16 or wider, within the bound.
No kernel may reach another device: no remote copies, remote signals or barrier semaphores. Data moves between devices by JAX's collectives and lax.ppermute only.
A program may use at most 192 MiB of HBM per device.

v0:
```python
import jax
import jax.numpy as jnp
from jax import lax
from jax.sharding import PartitionSpec as P

HEADS = 16
HEAD_DIM = 64
TILE = 128


NEG_FILL = -1e30


def attend_group(query_group, grad_group, key_group, value_group, alive_keys):
    scale = HEAD_DIM ** (-0.5)
    scores = (
        jnp.einsum("tqhe,tkhe->thqk", query_group, key_group, preferred_element_type=jnp.float32)
        * scale
    )
    scores = jnp.where(alive_keys[:, None, None, :], scores, NEG_FILL)
    row_max = jnp.max(scores, axis=-1, keepdims=True)
    expo_terms = jnp.exp(scores - row_max)
    weights = expo_terms / jnp.sum(expo_terms, axis=-1, keepdims=True)
    weights_low = weights.astype(jnp.bfloat16)
    attended = jnp.einsum(
        "thqk,tkhe->tqhe", weights_low, value_group, preferred_element_type=jnp.float32
    )
    dweights = jnp.einsum(
        "tqhe,tkhe->thqk", grad_group, value_group, preferred_element_type=jnp.float32
    )
    row_delta = jnp.sum(weights * dweights, axis=-1, keepdims=True)
    dscores = (weights * (dweights - row_delta)).astype(jnp.bfloat16)
    query_grad = (
        jnp.einsum("thqk,tkhe->tqhe", dscores, key_group, preferred_element_type=jnp.float32)
        * scale
    )
    key_grad = (
        jnp.einsum("thqk,tqhe->tkhe", dscores, query_group, preferred_element_type=jnp.float32)
        * scale
    )
    value_grad = jnp.einsum(
        "thqk,tqhe->tkhe", weights_low, grad_group, preferred_element_type=jnp.float32
    )
    return (attended, query_grad, key_grad, value_grad)


def body(queries, key_rows, value_rows, cotangent, block_lists, tile_lengths):
    owners = lax.axis_size("dim")
    tile_count = block_lists.shape[0]
    slot_count = block_lists.shape[1]
    blocks_here = key_rows.shape[0] // TILE
    model_width = key_rows.shape[1]
    head_size = HEAD_DIM
    half_heads = HEADS // 2
    alive_slots = jnp.arange(slot_count, dtype=jnp.int32)[None, :] < tile_lengths[:, None]
    owner_of = block_lists // blocks_here
    local_of = block_lists % blocks_here
    owner_ids = jnp.arange(owners, dtype=jnp.int32)
    matched = (owner_of[:, :, None] == owner_ids[None, None, :]) & alive_slots[:, :, None]
    wanted = jnp.max(jnp.where(matched, local_of[:, :, None], -1), axis=(0, 1))
    requests = lax.all_to_all(
        wanted.reshape(owners, 1), "dim", split_axis=0, concat_axis=0, tiled=True
    )
    block_ids = jnp.arange(blocks_here, dtype=jnp.int32)[None, :]
    slot_selector = (requests == block_ids).astype(jnp.bfloat16)
    gathered_key_blocks = key_rows.reshape(blocks_here, TILE, model_width)
    gathered_value_blocks = value_rows.reshape(blocks_here, TILE, model_width)
    reply_keys = jnp.einsum(
        "nh,hcm->ncm", slot_selector, gathered_key_blocks, preferred_element_type=jnp.float32
    ).astype(jnp.bfloat16)
    reply_values = jnp.einsum(
        "nh,hcm->ncm", slot_selector, gathered_value_blocks, preferred_element_type=jnp.float32
    ).astype(jnp.bfloat16)
    fetched_keys, fetched_values = (
        lax.all_to_all(reply_keys, "dim", split_axis=0, concat_axis=0, tiled=True),
        lax.all_to_all(reply_values, "dim", split_axis=0, concat_axis=0, tiled=True),
    )
    per_step = min(4, tile_count)
    step_count = tile_count // per_step
    query_steps = queries.reshape(step_count, per_step, TILE, model_width)
    grad_steps = cotangent.reshape(step_count, per_step, TILE, model_width)
    owner_steps = owner_of.reshape(step_count, per_step, slot_count)
    alive_steps = alive_slots.reshape(step_count, per_step, slot_count)
    match_steps = matched.astype(jnp.float32).reshape(step_count, per_step, slot_count, owners)
    span = half_heads * head_size

    def one_group(totals, inputs_step):
        key_total, value_total = totals
        query_block, grad_block, owner_step, alive_step, match_step = inputs_step
        key_group = fetched_keys[owner_step]
        value_group = fetched_values[owner_step]
        alive_keys = jnp.repeat(alive_step, TILE, axis=1)
        attended_parts = []
        query_parts = []
        key_parts = []
        value_parts = []
        for portion in range(2):
            start = portion * span
            query_half = query_block[..., start : start + span].reshape(
                per_step, TILE, half_heads, head_size
            )
            grad_half = grad_block[..., start : start + span].reshape(
                per_step, TILE, half_heads, head_size
            )
            key_half = key_group[..., start : start + span].reshape(
                per_step, slot_count * TILE, half_heads, head_size
            )
            value_half = value_group[..., start : start + span].reshape(
                per_step, slot_count * TILE, half_heads, head_size
            )
            attended, query_grad, key_grad, value_grad = attend_group(
                query_half, grad_half, key_half, value_half, alive_keys
            )
            attended_parts.append(attended.reshape(per_step, TILE, span))
            query_parts.append(query_grad.reshape(per_step, TILE, span))
            key_parts.append(key_grad.reshape(per_step, slot_count, TILE, span))
            value_parts.append(value_grad.reshape(per_step, slot_count, TILE, span))
        key_full = jnp.concatenate(key_parts, axis=-1)
        value_full = jnp.concatenate(value_parts, axis=-1)
        key_total = key_total + jnp.einsum(
            "tjo,tjkd->okd", match_step, key_full, precision=lax.Precision.HIGHEST
        )
        value_total = value_total + jnp.einsum(
            "tjo,tjkd->okd", match_step, value_full, precision=lax.Precision.HIGHEST
        )
        attended_block = jnp.concatenate(attended_parts, axis=-1).astype(jnp.bfloat16)
        query_block_grad = jnp.concatenate(query_parts, axis=-1).astype(jnp.bfloat16)
        return ((key_total, value_total), (attended_block, query_block_grad))

    empty_total = jnp.zeros((owners, TILE, model_width), jnp.float32)
    (partial_keys, partial_values), (attended_all, query_grad_all) = lax.scan(
        one_group,
        (empty_total, empty_total),
        (query_steps, grad_steps, owner_steps, alive_steps, match_steps),
    )
    attended_out = attended_all.reshape(tile_count * TILE, model_width)
    query_grad_out = query_grad_all.reshape(tile_count * TILE, model_width)
    incoming_key_rows, incoming_value_rows = (
        lax.all_to_all(partial_keys, "dim", split_axis=0, concat_axis=0, tiled=True),
        lax.all_to_all(partial_values, "dim", split_axis=0, concat_axis=0, tiled=True),
    )
    block_selector = (requests == block_ids).astype(jnp.float32)
    reduced_key_grad = jnp.einsum(
        "ep,ejs->pjs", block_selector, incoming_key_rows, precision=lax.Precision.HIGHEST
    )
    summed_values = jnp.einsum(
        "ep,ejs->pjs", block_selector, incoming_value_rows, precision=lax.Precision.HIGHEST
    )
    key_grad_out, value_grad_out = (
        lax.psum_scatter(
            reduced_key_grad.reshape(blocks_here * TILE, model_width),
            "fact",
            scatter_dimension=1,
            tiled=True,
        ),
        lax.psum_scatter(
            summed_values.reshape(blocks_here * TILE, model_width),
            "fact",
            scatter_dimension=1,
            tiled=True,
        ),
    )
    return (
        attended_out,
        query_grad_out,
        key_grad_out.astype(jnp.bfloat16),
        value_grad_out.astype(jnp.bfloat16),
    )


def solution(mesh):
    in_specs = (
        P(("fact", "dim"), None),
        P("dim", None),
        P("dim", None),
        P(("fact", "dim"), None),
        P(("fact", "dim"), None),
        P(("fact", "dim")),
    )
    out_specs = (
        P(("fact", "dim"), None),
        P(("fact", "dim"), None),
        P("dim", "fact"),
        P("dim", "fact"),
    )
    return jax.shard_map(body, mesh=mesh, in_specs=in_specs, out_specs=out_specs, check_vma=False)
```

profile of v0, /device:TPU:0, one launch (start us, length us, event | category | flops | bytes accessed | tf_op | source)
XLA Modules:
  0.0 450.6 jit_solution(16996823080292400133)
XLA Ops:
  9.0 13.5 %all_to_all.29 = s32[8,1,1]{2,1,0:T(1,128)S(1)} all-to-all(s32[8,1,1]{2,1,0:T(1,128)S(1)} %copy.99), channel_id=1, replica_groups=mesh['fact'=4,'dim'=8] {'dim'}, dimensions={0} | all-to-all | bytes 64 | tf_op jit(solution)/shard_map/all_to_all | solution.py:61
  24.3 2.5 copy.106
  26.7 3.6 all-to-all-start.2
  32.4 2.9 fusion.52
  35.3 2.5 copy.102
  37.8 39.6 %all-to-all-done.2 = bf16[8,128,1024]{2,1,0:T(8,128)(2,1)S(1)} async-done(((bf16[8,128,1024]{2,1,0:T(8,128)(2,1)}), bf16[8,128,1024]{2,1,0:T(8,128)(2,1)S(1)}, u32[]{:S(2)}, u32[]{:S(2)}) %all-to-all-start.2) | async-done | bytes 2097184 | tf_op jit(solution)/shard_map/all_to_all | solution.py:75
  78.7 3.8 all-to-all-start.1
  82.5 4.3 gather_fusion.1
  86.8 4.6 %fusion.101 = (bf16[2,8,128,512]{3,2,1,0:T(8,128)(2,1)}, bf16[2,8,128,512]{3,2,1,0:T(8,128)(2,1)}) fusion(bf16[2,8,128,1024]{3,2,1,0:T(8,128)(2,1)} %bitcast.184), kind=kLoop, calls=%fused_computation.112 | loop fusion | bytes 8388608 | tf_op jit(solution)/shard_map/while/body/eval_jaxpr/slice | solution.py:105
  91.5 4.3 copy.153
  95.8 4.2 reshape.146
  100.0 4.3 copy.156
  104.3 4.2 reshape.149
  108.4 8.1 %fusion.105 = (f32[2,8,128]{2,1,0:T(8,128)S(1)}, f32[2,8,128,1024]{2,3,1,0:T(8,128)}) fusion(pred[2,1024]{1,0:T(4,128)(4,1)S(1)} %bitcast.208, bf16[2,1024,8,64]{1,3,2,0:T(8,128)(2,1)} %reshape.149, bf16[2,128,8,64]{1,3,2,0:T(8,128)(2,1)S(1)} %bitcast.196), kind=kOutput, calls=%fused_computation.116 | convolution fusion | flops 276825088 | bytes 10758144 | tf_op jit(solution)/shard_map/while/body/eval_jaxpr/sub | solution.py:22
  116.6 5.0 %fusion.44 = f32[2,8,1024,64]{2,3,1,0:T(8,128)S(1)} fusion(bf16[2,128,8,64]{1,3,2,0:T(8,128)(2,1)S(1)} %bitcast.206, f32[2,8,128,1024]{2,3,1,0:T(8,128)} %get-tuple-element.64, f32[2,8,128]{2,1,0:T(8,128)S(1)} %get-tuple-element.63), kind=kOutput, calls=%fused_computation.52 | convolution fusion | flops 272629760 | bytes 12853248 | tf_op jit(solution)/shard_map/while/body/eval_jaxpr/thqk,tqhe->tkhe/dot_general | solution.py:41
  121.5 2.9 copy.168
  124.5 5.8 %copy.132 = f32[2,8,128,512]{3,1,0,2:T(8,128)} copy(f32[2,8,128,512]{2,1,3,0:T(8,128)} %bitcast.185) | data formatting | bytes 8388608 | tf_op jit(solution)/shard_map/while/body/eval_jaxpr/reshape | solution.py:117
  130.3 8.1 %fusion.106 = (f32[2,8,128]{2,1,0:T(8,128)S(1)}, f32[2,8,128,1024]{2,3,1,0:T(8,128)}) fusion(pred[2,1024]{1,0:T(4,128)(4,1)S(1)} %bitcast.209, bf16[2,1024,8,64]{1,3,2,0:T(8,128)(2,1)} %reshape.146, bf16[2,128,8,64]{1,3,2,0:T(8,128)(2,1)S(1)} %bitcast.194), kind=kOutput, calls=%fused_computation.117 | convolution fusion | flops 276825088 | bytes 10758144 | tf_op jit(solution)/shard_map/while/body/eval_jaxpr/sub | solution.py:22
  138.4 5.0 %fusion.48 = f32[2,8,1024,64]{2,3,1,0:T(8,128)S(1)} fusion(bf16[2,128,8,64]{1,3,2,0:T(8,128)(2,1)S(1)} %bitcast.204, f32[2,8,128,1024]{2,3,1,0:T(8,128)} %get-tuple-element.66, f32[2,8,128]{2,1,0:T(8,128)S(1)} %get-tuple-element.65), kind=kOutput, calls=%fused_computation.56 | convolution fusion | flops 272629760 | bytes 12853248 | tf_op jit(solution)/shard_map/while/body/eval_jaxpr/thqk,tqhe->tkhe/dot_general | solution.py:41
  143.4 3.0 copy.167
  146.4 5.6 %copy.131 = f32[2,8,128,512]{3,1,0,2:T(8,128)} copy(f32[2,8,128,512]{2,1,3,0:T(8,128)} %bitcast.186) | data formatting | bytes 8388608 | tf_op jit(solution)/shard_map/while/body/eval_jaxpr/reshape | solution.py:117
  152.0 5.4 %fusion.34 = f32[8,128,1024]{2,0,1:T(8,128)S(1)} fusion(f32[2,8,128,512]{3,1,0,2:T(8,128)} %copy.132, f32[2,8,128,512]{3,1,0,2:T(8,128)} %copy.131, s32[2,8]{1,0:T(2,128)S(1)} %get-tuple-element.53, pred[2,8]{1,0:T(4,128)(4,1)S(1)} %iota_compare_fusion.2), kind=kOutput, calls=%fused_computation.44 | convolution fusion | flops 203424000 | bytes 12582992 | tf_op jit(solution)/shard_map/while/body/eval_jaxpr/tjo,tjkd->okd/dot_general | solution.py:123
  157.4 4.4 copy.133
  161.8 6.0 %all-to-all-start.4 = ((f32[8,128,1024]{2,1,0:T(8,128)}), f32[8,128,1024]{2,1,0:T(8,128)}, u32[]{:S(2)}, u32[]{:S(2)}) async-start(f32[8,128,1024]{2,1,0:T(8,128)} %copy.133), calls=%async_computation.5 | async-start | bytes 8388608 | tf_op jit(solution)/shard_map/all_to_all | solution.py:140
  167.8 2.7 gather_fusion
  170.6 4.6 %fusion.102 = (bf16[2,8,128,512]{3,2,1,0:T(8,128)(2,1)}, bf16[2,8,128,512]{3,2,1,0:T(8,128)(2,1)}) fusion(bf16[2,8,128,1024]{3,2,1,0:T(8,128)(2,1)} %bitcast.183), kind=kLoop, calls=%fused_computation.113 | loop fusion | bytes 8388608 | tf_op jit(solution)/shard_map/while/body/eval_jaxpr/slice | solution.py:108
  175.2 3.5 copy.152
  181.0 3.1 copy.155
  186.5 5.9 %fusion.10 = (f32[2,8,128]{2,1,0:T(8,128)S(1)}, f32[2,8,1024,128]{3,2,1,0:T(8,128)S(1)}) fusion(f32[2,8,128,1024]{2,3,1,0:T(8,128)} %get-tuple-element.64, f32[2,8,128]{2,1,0:T(8,128)S(1)} %get-tuple-element.63, bf16[2,1024,8,64]{1,3,2,0:T(8,128)(2,1)} %reshape.148, bf16[2,128,8,64]{1,3,2,0:T(8,128)(2,1)S(1)} %bitcast.207), kind=kOutput, calls=%fused_computation.14 | convolution fusion | flops 274724864 | bytes 19152896 | tf_op jit(solution)/shard_map/while/body/eval_jaxpr/tqhe,tkhe->thqk/dot_general | solution.py:28
  192.4 4.1 fusion.12
  198.5 2.9 copy.166
  201.4 5.8 %copy.125 = f32[2,8,128,512]{3,1,0,2:T(8,128)} copy(f32[2,8,128,512]{2,1,3,0:T(8,128)} %bitcast.188) | data formatting | bytes 8388608 | tf_op jit(solution)/shard_map/while/body/eval_jaxpr/reshape | solution.py:116
  207.2 5.2 %fusion.13 = (f32[2,8,128]{2,1,0:T(8,128)S(1)}, f32[2,8,1024,128]{3,2,1,0:T(8,128)S(1)}) fusion(f32[2,8,128,1024]{2,3,1,0:T(8,128)} %get-tuple-element.66, f32[2,8,128]{2,1,0:T(8,128)S(1)} %get-tuple-element.65, bf16[2,1024,8,64]{1,3,2,0:T(8,128)(2,1)S(1)} %copy-done.6, bf16[2,128,8,64]{1,3,2,0:T(8,128)(2,1)S(1)} %bitcast.205), kind=kOutput, calls=%fused_computation.19 | convolution fusion | flops 274724864 | bytes 19152896 | tf_op jit(solution)/shard_map/while/body/eval_jaxpr/tqhe,tkhe->thqk/dot_general | solution.py:28
  212.4 5.6 %fusion.15 = bf16[2,8,128,1024]{2,3,1,0:T(8,128)(2,1)} fusion(f32[2,8,1024,128]{3,2,1,0:T(8,128)S(1)} %get-tuple-element.70, f32[2,8,128]{2,1,0:T(8,128)S(1)} %get-tuple-element.69, f32[2,8,128,1024]{2,3,1,0:T(8,128)} %get-tuple-element.66, f32[2,8,128]{2,1,0:T(8,128)S(1)} %get-tuple-element.65), kind=kLoop, calls=%fused_computation.21 | loop fusion | flops 8388608 | bytes 20987904 | tf_op jit(solution)/shard_map/while/body/eval_jaxpr/convert_element_type | solution.py:32
  218.1 42.6 %all-to-all-done.4 = f32[8,128,1024]{2,1,0:T(8,128)} async-done(((f32[8,128,1024]{2,1,0:T(8,128)}), f32[8,128,1024]{2,1,0:T(8,128)}, u32[]{:S(2)}, u32[]{:S(2)}) %all-to-all-start.4) | async-done | bytes 4194336 | tf_op jit(solution)/shard_map/all_to_all | solution.py:140
  260.7 6.4 %fusion.24 = f32[8,128,1024]{2,0,1:T(8,128)S(1)} fusion(f32[8,128,1024]{2,1,0:T(8,128)} %all-to-all-done.4, s32[8]{0:T(128)S(1)} %reduce), kind=kOutput, calls=%fused_computation.32 | convolution fusion | flops 100663360 | bytes 8388640 | tf_op jit(solution)/shard_map/ep,ejs->pjs/dot_general | solution.py:146
  267.1 4.4 copy.135
  271.6 3.7 convolution_multiply_fusion.1
  275.3 3.0 copy.165
  278.3 5.9 %copy.124 = f32[2,8,128,512]{3,1,0,2:T(8,128)} copy(f32[2,8,128,512]{2,1,3,0:T(8,128)} %bitcast.190) | data formatting | bytes 8388608 | tf_op jit(solution)/shard_map/while/body/eval_jaxpr/reshape | solution.py:116
  284.2 5.4 %fusion.37 = f32[8,128,1024]{2,0,1:T(8,128)S(1)} fusion(f32[2,8,128,512]{3,1,0,2:T(8,128)} %copy.125, f32[2,8,128,512]{3,1,0,2:T(8,128)} %copy.124, s32[2,8]{1,0:T(2,128)S(1)} %get-tuple-element.53, pred[2,8]{1,0:T(4,128)(4,1)S(1)} %iota_compare_fusion.2), kind=kOutput, calls=%fused_computation.45 | convolution fusion | flops 203424000 | bytes 12582992 | tf_op jit(solution)/shard_map/while/body/eval_jaxpr/tjo,tjkd->okd/dot_general | solution.py:120
  292.1 96.9 %all_to_all.30 = f32[8,128,1024]{2,1,0:T(8,128)S(1)} all-to-all(f32[8,128,1024]{2,1,0:T(8,128)S(1)} %copy.126), channel_id=1, replica_groups=mesh['fact'=4,'dim'=8] {'dim'}, dimensions={0} | all-to-all | bytes 8388608 | tf_op jit(solution)/shard_map/all_to_all | solution.py:139
  389.0 4.3 fusion.26
  393.3 4.4 copy.128
  397.7 5.0 %fusion.66 = bf16[2,128,8,64]{1,3,2,0:T(8,128)(2,1)S(1)} fusion(bf16[2,1024,8,64]{1,3,2,0:T(8,128)(2,1)} %reshape.148, f32[2,8,128,1024]{2,3,1,0:T(8,128)} %get-tuple-element.64, f32[2,8,128]{2,1,0:T(8,128)S(1)} %get-tuple-element.63), kind=kOutput, calls=%fused_computation.68 | convolution fusion | flops 272760832 | bytes 10756096 | tf_op jit(solution)/shard_map/while/body/eval_jaxpr/thqk,tkhe->tqhe/dot_general | solution.py:25
  405.4 4.8 %fusion.69 = bf16[2,128,8,64]{1,3,2,0:T(8,128)(2,1)S(1)} fusion(bf16[2,1024,8,64]{1,3,2,0:T(8,128)(2,1)S(1)} %copy-done.7, f32[2,8,128,1024]{2,3,1,0:T(8,128)} %get-tuple-element.66, f32[2,8,128]{2,1,0:T(8,128)S(1)} %get-tuple-element.65), kind=kOutput, calls=%fused_computation.69 | convolution fusion | flops 272760832 | bytes 10756096 | tf_op jit(solution)/shard_map/while/body/eval_jaxpr/thqk,tkhe->tqhe/dot_general | solution.py:25
  411.7 3.8 fusion.73
  418.9 22.5 %reduce-scatter.3.cloned.1.call-done = f32[1024,256]{1,0:T(8,128)} async-done(((f32[1024,1024]{1,0:T(8,128)}), f32[1024,256]{1,0:T(8,128)}) %reduce-scatter.3.cloned.1.call-update) | async-done | bytes 1048592 | tf_op jit(solution)/shard_map/reduce_scatter | solution.py:150
  (57 shorter events, 25.5 us)
Async XLA Ops:
  7.2 15.6 %copy-start = (bf16[1024,1024]{1,0:T(8,128)(2,1)S(1)}, bf16[1024,1024]{1,0:T(8,128)(2,1)}, u32[]{:S(2)}) copy-start(bf16[1024,1024]{1,0:T(8,128)(2,1)} %param.7) | copy-start | bytes 6291460
  24.2 6.3 %copy-start.8 = (bf16[256,1024]{1,0:T(8,128)(2,1)S(1)}, bf16[256,1024]{1,0:T(8,128)(2,1)}, u32[]{:S(2)}) copy-start(bf16[256,1024]{1,0:T(8,128)(2,1)} %param.6) | copy-start | bytes 1572868
  26.7 50.6 %all-to-all-start.2 = ((bf16[8,128,1024]{2,1,0:T(8,128)(2,1)}), bf16[8,128,1024]{2,1,0:T(8,128)(2,1)S(1)}, u32[]{:S(2)}, u32[]{:S(2)}) async-start(bf16[8,128,1024]{2,1,0:T(8,128)(2,1)} %copy.106), calls=%async_computation.2 | async-start | bytes 4194304 | tf_op jit(solution)/shard_map/all_to_all | solution.py:75
  77.4 1.3 copy-start.4
  78.7 83.1 %all-to-all-start.1 = ((bf16[8,128,1024]{2,1,0:T(8,128)(2,1)}), bf16[8,128,1024]{2,1,0:T(8,128)(2,1)S(1)}, u32[]{:S(2)}, u32[]{:S(2)}) async-start(bf16[8,128,1024]{2,1,0:T(8,128)(2,1)} %copy.102), calls=%async_computation.1 | async-start | bytes 4194304 | tf_op jit(solution)/shard_map/all_to_all | solution.py:76
  161.8 98.9 %all-to-all-start.4 = ((f32[8,128,1024]{2,1,0:T(8,128)}), f32[8,128,1024]{2,1,0:T(8,128)}, u32[]{:S(2)}, u32[]{:S(2)}) async-start(f32[8,128,1024]{2,1,0:T(8,128)} %copy.133), calls=%async_computation.5 | async-start | bytes 8388608 | tf_op jit(solution)/shard_map/all_to_all | solution.py:140
  167.8 249.1 %reduce-scatter.5.cloned.1.call-start = ((), (), s32[]{:S(2)}) async-start(), calls=%async_computation.8 | async-start | bytes 5242880 | tf_op jit(solution)/shard_map/reduce_scatter | solution.py:156
  196.5 2.0 copy-start.2
  201.4 5.8 %copy-start.6 = (bf16[2,1024,8,64]{1,3,2,0:T(8,128)(2,1)S(1)}, bf16[2,1024,8,64]{1,3,2,0:T(8,128)(2,1)}, u32[]{:S(2)}) copy-start(bf16[2,1024,8,64]{1,3,2,0:T(8,128)(2,1)} %reshape.144) | copy-start | bytes 6291460
  271.5 169.9 %reduce-scatter.3.cloned.1.call-start = ((), (), s32[]{:S(2)}) async-start(), calls=%async_computation.7 | async-start | bytes 5242880 | tf_op jit(solution)/shard_map/reduce_scatter | solution.py:150
  397.7 5.9 %copy-start.3 = (bf16[2,8,128,1024]{2,3,1,0:T(8,128)(2,1)S(1)}, bf16[2,8,128,1024]{2,3,1,0:T(8,128)(2,1)}, u32[]{:S(2)}) copy-start(bf16[2,8,128,1024]{2,3,1,0:T(8,128)(2,1)} %copy-done.2) | copy-start | bytes 12582916
  397.7 6.6 %copy-start.5 = (bf16[2,1024,8,64]{1,3,2,0:T(8,128)(2,1)S(1)}, bf16[2,1024,8,64]{1,3,2,0:T(8,128)(2,1)}, u32[]{:S(2)}) copy-start(bf16[2,1024,8,64]{1,3,2,0:T(8,128)(2,1)} %reshape.149) | copy-start | bytes 6291460
  402.7 2.7 copy-start.7
  411.7 31.9 %copy-start.1 = (bf16[1024,1024]{1,0:T(8,128)(2,1)S(1)}, bf16[1024,1024]{1,0:T(8,128)(2,1)}, u32[]{:S(2)}) copy-start(bf16[1024,1024]{1,0:T(8,128)(2,1)} %param.7) | copy-start | bytes 6291460
Sparse Core Ops, SparseCore 0:
  271.7 43.5 reduce-scatter.4
  397.8 43.5 reduce-scatter.2
where the time goes:
time: 457 us; the launch traced here: 451 us
  blocking collectives  110 us (24%)
  local copies, waits for them, and re-layouts  108 us (24%)
  waiting for transfers between devices  105 us (23%)
  matrix products  83.2 us (18%)
  other arithmetic  15.8 us (3%)
  between operations  14.6 us (3%)
  starting transfers between devices  13.5 us (3%)
    all_to_all x1, blocking collectives, body(): lax.all_to_all(partial_keys, 'dim', split_axis=0, concat_axis=0, tiled=True)  96.9 us
    all_to_all x1, waiting for transfers between devices, body(): lax.all_to_all(partial_values, 'dim', split_axis=0, concat_axis=0, tiled=...  42.6 us
    all_to_all x1, waiting for transfers between devices, body(): lax.all_to_all(reply_keys, 'dim', split_axis=0, concat_axis=0, tiled=True)  39.6 us
    unnamed x34, local copies, waits for them, and re-layouts  32.8 us
    reduce_scatter x1, waiting for transfers between devices, body(): lax.psum_scatter(reduced_key_grad.reshape(blocks_here * TILE, model_width...  22.5 us
    sub x2, matrix products, attend_group(): expo_terms = jnp.exp(scores - row_max)  16.3 us
    all_to_all x1, blocking collectives, body(): lax.all_to_all(wanted.reshape(owners, 1), 'dim', split_axis=0, concat_axi...  13.5 us
    reshape x2, local copies, waits for them, and re-layouts, one_group(): key_parts.append(key_grad.reshape(per_step, slot_count, TILE, span))  11.7 us
  transfers between devices with their start and end apart: 5, of which 3 were waited for; matrix products, arithmetic and copies ran while one was open for 41% of the time, Pallas kernels for 0%

commit v1 on v0

v1 whole, which is shorter than its diff:
```python
import functools

import jax
import jax.numpy as jnp
from jax import lax
from jax.experimental import pallas as pl
from jax.experimental.pallas import tpu as pltpu
from jax.sharding import Mesh, PartitionSpec as P

HEADS = 16
HEAD_DIM = 64
TILE = 128
LANES = 2 * HEAD_DIM
META_ROWS = 16
LOG2E = 1.4426950408889634
SCALE = HEAD_DIM ** (-0.5)
VMEM_LIMIT = 56 * 1024 * 1024


def low_lanes(shape):
    return lax.broadcasted_iota(jnp.int32, shape, len(shape) - 1) < HEAD_DIM


def swap_halves(x):
    return jnp.concatenate([x[:, HEAD_DIM:], x[:, :HEAD_DIM]], axis=1)


def interleave(first, second):
    low = low_lanes(first.shape)
    swapped = swap_halves(second)
    return jnp.where(low, first, swapped), jnp.where(low, swapped, first)


def separate(even, odd):
    low = low_lanes(even.shape)
    return jnp.where(low, even, odd), swap_halves(jnp.where(low, odd, even))


def pack_dimension_kernel(pairs, place, *refs):
    keys, values, outs = refs[:pairs], refs[pairs : 2 * pairs], refs[2 * pairs :]
    odd = (place[2] & 1) == 1
    for i in range(pairs):
        a, b = interleave(keys[i][...], values[i][...])

        @pl.when(odd)
        def _():
            outs[2 * i][...] = b
            outs[2 * i + 1][...] = a

        @pl.when(jnp.logical_not(odd))
        def _():
            outs[2 * i][...] = a
            outs[2 * i + 1][...] = b


def pack_dimension(place, key_rows, value_rows, per_fact):
    rows = key_rows.shape[0]
    pairs = per_fact // 2

    def spec(i):
        return pl.BlockSpec((rows, LANES), lambda _, p: (0, p[0] * pairs + ((p[2] >> 1) ^ i)))

    return pl.pallas_call(
        functools.partial(pack_dimension_kernel, pairs),
        grid_spec=pltpu.PrefetchScalarGridSpec(
            num_scalar_prefetch=1,
            grid=(1,),
            in_specs=[spec(i) for i in range(pairs)] * 2,
            out_specs=[pl.BlockSpec((rows, LANES), lambda _, p: (0, 0))] * per_fact,
        ),
        out_shape=[jax.ShapeDtypeStruct((rows, LANES), jnp.bfloat16)] * per_fact,
        compiler_params=pltpu.CompilerParams(vmem_limit_bytes=VMEM_LIMIT),
        name="pack_dimension",
    )(place, *([key_rows] * pairs), *([value_rows] * pairs))


def pack_fact_kernel(queries, cotangent, meta, out):
    rows = queries.shape[0]
    for p in range(HEADS // 2):
        span = slice(p * LANES, (p + 1) * LANES)
        a, b = interleave(queries[:, span], cotangent[:, span])
        out[2 * p, :rows, :] = a
        out[2 * p + 1, :rows, :] = b
        out[2 * p, rows:, :] = meta[...]
        out[2 * p + 1, rows:, :] = meta[...]


def pack_fact(queries, cotangent, meta):
    rows = queries.shape[0]
    return pl.pallas_call(
        pack_fact_kernel,
        out_shape=jax.ShapeDtypeStruct((HEADS, rows + META_ROWS, LANES), jnp.bfloat16),
        compiler_params=pltpu.CompilerParams(vmem_limit_bytes=VMEM_LIMIT),
        name="pack_fact",
    )(queries, cotangent, meta)


def attend_kernel(owners, slots, place, *refs):
    facts = refs[0]
    tables = refs[1 : 1 + owners]
    fact_out = refs[1 + owners]
    grad_outs = refs[2 + owners : 2 + 2 * owners]
    table, total, meta_words, meta, copy_sems, meta_sem = refs[2 + 2 * owners :]
    sources = facts.shape[0]
    rows = facts.shape[1] - META_ROWS
    tiles_each = rows // TILE
    owner_rows = table.shape[0] // owners
    blocks_each = owner_rows // TILE
    copies = [
        pltpu.make_async_copy(
            tables[i], table.at[pl.ds(i * owner_rows, owner_rows), :], copy_sems.at[i]
        )
        for i in range(owners)
    ]
    for copy in copies:
        copy.start()
    meta_words[...] = facts[:, rows:, :].astype(jnp.float32).astype(jnp.int32)
    meta_copy = pltpu.make_async_copy(meta_words, meta, meta_sem)
    meta_copy.start()
    total[...] = jnp.zeros_like(total)
    meta_copy.wait()
    for copy in copies:
        copy.wait()
    odd = place[2] & 1
    flip = place[1] * blocks_each
    lane = lax.broadcasted_iota(jnp.int32, (TILE, LANES), 1)
    first = (lane // HEAD_DIM) == odd

    def tile_step(index, carry):
        source = index // tiles_each
        tile = index % tiles_each
        length = meta[source, tile, slots]
        start = pl.multiple_of(tile * TILE, TILE)

        def attend(count):
            both = facts[source, pl.ds(start, TILE), :]
            zero = jnp.zeros_like(both)
            left = jnp.concatenate(
                [jnp.where(first, both, zero), jnp.where(first, zero, both)], axis=0
            )
            places = [
                pl.multiple_of((meta[source, tile, j] ^ flip) * TILE, TILE) for j in range(count)
            ]
            kv = jnp.concatenate([table[pl.ds(at, TILE), :] for at in places], axis=0)
            products = lax.dot_general(
                kv, left, (((1,), (1,)), ((), ())), preferred_element_type=jnp.float32
            )
            scores = products[:, :TILE] * (SCALE * LOG2E)
            dweights = products[:, TILE:]
            terms = jnp.exp2(scores - jnp.max(scores, axis=0, keepdims=True))
            weights = terms * (1.0 / jnp.sum(terms, axis=0, keepdims=True))
            row_delta = jnp.sum(weights * dweights, axis=0, keepdims=True)
            dscores = weights * (dweights - row_delta)
            pair = jnp.concatenate(
                [dscores.astype(jnp.bfloat16), weights.astype(jnp.bfloat16)], axis=1
            )
            out = lax.dot_general(
                pair, kv, (((0,), (0,)), ((), ())), preferred_element_type=jnp.float32
            )
            fact_out[source, pl.ds(start, TILE), :] = jnp.where(
                first, out[:TILE] * SCALE, out[TILE:]
            ).astype(jnp.bfloat16)
            grads = jnp.dot(pair, left, preferred_element_type=jnp.float32)
            for j, at in enumerate(places):
                total[pl.ds(at, TILE), :] += grads[j * TILE : (j + 1) * TILE]

        for count in range(1, slots + 1):
            pl.when(length == count)(functools.partial(attend, count))
        return carry

    lax.fori_loop(0, sources * tiles_each, tile_step, 0)
    wide = lax.broadcasted_iota(jnp.int32, (owner_rows, LANES), 1)
    factor = jnp.where((wide // HEAD_DIM) == odd, SCALE, 1.0)
    for i in range(owners):
        grad_outs[i][...] = (
            total[i * owner_rows : (i + 1) * owner_rows, :] * factor
        ).astype(jnp.bfloat16)


def attend(place, facts, tables, slots):
    owners = len(tables)
    owner_rows = tables[0].shape[0]
    sources, rows, _ = facts.shape
    rows -= META_ROWS
    whole = pl.BlockSpec(memory_space=pltpu.VMEM)
    results = pl.pallas_call(
        functools.partial(attend_kernel, owners, slots),
        in_specs=[pl.BlockSpec(memory_space=pltpu.SMEM), whole]
        + [pl.BlockSpec(memory_space=pl.ANY)] * owners,
        out_specs=[whole] * (1 + owners),
        out_shape=[jax.ShapeDtypeStruct((sources, rows, LANES), jnp.bfloat16)]
        + [jax.ShapeDtypeStruct((owner_rows, LANES), jnp.bfloat16)] * owners,
        scratch_shapes=[
            pltpu.VMEM((owners * owner_rows, LANES), jnp.bfloat16),
            pltpu.VMEM((owners * owner_rows, LANES), jnp.float32),
            pltpu.VMEM((sources, META_ROWS, LANES), jnp.int32),
            pltpu.SMEM((sources, META_ROWS, LANES), jnp.int32),
            pltpu.SemaphoreType.DMA((owners,)),
            pltpu.SemaphoreType.DMA,
        ],
        compiler_params=pltpu.CompilerParams(vmem_limit_bytes=VMEM_LIMIT),
        name="attend",
    )(place, facts, *tables)
    return results[0], results[1:]


def unpack_fact_kernel(parts, attended, query_grad):
    for p in range(HEADS // 2):
        span = slice(p * LANES, (p + 1) * LANES)
        query_grad[:, span], attended[:, span] = separate(parts[2 * p], parts[2 * p + 1])


def unpack_fact(parts):
    rows = parts.shape[1]
    shape = jax.ShapeDtypeStruct((rows, HEADS * HEAD_DIM), jnp.bfloat16)
    return pl.pallas_call(
        unpack_fact_kernel,
        out_shape=[shape, shape],
        compiler_params=pltpu.CompilerParams(vmem_limit_bytes=VMEM_LIMIT),
        name="unpack_fact",
    )(parts)


def unpack_dimension_kernel(halves, per_fact, place, *refs):
    parts = refs[: halves * per_fact]
    key_grad, value_grad = refs[halves * per_fact :]
    odd = (place[2] & 1) == 1
    high = place[2] >> 1
    for i in range(per_fact // 2):
        sums = []
        for s in range(2):
            terms = [parts[a * per_fact + 2 * i + s][...].astype(jnp.float32) for a in range(halves)]
            sums.append(functools.reduce(jnp.add, terms).astype(jnp.bfloat16))
        even = jnp.where(odd, sums[1], sums[0])
        uneven = jnp.where(odd, sums[0], sums[1])
        keys, values = separate(even, uneven)
        at = pl.ds(pl.multiple_of((high ^ i) * LANES, LANES), LANES)
        key_grad[:, at] = keys
        value_grad[:, at] = values


def unpack_dimension(place, parts, halves, per_fact):
    rows = parts[0].shape[0]
    shape = jax.ShapeDtypeStruct((rows, per_fact * HEAD_DIM), jnp.bfloat16)
    whole = pl.BlockSpec(memory_space=pltpu.VMEM)
    return pl.pallas_call(
        functools.partial(unpack_dimension_kernel, halves, per_fact),
        in_specs=[pl.BlockSpec(memory_space=pltpu.SMEM)] + [whole] * len(parts),
        out_specs=[whole, whole],
        out_shape=[shape, shape],
        compiler_params=pltpu.CompilerParams(vmem_limit_bytes=VMEM_LIMIT),
        name="unpack_dimension",
    )(place, *parts)


def exchange(parts, halves, per_fact):
    moved = []
    for index, part in enumerate(parts):
        if index == 0:
            moved.append(part)
            continue
        count = halves * per_fact
        moved.append(lax.ppermute(part, ("half", "head"), [(i, i ^ index) for i in range(count)]))
    return moved


def body(halves, per_fact, queries, key_rows, value_rows, cotangent, block_lists, tile_lengths):
    tiles, slots = block_lists.shape
    half, head = lax.axis_index("half"), lax.axis_index("head")
    place = jnp.stack([lax.axis_index("fact"), half * per_fact + head, head]).astype(jnp.int32)
    words = jnp.concatenate([block_lists, tile_lengths[:, None]], axis=1).astype(jnp.bfloat16)
    meta = jnp.pad(words, ((0, META_ROWS - tiles), (0, LANES - slots - 1)))
    packed = pack_dimension(place, key_rows, value_rows, per_fact)
    tables = exchange(list(packed) * halves, halves, per_fact)
    facts = lax.all_to_all(
        pack_fact(queries, cotangent, meta), ("fact", "head"), split_axis=0, concat_axis=0, tiled=True
    )
    fact_out, grads = attend(place, facts, tables, slots)
    grads = exchange(list(grads), halves, per_fact)
    fact_out = lax.all_to_all(fact_out, ("fact", "head"), split_axis=0, concat_axis=0, tiled=True)
    attended, query_grad = unpack_fact(fact_out)
    key_grad, value_grad = unpack_dimension(place, grads, halves, per_fact)
    return attended, query_grad, key_grad, value_grad


def solution(mesh):
    facts, dims = mesh.shape["fact"], mesh.shape["dim"]
    per_fact = HEADS // facts
    halves = dims // per_fact
    fine = Mesh(mesh.devices.reshape(facts, halves, per_fact), ("fact", "half", "head"))
    every = ("fact", "half", "head")
    owner = ("half", "head")
    in_specs = (
        P(every, None),
        P(owner, None),
        P(owner, None),
        P(every, None),
        P(every, None),
        P(every),
    )
    out_specs = (
        P(every, None),
        P(every, None),
        P(owner, "fact"),
        P(owner, "fact"),
    )
    return jax.shard_map(
        functools.partial(body, halves, per_fact),
        mesh=fine,
        in_specs=in_specs,
        out_specs=out_specs,
        check_vma=False,
    )
```

time: 457 us -> 166 us (0.36)
  the two profiles are of different devices: /device:TPU:0 before, /device:TPU:10 now
where the time goes in v1:
time: 166 us
  waiting for transfers between devices  89.8 us (54%)
  Pallas kernels  42.9 us (26%)
  starting transfers between devices  26.1 us (16%)
  local copies, waits for them, and re-layouts  3.59 us (2%)
  other arithmetic  2.62 us (2%)
    ppermute x14, waiting for transfers between devices, exchange(): lax.ppermute(part, ('half', 'head'), [(i, i ^ index) for i in range(count)])  89.8 us
    pallas_call x1, Pallas kernels, attend(): pl.pallas_call(functools.partial(attend_kernel, owners, slots), in_specs=...  32 us
    ppermute x14, starting transfers between devices, exchange(): lax.ppermute(part, ('half', 'head'), [(i, i ^ index) for i in range(count)])  15.8 us
    all_to_all x1, starting transfers between devices, body(): lax.all_to_all(pack_fact(queries, cotangent, meta), ('fact', 'head'), spl...  5.17 us
    all_to_all x1, starting transfers between devices, body(): lax.all_to_all(fact_out, ('fact', 'head'), split_axis=0, concat_axis=0, t...  5.14 us
    unnamed x46, local copies, waits for them, and re-layouts  3.48 us
  transfers between devices with their start and end apart: 16, of which 9 were waited for; matrix products, arithmetic and copies ran while one was open for 0% of the time, Pallas kernels for 4%

profile of v1, /device:TPU:10, one launch (start us, length us, event | category | flops | bytes accessed | tf_op | source)
XLA Modules:
  0.0 165.9 jit_solution(5526714951252183852)
XLA Ops:
  0.6 0.7 convert.7
  1.3 0.7 convert_bitcast_fusion
  2.0 0.1 copy.10
  2.1 0.7 fusion.5.meta
  2.8 2.5 %pack_fact.1 = bf16[16,272,128]{2,1,0:T(8,128)(2,1)} custom-call(bf16[256,1024]{1,0:T(8,128)(2,1)} %queries.1, bf16[256,1024]{1,0:T(8,128)(2,1)} %cotangent.1, bf16[16,128]{1,0:T(8,128)(2,1)} %fusion.5.meta), custom_call_target="tpu_custom_call" | custom-call | tf_op jit(solution)/shard_map/pack_fact/pallas_call | solution.py:90
  5.2 5.2 %all-to-all-start = ((bf16[16,272,128]{2,1,0:T(8,128)(2,1)}), bf16[16,272,128]{2,1,0:T(8,128)(2,1)S(1)}, u32[]{:S(2)}, u32[]{:S(2)}) async-start(bf16[16,272,128]{2,1,0:T(8,128)(2,1)} %pack_fact.1), calls=%async_computation | async-start | bytes 2228224 | tf_op jit(solution)/shard_map/all_to_all | solution.py:275
  10.4 0.6 pad_add_fusion.place
  11.0 3.2 %pack_dimension.1 = (bf16[1024,128]{1,0:T(8,128)(2,1)}, bf16[1024,128]{1,0:T(8,128)(2,1)}, bf16[1024,128]{1,0:T(8,128)(2,1)}, bf16[1024,128]{1,0:T(8,128)(2,1)}) custom-call(s32[3]{0:T(128)} %pad_add_fusion.place, bf16[1024,1024]{1,0:T(8,128)(2,1)} %refs_1_.1, bf16[1024,1024]{1,0:T(8,128)(2,1)} %refs_1_.1, bf16[1024,1024]{1,0:T(8,128)(2,1)} %refs_3_.1, ...), custom_call_target="tpu_custom_call" | custom-call | tf_op jit(solution)/shard_map/pack_dimension/pallas_call | solution.py:63
  14.3 2.6 %collective-permute-start.3 = (bf16[1024,128]{1,0:T(8,128)(2,1)}, bf16[1024,128]{1,0:T(8,128)(2,1)S(1)}, u32[]{:S(2)}, u32[]{:S(2)}) collective-permute-start(bf16[1024,128]{1,0:T(8,128)(2,1)} %get-tuple-element.21.refs_1_), channel_id=1, source_target_pairs={{0,4},{1,5},{2,6},{3,7},{4,0},{5,1},{6,2},{7,3},{8,12},{9,13},{10,... | collective-permute-start | bytes 786440 | tf_op jit(solution)/shard_map/ppermute | solution.py:263
  16.9 1.2 collective-permute-start.4
  18.1 0.6 collective-permute-start
  18.7 1.7 %collective-permute-start.5 = (bf16[1024,128]{1,0:T(8,128)(2,1)}, bf16[1024,128]{1,0:T(8,128)(2,1)S(1)}, u32[]{:S(2)}, u32[]{:S(2)}) collective-permute-start(bf16[1024,128]{1,0:T(8,128)(2,1)} %get-tuple-element.23), channel_id=1, source_target_pairs={{0,6},{1,7},{2,4},{3,5},{4,2},{5,3},{6,0},{7,1},{8,14},{9,15},{10,... | collective-permute-start | bytes 786440 | tf_op jit(solution)/shard_map/ppermute | solution.py:263
  20.4 2.4 %collective-permute-start.1 = (bf16[1024,128]{1,0:T(8,128)(2,1)}, bf16[1024,128]{1,0:T(8,128)(2,1)S(1)}, u32[]{:S(2)}, u32[]{:S(2)}) collective-permute-start(bf16[1024,128]{1,0:T(8,128)(2,1)} %get-tuple-element.23), channel_id=1, source_target_pairs={{0,2},{1,3},{2,0},{3,1},{4,6},{5,7},{6,4},{7,5},{8,10},{9,11},{10,... | collective-permute-start | bytes 786440 | tf_op jit(solution)/shard_map/ppermute | solution.py:263
  22.7 17.7 %collective-permute-done.3.refs_5_ = bf16[1024,128]{1,0:T(8,128)(2,1)S(1)} collective-permute-done((bf16[1024,128]{1,0:T(8,128)(2,1)}, bf16[1024,128]{1,0:T(8,128)(2,1)S(1)}, u32[]{:S(2)}, u32[]{:S(2)}) %collective-permute-start.3) | collective-permute-done | bytes 262176 | tf_op jit(solution)/shard_map/ppermute | solution.py:263
  40.4 0.0 collective-permute-start.6
  40.4 10.1 %collective-permute-done.4.refs_6_ = bf16[1024,128]{1,0:T(8,128)(2,1)S(1)} collective-permute-done((bf16[1024,128]{1,0:T(8,128)(2,1)}, bf16[1024,128]{1,0:T(8,128)(2,1)S(1)}, u32[]{:S(2)}, u32[]{:S(2)}) %collective-permute-start.4) | collective-permute-done | bytes 262176 | tf_op jit(solution)/shard_map/ppermute | solution.py:263
  50.6 0.0 collective-permute-start.2
  50.6 0.0 collective-permute-done.refs_2_
  50.6 7.1 %collective-permute-done.5.refs_7_ = bf16[1024,128]{1,0:T(8,128)(2,1)S(1)} collective-permute-done((bf16[1024,128]{1,0:T(8,128)(2,1)}, bf16[1024,128]{1,0:T(8,128)(2,1)S(1)}, u32[]{:S(2)}, u32[]{:S(2)}) %collective-permute-start.5) | collective-permute-done | bytes 262176 | tf_op jit(solution)/shard_map/ppermute | solution.py:263
  57.6 0.0 collective-permute-done.1.refs_3_
  57.6 6.9 %collective-permute-done.6.refs_8_ = bf16[1024,128]{1,0:T(8,128)(2,1)S(1)} collective-permute-done((bf16[1024,128]{1,0:T(8,128)(2,1)}, bf16[1024,128]{1,0:T(8,128)(2,1)S(1)}, u32[]{:S(2)}, u32[]{:S(2)}) %collective-permute-start.6) | collective-permute-done | bytes 262176 | tf_op jit(solution)/shard_map/ppermute | solution.py:263
  64.5 0.0 collective-permute-done.2.refs_4_
  64.5 0.0 all-to-all-done.refs_0_
  64.6 0.6 copy-done.14
  65.2 0.1 copy-done.15
  65.3 1.0 copy-done
  66.3 32.0 %attend.1 = (bf16[16,256,128]{2,1,0:T(8,128)(2,1)}, bf16[1024,128]{1,0:T(8,128)(2,1)}, bf16[1024,128]{1,0:T(8,128)(2,1)}, bf16[1024,128]{1,0:T(8,128)(2,1)}, bf1...) custom-call(s32[3]{0:T(128)} %pad_add_fusion.place, ...), custom_call_target="tpu_custom_call" | custom-call | tf_op jit(solution)/shard_map/attend/pallas_call | solution.py:186
  98.3 0.0 copy-start.22
  98.4 5.1 %all-to-all-start.1 = ((bf16[16,256,128]{2,1,0:T(8,128)(2,1)}), bf16[16,256,128]{2,1,0:T(8,128)(2,1)S(1)}, u32[]{:S(2)}, u32[]{:S(2)}) async-start(bf16[16,256,128]{2,1,0:T(8,128)(2,1)} %get-tuple-element.25), calls=%async_computation.1 | async-start | bytes 2097152 | tf_op jit(solution)/shard_map/all_to_all | solution.py:280
  103.5 1.5 collective-permute-start.7
  105.1 0.6 collective-permute-start.8
  105.6 1.5 collective-permute-start.9
  107.1 0.0 collective-permute-start.10
  107.1 3.8 %collective-permute-start.11 = (bf16[1024,128]{1,0:T(8,128)(2,1)S(1)}, bf16[1024,128]{1,0:T(8,128)(2,1)S(1)}, u32[]{:S(2)}, u32[]{:S(2)}) collective-permute-start(bf16[1024,128]{1,0:T(8,128)(2,1)S(1)} %copy-done.18), channel_id=1, source_target_pairs={{0,5},{1,4},{2,7},{3,6},{4,1},{5,0},{6,3},{7,2},{8,13},{9,12},{10,... | collective-permute-start | bytes 786440 | tf_op jit(solution)/shard_map/ppermute | solution.py:263
  110.9 12.6 %collective-permute-done.7.refs_1_ = bf16[1024,128]{1,0:T(8,128)(2,1)S(1)} collective-permute-done((bf16[1024,128]{1,0:T(8,128)(2,1)S(1)}, bf16[1024,128]{1,0:T(8,128)(2,1)S(1)}, u32[]{:S(2)}, u32[]{:S(2)}) %collective-permute-start.7) | collective-permute-done | bytes 262176 | tf_op jit(solution)/shard_map/ppermute | solution.py:263
  123.5 0.0 collective-permute-start.12
  123.5 9.3 %collective-permute-done.8.refs_2_ = bf16[1024,128]{1,0:T(8,128)(2,1)S(1)} collective-permute-done((bf16[1024,128]{1,0:T(8,128)(2,1)S(1)}, bf16[1024,128]{1,0:T(8,128)(2,1)S(1)}, u32[]{:S(2)}, u32[]{:S(2)}) %collective-permute-start.8) | collective-permute-done | bytes 262176 | tf_op jit(solution)/shard_map/ppermute | solution.py:263
  132.8 0.0 collective-permute-start.13
  132.8 16.4 %collective-permute-done.9.refs_3_ = bf16[1024,128]{1,0:T(8,128)(2,1)S(1)} collective-permute-done((bf16[1024,128]{1,0:T(8,128)(2,1)S(1)}, bf16[1024,128]{1,0:T(8,128)(2,1)S(1)}, u32[]{:S(2)}, u32[]{:S(2)}) %collective-permute-start.9) | collective-permute-done | bytes 262176 | tf_op jit(solution)/shard_map/ppermute | solution.py:263
  149.2 0.0 collective-permute-done.10.refs_4_
  149.3 0.0 collective-permute-done.11.refs_5_
  149.3 5.7 %collective-permute-done.12.refs_6_ = bf16[1024,128]{1,0:T(8,128)(2,1)S(1)} collective-permute-done((bf16[1024,128]{1,0:T(8,128)(2,1)S(1)}, bf16[1024,128]{1,0:T(8,128)(2,1)S(1)}, u32[]{:S(2)}, u32[]{:S(2)}) %collective-permute-start.12) | collective-permute-done | bytes 262176 | tf_op jit(solution)/shard_map/ppermute | solution.py:263
  155.0 4.0 %collective-permute-done.13.refs_7_ = bf16[1024,128]{1,0:T(8,128)(2,1)S(1)} collective-permute-done((bf16[1024,128]{1,0:T(8,128)(2,1)S(1)}, bf16[1024,128]{1,0:T(8,128)(2,1)S(1)}, u32[]{:S(2)}, u32[]{:S(2)}) %collective-permute-start.13) | collective-permute-done | bytes 262176 | tf_op jit(solution)/shard_map/ppermute | solution.py:263
  159.0 0.7 copy-done.8
  159.7 2.8 %unpack_dimension.1 = (bf16[1024,256]{1,0:T(8,128)(2,1)}, bf16[1024,256]{1,0:T(8,128)(2,1)}) custom-call(s32[3]{0:T(128)} %pad_add_fusion.place, bf16[1024,128]{1,0:T(8,128)(2,1)} %get-tuple-element.28.refs_0_, bf16[1024,128]{1,0:T(8,128)(2,1)} %copy-done.2, bf16[1024,128]{1,0:T(8,128)(2,1)} %copy-done.3, bf16[1024,128]{1,0:T(8,128)(2,1)} %copy-done.4, ...), custom_call_target="tpu_custom_call" | custom-call | tf_op jit(solution)/shard_map/unpack_dimension/pallas_call | solution.py:246
  162.5 0.0 all-to-all-done.1.parts
  162.5 1.0 copy-done.1
  163.5 2.3 %unpack_fact.1 = (bf16[256,1024]{1,0:T(8,128)(2,1)}, bf16[256,1024]{1,0:T(8,128)(2,1)}) custom-call(bf16[16,256,128]{2,1,0:T(8,128)(2,1)} %copy-done.1), custom_call_target="tpu_custom_call" | custom-call | tf_op jit(solution)/shard_map/unpack_fact/pallas_call | solution.py:216
  (40 shorter events, 0.1 us)
Async XLA Ops:
  5.2 59.3 %all-to-all-start = ((bf16[16,272,128]{2,1,0:T(8,128)(2,1)}), bf16[16,272,128]{2,1,0:T(8,128)(2,1)S(1)}, u32[]{:S(2)}, u32[]{:S(2)}) async-start(bf16[16,272,128]{2,1,0:T(8,128)(2,1)} %pack_fact.1), calls=%async_computation | async-start | bytes 2228224 | tf_op jit(solution)/shard_map/all_to_all | solution.py:275
  14.3 26.1 %collective-permute-start.3 = (bf16[1024,128]{1,0:T(8,128)(2,1)}, bf16[1024,128]{1,0:T(8,128)(2,1)S(1)}, u32[]{:S(2)}, u32[]{:S(2)}) collective-permute-start(bf16[1024,128]{1,0:T(8,128)(2,1)} %get-tuple-element.21.refs_1_), channel_id=1, source_target_pairs={{0,4},{1,5},{2,6},{3,7},{4,0},{5,1},{6,2},{7,3},{8,12},{9,13},{10,... | collective-permute-start | bytes 786440 | tf_op jit(solution)/shard_map/ppermute | solution.py:263
  16.9 33.7 %collective-permute-start.4 = (bf16[1024,128]{1,0:T(8,128)(2,1)}, bf16[1024,128]{1,0:T(8,128)(2,1)S(1)}, u32[]{:S(2)}, u32[]{:S(2)}) collective-permute-start(bf16[1024,128]{1,0:T(8,128)(2,1)} %get-tuple-element.22), channel_id=1, source_target_pairs={{0,5},{1,4},{2,7},{3,6},{4,1},{5,0},{6,3},{7,2},{8,13},{9,12},{10,... | collective-permute-start | bytes 786440 | tf_op jit(solution)/shard_map/ppermute | solution.py:263
  18.1 32.5 %collective-permute-start = (bf16[1024,128]{1,0:T(8,128)(2,1)}, bf16[1024,128]{1,0:T(8,128)(2,1)S(1)}, u32[]{:S(2)}, u32[]{:S(2)}) collective-permute-start(bf16[1024,128]{1,0:T(8,128)(2,1)} %get-tuple-element.22), channel_id=1, source_target_pairs={{0,1},{1,0},{2,3},{3,2},{4,5},{5,4},{6,7},{7,6},{8,9},{9,8},{10,11... | collective-permute-start | bytes 786440 | tf_op jit(solution)/shard_map/ppermute | solution.py:263
  18.7 39.0 %collective-permute-start.5 = (bf16[1024,128]{1,0:T(8,128)(2,1)}, bf16[1024,128]{1,0:T(8,128)(2,1)S(1)}, u32[]{:S(2)}, u32[]{:S(2)}) collective-permute-start(bf16[1024,128]{1,0:T(8,128)(2,1)} %get-tuple-element.23), channel_id=1, source_target_pairs={{0,6},{1,7},{2,4},{3,5},{4,2},{5,3},{6,0},{7,1},{8,14},{9,15},{10,... | collective-permute-start | bytes 786440 | tf_op jit(solution)/shard_map/ppermute | solution.py:263
  20.4 37.3 %collective-permute-start.1 = (bf16[1024,128]{1,0:T(8,128)(2,1)}, bf16[1024,128]{1,0:T(8,128)(2,1)S(1)}, u32[]{:S(2)}, u32[]{:S(2)}) collective-permute-start(bf16[1024,128]{1,0:T(8,128)(2,1)} %get-tuple-element.23), channel_id=1, source_target_pairs={{0,2},{1,3},{2,0},{3,1},{4,6},{5,7},{6,4},{7,5},{8,10},{9,11},{10,... | collective-permute-start | bytes 786440 | tf_op jit(solution)/shard_map/ppermute | solution.py:263
  40.4 24.1 %copy-start.9 = (bf16[1024,128]{1,0:T(8,128)(2,1)}, bf16[1024,128]{1,0:T(8,128)(2,1)S(1)}, u32[]{:S(2)}) copy-start(bf16[1024,128]{1,0:T(8,128)(2,1)S(1)} %collective-permute-done.3.refs_5_) | copy-start | bytes 786436
  40.4 24.1 %collective-permute-start.6 = (bf16[1024,128]{1,0:T(8,128)(2,1)}, bf16[1024,128]{1,0:T(8,128)(2,1)S(1)}, u32[]{:S(2)}, u32[]{:S(2)}) collective-permute-start(bf16[1024,128]{1,0:T(8,128)(2,1)} %get-tuple-element.24), channel_id=1, source_target_pairs={{0,7},{1,6},{2,5},{3,4},{4,3},{5,2},{6,1},{7,0},{8,15},{9,14},{10,... | collective-permute-start | bytes 786440 | tf_op jit(solution)/shard_map/ppermute | solution.py:263
  50.6 14.0 %copy-start.10 = (bf16[1024,128]{1,0:T(8,128)(2,1)}, bf16[1024,128]{1,0:T(8,128)(2,1)S(1)}, u32[]{:S(2)}) copy-start(bf16[1024,128]{1,0:T(8,128)(2,1)S(1)} %collective-permute-done.4.refs_6_) | copy-start | bytes 786436
  50.6 14.0 %collective-permute-start.2 = (bf16[1024,128]{1,0:T(8,128)(2,1)}, bf16[1024,128]{1,0:T(8,128)(2,1)S(1)}, u32[]{:S(2)}, u32[]{:S(2)}) collective-permute-start(bf16[1024,128]{1,0:T(8,128)(2,1)} %get-tuple-element.24), channel_id=1, source_target_pairs={{0,3},{1,2},{2,1},{3,0},{4,7},{5,6},{6,5},{7,4},{8,11},{9,10},{10,... | collective-permute-start | bytes 786440 | tf_op jit(solution)/shard_map/ppermute | solution.py:263
  50.6 14.0 %copy-start.11 = (bf16[1024,128]{1,0:T(8,128)(2,1)}, bf16[1024,128]{1,0:T(8,128)(2,1)S(1)}, u32[]{:S(2)}) copy-start(bf16[1024,128]{1,0:T(8,128)(2,1)S(1)} %collective-permute-done.refs_2_) | copy-start | bytes 786436
  57.6 6.9 %copy-start.12 = (bf16[1024,128]{1,0:T(8,128)(2,1)}, bf16[1024,128]{1,0:T(8,128)(2,1)S(1)}, u32[]{:S(2)}) copy-start(bf16[1024,128]{1,0:T(8,128)(2,1)S(1)} %collective-permute-done.5.refs_7_) | copy-start | bytes 786436
  57.6 6.9 %copy-start.13 = (bf16[1024,128]{1,0:T(8,128)(2,1)}, bf16[1024,128]{1,0:T(8,128)(2,1)S(1)}, u32[]{:S(2)}) copy-start(bf16[1024,128]{1,0:T(8,128)(2,1)S(1)} %collective-permute-done.1.refs_3_) | copy-start | bytes 786436
  64.5 0.7 copy-start.14
  64.5 0.8 copy-start.15
  65.3 1.0 copy-start
  98.3 5.2 %copy-start.22 = (bf16[1024,128]{1,0:T(8,128)(2,1)S(1)}, bf16[1024,128]{1,0:T(8,128)(2,1)}, u32[]{:S(2)}) copy-start(bf16[1024,128]{1,0:T(8,128)(2,1)} %get-tuple-element.29) | copy-start | bytes 786436
  98.3 6.7 %copy-start.21 = (bf16[1024,128]{1,0:T(8,128)(2,1)S(1)}, bf16[1024,128]{1,0:T(8,128)(2,1)}, u32[]{:S(2)}) copy-start(bf16[1024,128]{1,0:T(8,128)(2,1)} %get-tuple-element.30) | copy-start | bytes 786436
  98.3 7.3 %copy-start.20 = (bf16[1024,128]{1,0:T(8,128)(2,1)S(1)}, bf16[1024,128]{1,0:T(8,128)(2,1)}, u32[]{:S(2)}) copy-start(bf16[1024,128]{1,0:T(8,128)(2,1)} %get-tuple-element.31) | copy-start | bytes 786436
  98.3 8.7 %copy-start.19 = (bf16[1024,128]{1,0:T(8,128)(2,1)S(1)}, bf16[1024,128]{1,0:T(8,128)(2,1)}, u32[]{:S(2)}) copy-start(bf16[1024,128]{1,0:T(8,128)(2,1)} %get-tuple-element.32) | copy-start | bytes 786436
  98.3 8.7 %copy-start.18 = (bf16[1024,128]{1,0:T(8,128)(2,1)S(1)}, bf16[1024,128]{1,0:T(8,128)(2,1)}, u32[]{:S(2)}) copy-start(bf16[1024,128]{1,0:T(8,128)(2,1)} %get-tuple-element.33) | copy-start | bytes 786436
  98.4 25.2 %copy-start.17 = (bf16[1024,128]{1,0:T(8,128)(2,1)S(1)}, bf16[1024,128]{1,0:T(8,128)(2,1)}, u32[]{:S(2)}) copy-start(bf16[1024,128]{1,0:T(8,128)(2,1)} %get-tuple-element.34) | copy-start | bytes 786436
  98.4 34.5 %copy-start.16 = (bf16[1024,128]{1,0:T(8,128)(2,1)S(1)}, bf16[1024,128]{1,0:T(8,128)(2,1)}, u32[]{:S(2)}) copy-start(bf16[1024,128]{1,0:T(8,128)(2,1)} %get-tuple-element.35) | copy-start | bytes 786436
  98.4 64.2 %all-to-all-start.1 = ((bf16[16,256,128]{2,1,0:T(8,128)(2,1)}), bf16[16,256,128]{2,1,0:T(8,128)(2,1)S(1)}, u32[]{:S(2)}, u32[]{:S(2)}) async-start(bf16[16,256,128]{2,1,0:T(8,128)(2,1)} %get-tuple-element.25), calls=%async_computation.1 | async-start | bytes 2097152 | tf_op jit(solution)/shard_map/all_to_all | solution.py:280
  103.5 20.0 %collective-permute-start.7 = (bf16[1024,128]{1,0:T(8,128)(2,1)S(1)}, bf16[1024,128]{1,0:T(8,128)(2,1)S(1)}, u32[]{:S(2)}, u32[]{:S(2)}) collective-permute-start(bf16[1024,128]{1,0:T(8,128)(2,1)S(1)} %copy-done.22), channel_id=1, source_target_pairs={{0,1},{1,0},{2,3},{3,2},{4,5},{5,4},{6,7},{7,6},{8,9},{9,8},{10,11... | collective-permute-start | bytes 786440 | tf_op jit(solution)/shard_map/ppermute | solution.py:263
  105.1 27.8 %collective-permute-start.8 = (bf16[1024,128]{1,0:T(8,128)(2,1)S(1)}, bf16[1024,128]{1,0:T(8,128)(2,1)S(1)}, u32[]{:S(2)}, u32[]{:S(2)}) collective-permute-start(bf16[1024,128]{1,0:T(8,128)(2,1)S(1)} %copy-done.21), channel_id=1, source_target_pairs={{0,2},{1,3},{2,0},{3,1},{4,6},{5,7},{6,4},{7,5},{8,10},{9,11},{10,... | collective-permute-start | bytes 786440 | tf_op jit(solution)/shard_map/ppermute | solution.py:263
  105.6 43.6 %collective-permute-start.9 = (bf16[1024,128]{1,0:T(8,128)(2,1)S(1)}, bf16[1024,128]{1,0:T(8,128)(2,1)S(1)}, u32[]{:S(2)}, u32[]{:S(2)}) collective-permute-start(bf16[1024,128]{1,0:T(8,128)(2,1)S(1)} %copy-done.20), channel_id=1, source_target_pairs={{0,3},{1,2},{2,1},{3,0},{4,7},{5,6},{6,5},{7,4},{8,11},{9,10},{10,... | collective-permute-start | bytes 786440 | tf_op jit(solution)/shard_map/ppermute | solution.py:263
  107.1 42.2 %collective-permute-start.10 = (bf16[1024,128]{1,0:T(8,128)(2,1)S(1)}, bf16[1024,128]{1,0:T(8,128)(2,1)S(1)}, u32[]{:S(2)}, u32[]{:S(2)}) collective-permute-start(bf16[1024,128]{1,0:T(8,128)(2,1)S(1)} %copy-done.19), channel_id=1, source_target_pairs={{0,4},{1,5},{2,6},{3,7},{4,0},{5,1},{6,2},{7,3},{8,12},{9,13},{10,... | collective-permute-start | bytes 786440 | tf_op jit(solution)/shard_map/ppermute | solution.py:263
  107.1 42.2 %collective-permute-start.11 = (bf16[1024,128]{1,0:T(8,128)(2,1)S(1)}, bf16[1024,128]{1,0:T(8,128)(2,1)S(1)}, u32[]{:S(2)}, u32[]{:S(2)}) collective-permute-start(bf16[1024,128]{1,0:T(8,128)(2,1)S(1)} %copy-done.18), channel_id=1, source_target_pairs={{0,5},{1,4},{2,7},{3,6},{4,1},{5,0},{6,3},{7,2},{8,13},{9,12},{10,... | collective-permute-start | bytes 786440 | tf_op jit(solution)/shard_map/ppermute | solution.py:263
  123.5 35.5 %copy-start.2 = (bf16[1024,128]{1,0:T(8,128)(2,1)}, bf16[1024,128]{1,0:T(8,128)(2,1)S(1)}, u32[]{:S(2)}) copy-start(bf16[1024,128]{1,0:T(8,128)(2,1)S(1)} %collective-permute-done.7.refs_1_) | copy-start | bytes 786436
  123.5 31.5 %collective-permute-start.12 = (bf16[1024,128]{1,0:T(8,128)(2,1)S(1)}, bf16[1024,128]{1,0:T(8,128)(2,1)S(1)}, u32[]{:S(2)}, u32[]{:S(2)}) collective-permute-start(bf16[1024,128]{1,0:T(8,128)(2,1)S(1)} %copy-done.17), channel_id=1, source_target_pairs={{0,6},{1,7},{2,4},{3,5},{4,2},{5,3},{6,0},{7,1},{8,14},{9,15},{10,... | collective-permute-start | bytes 786440 | tf_op jit(solution)/shard_map/ppermute | solution.py:263
  132.8 26.2 %copy-start.3 = (bf16[1024,128]{1,0:T(8,128)(2,1)}, bf16[1024,128]{1,0:T(8,128)(2,1)S(1)}, u32[]{:S(2)}) copy-start(bf16[1024,128]{1,0:T(8,128)(2,1)S(1)} %collective-permute-done.8.refs_2_) | copy-start | bytes 786436
  132.8 26.1 %collective-permute-start.13 = (bf16[1024,128]{1,0:T(8,128)(2,1)S(1)}, bf16[1024,128]{1,0:T(8,128)(2,1)S(1)}, u32[]{:S(2)}, u32[]{:S(2)}) collective-permute-start(bf16[1024,128]{1,0:T(8,128)(2,1)S(1)} %copy-done.16), channel_id=1, source_target_pairs={{0,7},{1,6},{2,5},{3,4},{4,3},{5,2},{6,1},{7,0},{8,15},{9,14},{10,... | collective-permute-start | bytes 786440 | tf_op jit(solution)/shard_map/ppermute | solution.py:263
  149.2 9.7 %copy-start.4 = (bf16[1024,128]{1,0:T(8,128)(2,1)}, bf16[1024,128]{1,0:T(8,128)(2,1)S(1)}, u32[]{:S(2)}) copy-start(bf16[1024,128]{1,0:T(8,128)(2,1)S(1)} %collective-permute-done.9.refs_3_) | copy-start | bytes 786436
  149.3 9.7 %copy-start.5 = (bf16[1024,128]{1,0:T(8,128)(2,1)}, bf16[1024,128]{1,0:T(8,128)(2,1)S(1)}, u32[]{:S(2)}) copy-start(bf16[1024,128]{1,0:T(8,128)(2,1)S(1)} %collective-permute-done.10.refs_4_) | copy-start | bytes 786436
  149.3 9.7 %copy-start.6 = (bf16[1024,128]{1,0:T(8,128)(2,1)}, bf16[1024,128]{1,0:T(8,128)(2,1)S(1)}, u32[]{:S(2)}) copy-start(bf16[1024,128]{1,0:T(8,128)(2,1)S(1)} %collective-permute-done.11.refs_5_) | copy-start | bytes 786436
  155.0 4.0 %copy-start.7 = (bf16[1024,128]{1,0:T(8,128)(2,1)}, bf16[1024,128]{1,0:T(8,128)(2,1)S(1)}, u32[]{:S(2)}) copy-start(bf16[1024,128]{1,0:T(8,128)(2,1)S(1)} %collective-permute-done.12.refs_6_) | copy-start | bytes 786436
  159.0 0.7 copy-start.8
  162.5 1.0 copy-start.1

commit v2 on v0

v2 whole, which is shorter than its diff:
```python
import functools

import jax
import jax.numpy as jnp
from jax import lax
from jax.experimental import pallas as pl
from jax.experimental.pallas import tpu as pltpu
from jax.sharding import Mesh, PartitionSpec as P

HEADS = 16
HEAD_DIM = 64
TILE = 128
LANES = 2 * HEAD_DIM
META_ROWS = 16
LOG2E = 1.4426950408889634
SCALE = HEAD_DIM ** (-0.5)
NEG_FILL = -1e30
PEAK = 1.15e9
MIB = 1024 * 1024
ATTEND_COST = 20
SPLIT_COST = 2
STACK_COST = 2
UNPACK_COST = 3

SMEM = pl.BlockSpec(memory_space=pltpu.SMEM)
VMEM = pl.BlockSpec(memory_space=pltpu.VMEM)


def call(kernel, name, out_shape, in_specs, *, cost, vmem=24, **more):
    return pl.pallas_call(
        kernel,
        out_shape=out_shape,
        in_specs=in_specs,
        out_specs=jax.tree.map(lambda _: VMEM, out_shape),
        compiler_params=pltpu.CompilerParams(vmem_limit_bytes=vmem * MIB),
        cost_estimate=pl.CostEstimate(
            flops=int(cost * PEAK), bytes_accessed=0, transcendentals=0
        ),
        name=name,
        **more,
    )


def bf16(*shape):
    return jax.ShapeDtypeStruct(shape, jnp.bfloat16)


def low_lanes(shape):
    return lax.broadcasted_iota(jnp.int32, shape, len(shape) - 1) < HEAD_DIM


def swap_halves(x):
    return jnp.concatenate([x[:, HEAD_DIM:], x[:, :HEAD_DIM]], axis=1)


def interleave(first, second):
    low = low_lanes(first.shape)
    swapped = swap_halves(second)
    return jnp.where(low, first, swapped), jnp.where(low, swapped, first)


def separate(even, odd):
    low = low_lanes(even.shape)
    return jnp.where(low, even, odd), swap_halves(jnp.where(low, odd, even))


def lane_is(shape, odd):
    return (lax.broadcasted_iota(jnp.int32, shape, len(shape) - 1) // HEAD_DIM) == odd


def in_order(odd, pair):
    a, b = pair
    return jnp.where(odd, b, a), jnp.where(odd, a, b)


def pair_lanes(base, place, i):
    return pl.ds(pl.multiple_of((base + ((place[2] >> 1) ^ i)) * LANES, LANES), LANES)


def pack_dimension(place, key_rows, value_rows, dims, shares):
    rows = key_rows.shape[0] // shares
    pairs = dims // 2

    def kernel(place, *refs):
        keys, values, outs = refs[:pairs], refs[pairs : 2 * pairs], refs[2 * pairs :]
        odd = (place[2] & 1) == 1
        for i in range(pairs):
            outs[2 * i][...], outs[2 * i + 1][...] = in_order(
                odd, interleave(keys[i][...], values[i][...])
            )

    def spec(i):
        return pl.BlockSpec((rows, LANES), lambda _, p: (p[1], p[0] * pairs + ((p[2] >> 1) ^ i)))

    return pl.pallas_call(
        kernel,
        grid_spec=pltpu.PrefetchScalarGridSpec(
            num_scalar_prefetch=1,
            grid=(1,),
            in_specs=[spec(i) for i in range(pairs)] * 2,
            out_specs=[pl.BlockSpec((rows, LANES), lambda _, p: (0, 0))] * dims,
        ),
        out_shape=[bf16(rows, LANES)] * dims,
        compiler_params=pltpu.CompilerParams(vmem_limit_bytes=24 * MIB),
        name="pack_dimension",
    )(place, *([key_rows] * pairs), *([value_rows] * pairs))


def pack_fact(place, queries, cotangent, block_lists, tile_lengths, dims):
    rows = queries.shape[0]
    tiles, slots = block_lists.shape
    parts = HEADS // dims

    def kernel(place, queries, cotangent, block_lists, tile_lengths, *outs):
        odd = (place[2] & 1) == 1
        row = lax.broadcasted_iota(jnp.int32, (META_ROWS, LANES), 0)
        lane = lax.broadcasted_iota(jnp.int32, (META_ROWS, LANES), 1)
        words = jnp.zeros((META_ROWS, LANES), jnp.int32)
        for t in range(tiles):
            for j in range(slots):
                words = jnp.where((row == t) & (lane == j), block_lists[t, j], words)
            words = jnp.where((row == t) & (lane == slots), tile_lengths[t], words)
        meta = words.astype(jnp.float32).astype(jnp.bfloat16)
        for k in range(parts):
            base = (place[0] ^ k) * (dims // 2)
            for i in range(dims // 2):
                span = pair_lanes(base, place, i)
                pair = in_order(odd, interleave(queries[:, span], cotangent[:, span]))
                for s in range(2):
                    outs[k][2 * i + s, :rows, :] = pair[s]
                    outs[k][2 * i + s, rows:, :] = meta

    return call(
        kernel,
        "pack_fact",
        [bf16(dims, rows + META_ROWS, LANES)] * parts,
        [SMEM, VMEM, VMEM, SMEM, SMEM],
        cost=4,
    )(place, queries, cotangent, block_lists, tile_lengths)


def merge_fact(parts):
    dims, rows, _ = parts[0].shape

    def kernel(*refs):
        for r in range(dims):
            for k in range(len(parts)):
                refs[len(parts) + r][k] = refs[k][r]

    return call(
        kernel, "merge_fact", [bf16(len(parts), rows, LANES)] * dims, [VMEM] * len(parts), cost=2
    )(*parts)


def stack_chunks(chunks, cost):
    rows = chunks[0].shape[0]

    def kernel(*refs):
        for r in range(len(chunks)):
            refs[-1][r * rows : (r + 1) * rows, :] = refs[r][...]

    return call(
        kernel, "stack_chunks", bf16(len(chunks) * rows, LANES), [VMEM] * len(chunks), cost=cost
    )(*chunks)


def attend(place, facts, tables, rows, slots):
    dims, shares = len(facts), len(tables)
    parts = facts[0].shape[0]
    sources = dims * parts
    table_rows = tables[0].shape[0]
    owner_blocks = table_rows // TILE // dims
    tiles_each = rows // TILE

    def kernel(place, *refs):
        facts_in, tables_in = refs[:dims], refs[dims : dims + shares]
        fact_outs = refs[dims + shares : 2 * dims + shares]
        own_out = refs[2 * dims + shares]
        share_outs = refs[2 * dims + shares + 1 : 2 * dims + 2 * shares]
        fact, fact_out, table, total, words, meta, sem = refs[2 * dims + 2 * shares :]
        odd = place[2] & 1
        for r in range(dims):
            words[r * parts : (r + 1) * parts] = (
                facts_in[r][:, rows:, :].astype(jnp.float32).astype(jnp.int32)
            )
        copy = pltpu.make_async_copy(words, meta, sem)
        copy.start()
        for r in range(dims):
            fact[r * parts : (r + 1) * parts] = facts_in[r][:, :rows, :]
        for k in range(shares):
            table[k * table_rows : (k + 1) * table_rows, :] = tables_in[k][...]
        total[...] = jnp.zeros_like(total)
        copy.wait()
        first = lane_is((TILE, LANES), odd)

        def row_of(block):
            owner, place_in = block // (shares * owner_blocks), block % (shares * owner_blocks)
            share, at = place_in // owner_blocks, place_in % owner_blocks
            index = ((share ^ place[1]) * dims + (owner ^ place[2])) * owner_blocks + at
            return pl.multiple_of(index * TILE, TILE)

        def step(source, lengths, count):
            left, places, kept, pairs = [], [], [], []
            for tile in range(tiles_each):
                both = fact[source, tile * TILE : (tile + 1) * TILE, :]
                zero = jnp.zeros_like(both)
                left.append(
                    jnp.concatenate(
                        [jnp.where(first, both, zero), jnp.where(first, zero, both)], axis=0
                    )
                )
                places.append([row_of(meta[source, tile, j]) for j in range(count)])
            for tile in range(tiles_each):
                kv = jnp.concatenate([table[pl.ds(at, TILE), :] for at in places[tile]], axis=0)
                products = lax.dot_general(
                    kv, left[tile], (((1,), (1,)), ((), ())), preferred_element_type=jnp.float32
                )
                scores = products[:, :TILE] * (SCALE * LOG2E)
                live = [scores[:TILE]] + [
                    jnp.where(lengths[tile] > j, scores[j * TILE : (j + 1) * TILE], NEG_FILL)
                    for j in range(1, count)
                ]
                scores = jnp.concatenate(live, axis=0)
                dweights = products[:, TILE:]
                terms = jnp.exp2(scores - jnp.max(scores, axis=0, keepdims=True))
                weights = terms * (1.0 / jnp.sum(terms, axis=0, keepdims=True))
                row_delta = jnp.sum(weights * dweights, axis=0, keepdims=True)
                dscores = weights * (dweights - row_delta)
                kept.append(kv)
                pairs.append(
                    jnp.concatenate(
                        [dscores.astype(jnp.bfloat16), weights.astype(jnp.bfloat16)], axis=1
                    )
                )
            for tile in range(tiles_each):
                out = lax.dot_general(
                    pairs[tile],
                    kept[tile],
                    (((0,), (0,)), ((), ())),
                    preferred_element_type=jnp.float32,
                )
                fact_out[source, tile * TILE : (tile + 1) * TILE, :] = jnp.where(
                    first, out[:TILE] * SCALE, out[TILE:]
                ).astype(jnp.bfloat16)
                grads = jnp.dot(pairs[tile], left[tile], preferred_element_type=jnp.float32)
                for j, at in enumerate(places[tile]):
                    total[pl.ds(at, TILE), :] += grads[j * TILE : (j + 1) * TILE]

        def source_step(source, carry):
            lengths = [meta[source, tile, slots] for tile in range(tiles_each)]
            longest = functools.reduce(jnp.maximum, lengths)
            for count in range(1, slots + 1):
                pl.when(longest == count)(functools.partial(step, source, lengths, count))
            return carry

        lax.fori_loop(0, sources, source_step, 0)
        for r in range(dims):
            fact_outs[r][...] = fact_out[r * parts : (r + 1) * parts]
        factor = jnp.where(lane_is((table_rows, LANES), odd), SCALE, 1.0)
        own_out[...] = total[:table_rows] * factor
        for k in range(1, shares):
            share_outs[k - 1][...] = (
                total[k * table_rows : (k + 1) * table_rows] * factor
            ).astype(jnp.bfloat16)

    results = call(
        kernel,
        "attend",
        [bf16(parts, rows, LANES)] * dims
        + [jax.ShapeDtypeStruct((table_rows, LANES), jnp.float32)]
        + [bf16(table_rows, LANES)] * (shares - 1),
        [SMEM] + [VMEM] * (dims + shares),
        cost=ATTEND_COST,
        vmem=40,
        scratch_shapes=[
            pltpu.VMEM((sources, rows, LANES), jnp.bfloat16),
            pltpu.VMEM((sources, rows, LANES), jnp.bfloat16),
            pltpu.VMEM((shares * table_rows, LANES), jnp.bfloat16),
            pltpu.VMEM((shares * table_rows, LANES), jnp.float32),
            pltpu.VMEM((sources, META_ROWS, LANES), jnp.int32),
            pltpu.SMEM((sources, META_ROWS, LANES), jnp.int32),
            pltpu.SemaphoreType.DMA,
        ],
    )(place, *facts, *tables)
    return results[:dims], results[dims], results[dims + 1 :]


def split_fact(chunks):
    parts, rows, _ = chunks[0].shape
    dims = len(chunks)

    def kernel(*refs):
        for k in range(parts):
            for r in range(dims):
                refs[dims + k][r] = refs[r][k]

    return call(
        kernel, "split_fact", [bf16(dims, rows, LANES)] * parts, [VMEM] * dims, cost=SPLIT_COST
    )(*chunks)


def unpack_fact(place, parts):
    dims, rows, _ = parts[0].shape

    def kernel(place, *refs):
        attended, query_grad = refs[len(parts) :]
        odd = (place[2] & 1) == 1
        for k in range(len(parts)):
            base = (place[0] ^ k) * (dims // 2)
            for i in range(dims // 2):
                span = pair_lanes(base, place, i)
                pair = in_order(odd, (refs[k][2 * i], refs[k][2 * i + 1]))
                query_grad[:, span], attended[:, span] = separate(*pair)

    return call(
        kernel,
        "unpack_fact",
        [bf16(rows, HEADS * HEAD_DIM)] * 2,
        [SMEM] + [VMEM] * len(parts),
        cost=2.4,
    )(place, *parts)


def sum_shares(place, own, others, dims, per_fact):
    rows = own.shape[0] // dims

    def kernel(place, own, *refs):
        others_in, outs = refs[: len(others)], refs[len(others) :]
        for r in range(dims):
            at = pl.multiple_of((r ^ (place[1] * per_fact)) * rows, rows)
            total = own[pl.ds(at, rows), :]
            for other in others_in:
                total += other[pl.ds(at, rows), :].astype(jnp.float32)
            outs[r][...] = total.astype(jnp.bfloat16)

    return call(
        kernel, "sum_shares", [bf16(rows, LANES)] * dims, [SMEM] + [VMEM] * (1 + len(others)), cost=2
    )(place, own, *others)


def unpack_dimension(place, chunks, shares, per_fact):
    dims = len(chunks)
    rows = chunks[0].shape[0]

    def kernel(place, *refs):
        key_grad, value_grad = refs[dims:]
        odd = (place[2] & 1) == 1
        for i in range(dims // 2):
            source = place[2] ^ (2 * i)
            share = (source // per_fact) ^ place[1]
            pair = in_order(odd, (refs[2 * i][...], refs[2 * i + 1][...]))
            at = pl.ds(pl.multiple_of(share * rows, rows), rows)
            span = pl.ds(pl.multiple_of(((source % per_fact) // 2) * LANES, LANES), LANES)
            key_grad[at, span], value_grad[at, span] = separate(*pair)

    return call(
        kernel,
        "unpack_dimension",
        [bf16(shares * rows, per_fact * HEAD_DIM)] * 2,
        [SMEM] + [VMEM] * dims,
        cost=UNPACK_COST,
    )(place, *chunks)


def by_xor(part, axis, index, count):
    if index == 0:
        return part
    return lax.ppermute(part, axis, [(i, i ^ index) for i in range(count)])


def body(xs, shares, dims, queries, key_rows, value_rows, cotangent, block_lists, tile_lengths):
    per_fact = dims // shares
    rows, slots = queries.shape[0], block_lists.shape[1]
    place = jnp.stack([lax.axis_index(a) for a in ("x", "share", "dim")]).astype(jnp.int32)

    chunks = pack_dimension(place, key_rows, value_rows, dims, shares)
    chunks = [by_xor(chunk, "dim", r, dims) for r, chunk in enumerate(chunks)]
    table = stack_chunks(chunks, STACK_COST)
    tables = [by_xor(table, "share", k, shares) for k in range(shares)]

    parts = pack_fact(place, queries, cotangent, block_lists, tile_lengths, dims)
    parts = [by_xor(part, "x", k, xs) for k, part in enumerate(parts)]
    facts = merge_fact(parts)
    facts = [by_xor(chunk, "dim", r, dims) for r, chunk in enumerate(facts)]

    fact_outs, own, others = attend(place, facts, tables, rows, slots)

    fact_outs = [by_xor(chunk, "dim", r, dims) for r, chunk in enumerate(fact_outs)]
    parts = split_fact(fact_outs)
    parts = [by_xor(part, "x", k, xs) for k, part in enumerate(parts)]
    attended, query_grad = unpack_fact(place, parts)

    others = [by_xor(other, "share", k + 1, shares) for k, other in enumerate(others)]
    chunks = sum_shares(place, own, others, dims, per_fact)
    grads = []
    for r, chunk in enumerate(chunks):
        pairs = [
            (c * dims + d, (d // per_fact) * dims + (d ^ r ^ (c * per_fact)))
            for c in range(shares)
            for d in range(dims)
        ]
        grads.append(lax.ppermute(chunk, ("share", "dim"), pairs))
    key_grad, value_grad = unpack_dimension(place, grads, shares, per_fact)
    return attended, query_grad, key_grad, value_grad


def solution(mesh):
    facts, dims = mesh.shape["fact"], mesh.shape["dim"]
    xs = HEADS // dims
    shares = facts // xs
    fine = Mesh(mesh.devices.reshape(xs, shares, dims), ("x", "share", "dim"))
    every = ("x", "share", "dim")
    in_specs = (
        P(every, None),
        P("dim", None),
        P("dim", None),
        P(every, None),
        P(every, None),
        P(every),
    )
    out_specs = (
        P(every, None),
        P(every, None),
        P("dim", ("x", "share")),
        P("dim", ("x", "share")),
    )
    return jax.shard_map(
        functools.partial(body, xs, shares, dims),
        mesh=fine,
        in_specs=in_specs,
        out_specs=out_specs,
        check_vma=False,
    )
```

time: 457 us -> 145 us (0.32); the launches traced: 451 us -> 145 us
  blocking collectives: 110 us -> 0 us
  local copies, waits for them, and re-layouts: 108 us -> 3.2 us
  matrix products: 83.2 us -> 0 us
  waiting for transfers between devices: 105 us -> 43.6 us
  starting transfers between devices: 13.5 us -> 71.6 us
  Pallas kernels: 0 us -> 25.4 us
  other arithmetic: 15.8 us -> 0.08 us
  between operations: 14.6 us -> 0.78 us
    all_to_all x2 -> x0, blocking collectives: 110 us -> none  [the longest x1 96.9 us: body(): lax.all_to_all(partial_keys, 'dim', split_axis=0, concat_axis=0, tiled=True)]
    all_to_all x3 -> x0, waiting for transfers between devices: 82.2 us -> none  [the longest x1 42.6 us: body(): lax.all_to_all(partial_values, 'dim', split_axis=0, concat_axis=0, tiled=...]
    ppermute x0 -> x33, starting transfers between devices: none -> 71.6 us  [the longest x25 51 us: by_xor(): return lax.ppermute(part, axis, [(i, i ^ index) for i in range(count)])]
    dot_general x16 -> x0, matrix products: 66.9 us -> none  [the longest x2 11.2 us: attend_group(): jnp.einsum('tqhe,tkhe->thqk', grad_group, value_group, preferred_element_...]
    ppermute x0 -> x33, waiting for transfers between devices: none -> 43.6 us  [the longest x25 38.8 us: by_xor(): return lax.ppermute(part, axis, [(i, i ^ index) for i in range(count)])]
    reshape x8 -> x0, local copies, waits for them, and re-layouts: 36.1 us -> none  [the longest x2 11.7 us: one_group(): key_parts.append(key_grad.reshape(per_step, slot_count, TILE, span))]
    unnamed x34 -> x12, local copies, waits for them, and re-layouts: 32.8 us -> 3.2 us
    pallas_call x0 -> x9, Pallas kernels: none -> 25.4 us  [the longest x1 18.9 us: attend(): call(kernel, 'attend', [bf16(parts, rows, LANES)] * dims + [jax.ShapeDtyp...]
  transfers between devices with their start and end apart: 5 -> 33, of which waited for: 3 -> 10; matrix products, arithmetic and copies ran while one was open for 41% -> 0% of each run, Pallas kernels for 0% -> 3%
where the time goes in v2:
time: 145 us
  starting transfers between devices  71.6 us (49%)
  waiting for transfers between devices  43.6 us (30%)
  Pallas kernels  25.4 us (18%)
  local copies, waits for them, and re-layouts  3.2 us (2%)
    ppermute x25, starting transfers between devices, by_xor(): return lax.ppermute(part, axis, [(i, i ^ index) for i in range(count)])  51 us
    ppermute x25, waiting for transfers between devices, by_xor(): return lax.ppermute(part, axis, [(i, i ^ index) for i in range(count)])  38.8 us
    ppermute x8, starting transfers between devices, body(): grads.append(lax.ppermute(chunk, ('share', 'dim'), pairs))  20.6 us
    pallas_call x1, Pallas kernels, attend(): call(kernel, 'attend', [bf16(parts, rows, LANES)] * dims + [jax.ShapeDtyp...  18.9 us
    ppermute x8, waiting for transfers between devices, body(): grads.append(lax.ppermute(chunk, ('share', 'dim'), pairs))  4.73 us
    unnamed x12, local copies, waits for them, and re-layouts  3.2 us
  transfers between devices with their start and end apart: 33, of which 10 were waited for; matrix products, arithmetic and copies ran while one was open for 0% of the time, Pallas kernels for 3%

profile of v2, /device:TPU:0, one launch (start us, length us, event | category | flops | bytes accessed | tf_op | source)
XLA Modules:
  0.0 144.6 jit_solution(6388958424502391688)
XLA Ops:
  0.6 0.1 pad_add_fusion.place
  0.7 1.6 %copy-done = bf16[1024,1024]{1,0:T(8,128)(2,1)S(1)} copy-done((bf16[1024,1024]{1,0:T(8,128)(2,1)S(1)}, bf16[1024,1024]{1,0:T(8,128)(2,1)}, u32[]{:S(2)}) %copy-start) | copy-done | bytes 2097176
  2.3 1.6 %copy-done.1 = bf16[1024,1024]{1,0:T(8,128)(2,1)S(1)} copy-done((bf16[1024,1024]{1,0:T(8,128)(2,1)S(1)}, bf16[1024,1024]{1,0:T(8,128)(2,1)}, u32[]{:S(2)}) %copy-start.1) | copy-done | bytes 2097176
  3.9 1.0 pack_dimension.1
  5.0 3.0 %collective-permute-start.8 = (bf16[512,128]{1,0:T(8,128)(2,1)S(1)}, bf16[512,128]{1,0:T(8,128)(2,1)S(1)}, u32[]{:S(2)}, u32[]{:S(2)}) collective-permute-start(bf16[512,128]{1,0:T(8,128)(2,1)S(1)} %get-tuple-element.57), channel_id=1, source_target_pairs={{0,1},{1,0},{2,3},{3,2},{4,5},{5,4},{6,7},{7,6},{8,9},{9,8},{10,11... | collective-permute-start | bytes 393224 | tf_op jit(solution)/shard_map/ppermute | solution.py:368
  8.0 1.6 %collective-permute-start.9 = (bf16[512,128]{1,0:T(8,128)(2,1)S(1)}, bf16[512,128]{1,0:T(8,128)(2,1)S(1)}, u32[]{:S(2)}, u32[]{:S(2)}) collective-permute-start(bf16[512,128]{1,0:T(8,128)(2,1)S(1)} %get-tuple-element.58), channel_id=1, source_target_pairs={{0,2},{1,3},{2,0},{3,1},{4,6},{5,7},{6,4},{7,5},{8,10},{9,11},{10,... | collective-permute-start | bytes 393224 | tf_op jit(solution)/shard_map/ppermute | solution.py:368
  9.6 3.0 %collective-permute-start.11 = (bf16[512,128]{1,0:T(8,128)(2,1)S(1)}, bf16[512,128]{1,0:T(8,128)(2,1)S(1)}, u32[]{:S(2)}, u32[]{:S(2)}) collective-permute-start(bf16[512,128]{1,0:T(8,128)(2,1)S(1)} %get-tuple-element.60), channel_id=1, source_target_pairs={{0,4},{1,5},{2,6},{3,7},{4,0},{5,1},{6,2},{7,3},{8,12},{9,13},{10,... | collective-permute-start | bytes 393224 | tf_op jit(solution)/shard_map/ppermute | solution.py:368
  12.6 1.3 collective-permute-start.12
  13.8 3.6 %collective-permute-start.13 = (bf16[512,128]{1,0:T(8,128)(2,1)S(1)}, bf16[512,128]{1,0:T(8,128)(2,1)S(1)}, u32[]{:S(2)}, u32[]{:S(2)}) collective-permute-start(bf16[512,128]{1,0:T(8,128)(2,1)S(1)} %get-tuple-element.62), channel_id=1, source_target_pairs={{0,6},{1,7},{2,4},{3,5},{4,2},{5,3},{6,0},{7,1},{8,14},{9,15},{10,... | collective-permute-start | bytes 393224 | tf_op jit(solution)/shard_map/ppermute | solution.py:368
  17.5 1.3 collective-permute-done.9.refs_2_
  18.7 0.7 collective-permute-start.14
  19.4 1.0 pack_fact.1
  20.4 1.6 %collective-permute-start = (bf16[8,272,128]{2,1,0:T(8,128)(2,1)S(1)}, bf16[8,272,128]{2,1,0:T(8,128)(2,1)S(1)}, u32[]{:S(2)}, u32[]{:S(2)}) collective-permute-start(bf16[8,272,128]{2,1,0:T(8,128)(2,1)S(1)} %get-tuple-element.47), channel_id=1, source_target_pairs={{0,16},{16,0},{1,17},{17,1},{2,18},{18,2},{3,19},{19,3},{4,20},{20... | collective-permute-start | bytes 1671176 | tf_op jit(solution)/shard_map/ppermute | solution.py:368
  22.0 10.0 %collective-permute-done.12.refs_5_ = bf16[512,128]{1,0:T(8,128)(2,1)S(1)} collective-permute-done((bf16[512,128]{1,0:T(8,128)(2,1)S(1)}, bf16[512,128]{1,0:T(8,128)(2,1)S(1)}, u32[]{:S(2)}, u32[]{:S(2)}) %collective-permute-start.12) | collective-permute-done | bytes 131104 | tf_op jit(solution)/shard_map/ppermute | solution.py:368
  32.2 0.8 collective-permute-done.refs_1_
  33.0 1.8 %collective-permute-start.1 = (bf16[2,272,128]{2,1,0:T(8,128)(2,1)S(1)}, bf16[2,272,128]{2,1,0:T(8,128)(2,1)S(1)}, u32[]{:S(2)}, u32[]{:S(2)}) collective-permute-start(bf16[2,272,128]{2,1,0:T(8,128)(2,1)S(1)} %get-tuple-element.49), channel_id=1, source_target_pairs={{0,1},{1,0},{2,3},{3,2},{4,5},{5,4},{6,7},{7,6},{8,9},{9,8},{10,11... | collective-permute-start | bytes 417800 | tf_op jit(solution)/shard_map/ppermute | solution.py:368
  34.9 2.8 %collective-permute-start.2 = (bf16[2,272,128]{2,1,0:T(8,128)(2,1)S(1)}, bf16[2,272,128]{2,1,0:T(8,128)(2,1)S(1)}, u32[]{:S(2)}, u32[]{:S(2)}) collective-permute-start(bf16[2,272,128]{2,1,0:T(8,128)(2,1)S(1)} %get-tuple-element.50), channel_id=1, source_target_pairs={{0,2},{1,3},{2,0},{3,1},{4,6},{5,7},{6,4},{7,5},{8,10},{9,11},{10,... | collective-permute-start | bytes 417800 | tf_op jit(solution)/shard_map/ppermute | solution.py:368
  37.7 1.1 collective-permute-start.3
  38.8 3.5 %collective-permute-start.4 = (bf16[2,272,128]{2,1,0:T(8,128)(2,1)S(1)}, bf16[2,272,128]{2,1,0:T(8,128)(2,1)S(1)}, u32[]{:S(2)}, u32[]{:S(2)}) collective-permute-start(bf16[2,272,128]{2,1,0:T(8,128)(2,1)S(1)} %get-tuple-element.52), channel_id=1, source_target_pairs={{0,4},{1,5},{2,6},{3,7},{4,0},{5,1},{6,2},{7,3},{8,12},{9,13},{10,... | collective-permute-start | bytes 417800 | tf_op jit(solution)/shard_map/ppermute | solution.py:368
  42.4 2.6 %collective-permute-start.5 = (bf16[2,272,128]{2,1,0:T(8,128)(2,1)S(1)}, bf16[2,272,128]{2,1,0:T(8,128)(2,1)S(1)}, u32[]{:S(2)}, u32[]{:S(2)}) collective-permute-start(bf16[2,272,128]{2,1,0:T(8,128)(2,1)S(1)} %get-tuple-element.53), channel_id=1, source_target_pairs={{0,5},{1,4},{2,7},{3,6},{4,1},{5,0},{6,3},{7,2},{8,13},{9,12},{10,... | collective-permute-start | bytes 417800 | tf_op jit(solution)/shard_map/ppermute | solution.py:368
  44.9 2.8 %collective-permute-start.6 = (bf16[2,272,128]{2,1,0:T(8,128)(2,1)S(1)}, bf16[2,272,128]{2,1,0:T(8,128)(2,1)S(1)}, u32[]{:S(2)}, u32[]{:S(2)}) collective-permute-start(bf16[2,272,128]{2,1,0:T(8,128)(2,1)S(1)} %get-tuple-element.54), channel_id=1, source_target_pairs={{0,6},{1,7},{2,4},{3,5},{4,2},{5,3},{6,0},{7,1},{8,14},{9,15},{10,... | collective-permute-start | bytes 417800 | tf_op jit(solution)/shard_map/ppermute | solution.py:368
  47.7 3.0 %collective-permute-done.3.refs_3_ = bf16[2,272,128]{2,1,0:T(8,128)(2,1)S(1)} collective-permute-done((bf16[2,272,128]{2,1,0:T(8,128)(2,1)S(1)}, bf16[2,272,128]{2,1,0:T(8,128)(2,1)S(1)}, u32[]{:S(2)}, u32[]{:S(2)}) %collective-permute-start.3) | collective-permute-done | bytes 139296 | tf_op jit(solution)/shard_map/ppermute | solution.py:368
  50.8 1.2 collective-permute-start.7
  51.9 10.8 %collective-permute-done.5.refs_5_ = bf16[2,272,128]{2,1,0:T(8,128)(2,1)S(1)} collective-permute-done((bf16[2,272,128]{2,1,0:T(8,128)(2,1)S(1)}, bf16[2,272,128]{2,1,0:T(8,128)(2,1)S(1)}, u32[]{:S(2)}, u32[]{:S(2)}) %collective-permute-start.5) | collective-permute-done | bytes 139296 | tf_op jit(solution)/shard_map/ppermute | solution.py:368
  62.7 18.9 %attend.1 = (bf16[2,256,128]{2,1,0:T(8,128)(2,1)S(1)}, bf16[2,256,128]{2,1,0:T(8,128)(2,1)S(1)}, bf16[2,256,128]{2,1,0:T(8,128)(2,1)S(1)}, bf16[2,256,128]{2,1,0...) custom-call(s32[3]{0:T(128)S(1)} %pad_add_fusion.place, ...), custom_call_target="tpu_custom_call" | custom-call | flops 23000000512 | tf_op jit(solution)/shard_map/attend/pallas_call | solution.py:266
  81.7 1.0 collective-permute-start.16
  82.8 6.5 %collective-permute-start.17 = (bf16[2,256,128]{2,1,0:T(8,128)(2,1)S(1)}, bf16[2,256,128]{2,1,0:T(8,128)(2,1)S(1)}, u32[]{:S(2)}, u32[]{:S(2)}) collective-permute-start(bf16[2,256,128]{2,1,0:T(8,128)(2,1)S(1)} %get-tuple-element.66), channel_id=1, source_target_pairs={{0,2},{1,3},{2,0},{3,1},{4,6},{5,7},{6,4},{7,5},{8,10},{9,11},{10,... | collective-permute-start | bytes 393224 | tf_op jit(solution)/shard_map/ppermute | solution.py:368
  89.3 2.9 %collective-permute-start.19 = (bf16[2,256,128]{2,1,0:T(8,128)(2,1)S(1)}, bf16[2,256,128]{2,1,0:T(8,128)(2,1)S(1)}, u32[]{:S(2)}, u32[]{:S(2)}) collective-permute-start(bf16[2,256,128]{2,1,0:T(8,128)(2,1)S(1)} %get-tuple-element.68), channel_id=1, source_target_pairs={{0,4},{1,5},{2,6},{3,7},{4,0},{5,1},{6,2},{7,3},{8,12},{9,13},{10,... | collective-permute-start | bytes 393224 | tf_op jit(solution)/shard_map/ppermute | solution.py:368
  92.2 2.9 %collective-permute-start.20 = (bf16[2,256,128]{2,1,0:T(8,128)(2,1)S(1)}, bf16[2,256,128]{2,1,0:T(8,128)(2,1)S(1)}, u32[]{:S(2)}, u32[]{:S(2)}) collective-permute-start(bf16[2,256,128]{2,1,0:T(8,128)(2,1)S(1)} %get-tuple-element.69), channel_id=1, source_target_pairs={{0,5},{1,4},{2,7},{3,6},{4,1},{5,0},{6,3},{7,2},{8,13},{9,12},{10,... | collective-permute-start | bytes 393224 | tf_op jit(solution)/shard_map/ppermute | solution.py:368
  95.1 2.8 %collective-permute-done.17.refs_2_ = bf16[2,256,128]{2,1,0:T(8,128)(2,1)S(1)} collective-permute-done((bf16[2,256,128]{2,1,0:T(8,128)(2,1)S(1)}, bf16[2,256,128]{2,1,0:T(8,128)(2,1)S(1)}, u32[]{:S(2)}, u32[]{:S(2)}) %collective-permute-start.17) | collective-permute-done | bytes 131104 | tf_op jit(solution)/shard_map/ppermute | solution.py:368
  97.8 2.6 %collective-permute-start.21 = (bf16[2,256,128]{2,1,0:T(8,128)(2,1)S(1)}, bf16[2,256,128]{2,1,0:T(8,128)(2,1)S(1)}, u32[]{:S(2)}, u32[]{:S(2)}) collective-permute-start(bf16[2,256,128]{2,1,0:T(8,128)(2,1)S(1)} %get-tuple-element.70), channel_id=1, source_target_pairs={{0,6},{1,7},{2,4},{3,5},{4,2},{5,3},{6,0},{7,1},{8,14},{9,15},{10,... | collective-permute-start | bytes 393224 | tf_op jit(solution)/shard_map/ppermute | solution.py:368
  100.4 2.8 %collective-permute-start.22 = (bf16[2,256,128]{2,1,0:T(8,128)(2,1)S(1)}, bf16[2,256,128]{2,1,0:T(8,128)(2,1)S(1)}, u32[]{:S(2)}, u32[]{:S(2)}) collective-permute-start(bf16[2,256,128]{2,1,0:T(8,128)(2,1)S(1)} %get-tuple-element.71), channel_id=1, source_target_pairs={{0,7},{1,6},{2,5},{3,4},{4,3},{5,2},{6,1},{7,0},{8,15},{9,14},{10,... | collective-permute-start | bytes 393224 | tf_op jit(solution)/shard_map/ppermute | solution.py:368
  103.3 7.8 %collective-permute-done.20.refs_5_ = bf16[2,256,128]{2,1,0:T(8,128)(2,1)S(1)} collective-permute-done((bf16[2,256,128]{2,1,0:T(8,128)(2,1)S(1)}, bf16[2,256,128]{2,1,0:T(8,128)(2,1)S(1)}, u32[]{:S(2)}, u32[]{:S(2)}) %collective-permute-start.20) | collective-permute-done | bytes 131104 | tf_op jit(solution)/shard_map/ppermute | solution.py:368
  111.1 1.5 %collective-permute-start.23 = (bf16[8,256,128]{2,1,0:T(8,128)(2,1)S(1)}, bf16[8,256,128]{2,1,0:T(8,128)(2,1)S(1)}, u32[]{:S(2)}, u32[]{:S(2)}) collective-permute-start(bf16[8,256,128]{2,1,0:T(8,128)(2,1)S(1)} %get-tuple-element.73), channel_id=1, source_target_pairs={{0,16},{16,0},{1,17},{17,1},{2,18},{18,2},{3,19},{19,3},{4,20},{20... | collective-permute-start | bytes 1572872 | tf_op jit(solution)/shard_map/ppermute | solution.py:368
  112.7 0.8 sum_shares.1
  113.5 0.7 collective-permute-start.25
  114.2 1.5 %collective-permute-start.26 = (bf16[512,128]{1,0:T(8,128)(2,1)S(1)}, bf16[512,128]{1,0:T(8,128)(2,1)S(1)}, u32[]{:S(2)}, u32[]{:S(2)}) collective-permute-start(bf16[512,128]{1,0:T(8,128)(2,1)S(1)} %get-tuple-element.79), channel_id=1, source_target_pairs={{0,1},{1,0},{2,3},{3,2},{4,13},{5,12},{6,15},{7,14},{8,5},{9,4},{1... | collective-permute-start | bytes 393224 | tf_op jit(solution)/shard_map/ppermute | solution.py:402
  115.7 4.7 %collective-permute-start.27 = (bf16[512,128]{1,0:T(8,128)(2,1)S(1)}, bf16[512,128]{1,0:T(8,128)(2,1)S(1)}, u32[]{:S(2)}, u32[]{:S(2)}) collective-permute-start(bf16[512,128]{1,0:T(8,128)(2,1)S(1)} %get-tuple-element.80), channel_id=1, source_target_pairs={{0,2},{1,3},{2,0},{3,1},{4,14},{5,15},{6,12},{7,13},{8,6},{9,7},{1... | collective-permute-start | bytes 393224 | tf_op jit(solution)/shard_map/ppermute | solution.py:402
  120.4 0.5 collective-permute-start.28
  120.9 2.3 %collective-permute-done.23.refs_1_ = bf16[8,256,128]{2,1,0:T(8,128)(2,1)S(1)} collective-permute-done((bf16[8,256,128]{2,1,0:T(8,128)(2,1)S(1)}, bf16[8,256,128]{2,1,0:T(8,128)(2,1)S(1)}, u32[]{:S(2)}, u32[]{:S(2)}) %collective-permute-start.23) | collective-permute-done | bytes 524320 | tf_op jit(solution)/shard_map/ppermute | solution.py:368
  123.2 8.2 %collective-permute-start.29 = (bf16[512,128]{1,0:T(8,128)(2,1)S(1)}, bf16[512,128]{1,0:T(8,128)(2,1)S(1)}, u32[]{:S(2)}, u32[]{:S(2)}) collective-permute-start(bf16[512,128]{1,0:T(8,128)(2,1)S(1)} %get-tuple-element.82), channel_id=1, source_target_pairs={{0,4},{1,5},{2,6},{3,7},{4,8},{5,9},{6,10},{7,11},{8,0},{9,1},{10,... | collective-permute-start | bytes 393224 | tf_op jit(solution)/shard_map/ppermute | solution.py:402
  131.4 0.8 collective-permute-start.30
  132.2 1.2 collective-permute-start.31
  133.4 3.1 %collective-permute-start.32 = (bf16[512,128]{1,0:T(8,128)(2,1)S(1)}, bf16[512,128]{1,0:T(8,128)(2,1)S(1)}, u32[]{:S(2)}, u32[]{:S(2)}) collective-permute-start(bf16[512,128]{1,0:T(8,128)(2,1)S(1)} %get-tuple-element.85), channel_id=1, source_target_pairs={{0,7},{1,6},{2,5},{3,4},{4,11},{5,10},{6,9},{7,8},{8,3},{9,2},{10,... | collective-permute-start | bytes 393224 | tf_op jit(solution)/shard_map/ppermute | solution.py:402
  136.4 1.7 %unpack_fact.1 = (bf16[256,1024]{1,0:T(8,128)(2,1)}, bf16[256,1024]{1,0:T(8,128)(2,1)}) custom-call(s32[3]{0:T(128)S(1)} %pad_add_fusion.place, bf16[8,256,128]{2,1,0:T(8,128)(2,1)S(1)} %get-tuple-element.72.refs_0_, bf16[8,256,128]{2,1,0:T(8,128)(2,1)S(1)} %collective-permute-done.23.refs_1_), custom_call_target="tpu_custom_call" | custom-call | flops 2760000000 | tf_op jit(solution)/shard_map/unpack_fact/pallas_call | solution.py:315
  138.2 1.3 collective-permute-done.31.refs_6_
  139.4 3.5 %collective-permute-done.32.refs_7_ = bf16[512,128]{1,0:T(8,128)(2,1)S(1)} collective-permute-done((bf16[512,128]{1,0:T(8,128)(2,1)S(1)}, bf16[512,128]{1,0:T(8,128)(2,1)S(1)}, u32[]{:S(2)}, u32[]{:S(2)}) %collective-permute-start.32) | collective-permute-done | bytes 131104 | tf_op jit(solution)/shard_map/ppermute | solution.py:402
  142.9 1.7 %unpack_dimension.1 = (bf16[1024,256]{1,0:T(8,128)(2,1)}, bf16[1024,256]{1,0:T(8,128)(2,1)}) custom-call(s32[3]{0:T(128)S(1)} %pad_add_fusion.place, bf16[512,128]{1,0:T(8,128)(2,1)S(1)} %collective-permute-done.25.refs_0_, bf16[512,128]{1,0:T(8,128)(2,1)S(1)} %collective-permute-done.26.refs_1_, bf16[512,128]{1,0:T(8,128)(2,1)S(1)} %collective-permute-done.27.refs_2_, ...), custom_call_target="tpu_custom_call" | custom-call | flops 3449999872 | tf_op jit(solution)/shard_map/unpack_dimension/pallas_call | solution.py:356
  (40 shorter events, 0.4 us)
Async XLA Ops:
  0.7 1.6 %copy-start = (bf16[1024,1024]{1,0:T(8,128)(2,1)S(1)}, bf16[1024,1024]{1,0:T(8,128)(2,1)}, u32[]{:S(2)}) copy-start(bf16[1024,1024]{1,0:T(8,128)(2,1)} %refs_3_.1) | copy-start | bytes 6291460
  2.3 1.6 %copy-start.1 = (bf16[1024,1024]{1,0:T(8,128)(2,1)S(1)}, bf16[1024,1024]{1,0:T(8,128)(2,1)}, u32[]{:S(2)}) copy-start(bf16[1024,1024]{1,0:T(8,128)(2,1)} %refs_7_.1) | copy-start | bytes 6291460
  3.9 15.5 %copy-start.2 = (bf16[256,1024]{1,0:T(8,128)(2,1)S(1)}, bf16[256,1024]{1,0:T(8,128)(2,1)}, u32[]{:S(2)}) copy-start(bf16[256,1024]{1,0:T(8,128)(2,1)} %queries.1) | copy-start | bytes 1572868
  3.9 15.5 %copy-start.3 = (bf16[256,1024]{1,0:T(8,128)(2,1)S(1)}, bf16[256,1024]{1,0:T(8,128)(2,1)}, u32[]{:S(2)}) copy-start(bf16[256,1024]{1,0:T(8,128)(2,1)} %cotangent.1) | copy-start | bytes 1572868
  3.9 15.5 %copy-start.4 = (s32[2,8]{1,0:T(2,128)S(1)}, s32[2,8]{1,0:T(2,128)}, u32[]{:S(2)}) copy-start(s32[2,8]{1,0:T(2,128)} %block_lists.1) | copy-start | bytes 196
  3.9 15.5 %copy-start.5 = (s32[2]{0:T(128)S(1)}, s32[2]{0:T(128)}, u32[]{:S(2)}) copy-start(s32[2]{0:T(128)} %tile_lengths.1) | copy-start | bytes 28
  5.0 8.9 %collective-permute-start.8 = (bf16[512,128]{1,0:T(8,128)(2,1)S(1)}, bf16[512,128]{1,0:T(8,128)(2,1)S(1)}, u32[]{:S(2)}, u32[]{:S(2)}) collective-permute-start(bf16[512,128]{1,0:T(8,128)(2,1)S(1)} %get-tuple-element.57), channel_id=1, source_target_pairs={{0,1},{1,0},{2,3},{3,2},{4,5},{5,4},{6,7},{7,6},{8,9},{9,8},{10,11... | collective-permute-start | bytes 393224 | tf_op jit(solution)/shard_map/ppermute | solution.py:368
  8.0 10.7 %collective-permute-start.9 = (bf16[512,128]{1,0:T(8,128)(2,1)S(1)}, bf16[512,128]{1,0:T(8,128)(2,1)S(1)}, u32[]{:S(2)}, u32[]{:S(2)}) collective-permute-start(bf16[512,128]{1,0:T(8,128)(2,1)S(1)} %get-tuple-element.58), channel_id=1, source_target_pairs={{0,2},{1,3},{2,0},{3,1},{4,6},{5,7},{6,4},{7,5},{8,10},{9,11},{10,... | collective-permute-start | bytes 393224 | tf_op jit(solution)/shard_map/ppermute | solution.py:368
  9.6 10.8 %collective-permute-start.10 = (bf16[512,128]{1,0:T(8,128)(2,1)S(1)}, bf16[512,128]{1,0:T(8,128)(2,1)S(1)}, u32[]{:S(2)}, u32[]{:S(2)}) collective-permute-start(bf16[512,128]{1,0:T(8,128)(2,1)S(1)} %get-tuple-element.59), channel_id=1, source_target_pairs={{0,3},{1,2},{2,1},{3,0},{4,7},{5,6},{6,5},{7,4},{8,11},{9,10},{10,... | collective-permute-start | bytes 393224 | tf_op jit(solution)/shard_map/ppermute | solution.py:368
  9.6 12.4 %collective-permute-start.11 = (bf16[512,128]{1,0:T(8,128)(2,1)S(1)}, bf16[512,128]{1,0:T(8,128)(2,1)S(1)}, u32[]{:S(2)}, u32[]{:S(2)}) collective-permute-start(bf16[512,128]{1,0:T(8,128)(2,1)S(1)} %get-tuple-element.60), channel_id=1, source_target_pairs={{0,4},{1,5},{2,6},{3,7},{4,0},{5,1},{6,2},{7,3},{8,12},{9,13},{10,... | collective-permute-start | bytes 393224 | tf_op jit(solution)/shard_map/ppermute | solution.py:368
  12.6 19.4 %collective-permute-start.12 = (bf16[512,128]{1,0:T(8,128)(2,1)S(1)}, bf16[512,128]{1,0:T(8,128)(2,1)S(1)}, u32[]{:S(2)}, u32[]{:S(2)}) collective-permute-start(bf16[512,128]{1,0:T(8,128)(2,1)S(1)} %get-tuple-element.61), channel_id=1, source_target_pairs={{0,5},{1,4},{2,7},{3,6},{4,1},{5,0},{6,3},{7,2},{8,13},{9,12},{10,... | collective-permute-start | bytes 393224 | tf_op jit(solution)/shard_map/ppermute | solution.py:368
  13.8 18.2 %collective-permute-start.13 = (bf16[512,128]{1,0:T(8,128)(2,1)S(1)}, bf16[512,128]{1,0:T(8,128)(2,1)S(1)}, u32[]{:S(2)}, u32[]{:S(2)}) collective-permute-start(bf16[512,128]{1,0:T(8,128)(2,1)S(1)} %get-tuple-element.62), channel_id=1, source_target_pairs={{0,6},{1,7},{2,4},{3,5},{4,2},{5,3},{6,0},{7,1},{8,14},{9,15},{10,... | collective-permute-start | bytes 393224 | tf_op jit(solution)/shard_map/ppermute | solution.py:368
  18.7 13.3 %collective-permute-start.14 = (bf16[512,128]{1,0:T(8,128)(2,1)S(1)}, bf16[512,128]{1,0:T(8,128)(2,1)S(1)}, u32[]{:S(2)}, u32[]{:S(2)}) collective-permute-start(bf16[512,128]{1,0:T(8,128)(2,1)S(1)} %get-tuple-element.63), channel_id=1, source_target_pairs={{0,7},{1,6},{2,5},{3,4},{4,3},{5,2},{6,1},{7,0},{8,15},{9,14},{10,... | collective-permute-start | bytes 393224 | tf_op jit(solution)/shard_map/ppermute | solution.py:368
  20.4 12.6 %collective-permute-start = (bf16[8,272,128]{2,1,0:T(8,128)(2,1)S(1)}, bf16[8,272,128]{2,1,0:T(8,128)(2,1)S(1)}, u32[]{:S(2)}, u32[]{:S(2)}) collective-permute-start(bf16[8,272,128]{2,1,0:T(8,128)(2,1)S(1)} %get-tuple-element.47), channel_id=1, source_target_pairs={{0,16},{16,0},{1,17},{17,1},{2,18},{18,2},{3,19},{19,3},{4,20},{20... | collective-permute-start | bytes 1671176 | tf_op jit(solution)/shard_map/ppermute | solution.py:368
  32.1 30.7 %collective-permute-start.15 = (bf16[4096,128]{1,0:T(8,128)(2,1)S(1)}, bf16[4096,128]{1,0:T(8,128)(2,1)S(1)}, u32[]{:S(2)}, u32[]{:S(2)}) collective-permute-start(bf16[4096,128]{1,0:T(8,128)(2,1)S(1)} %stack_chunks.1.refs_8_), channel_id=1, source_target_pairs={{0,8},{8,0},{1,9},{9,1},{2,10},{10,2},{3,11},{11,3},{4,12},{12,4},... | collective-permute-start | bytes 3145736 | tf_op jit(solution)/shard_map/ppermute | solution.py:368
  33.0 9.3 %collective-permute-start.1 = (bf16[2,272,128]{2,1,0:T(8,128)(2,1)S(1)}, bf16[2,272,128]{2,1,0:T(8,128)(2,1)S(1)}, u32[]{:S(2)}, u32[]{:S(2)}) collective-permute-start(bf16[2,272,128]{2,1,0:T(8,128)(2,1)S(1)} %get-tuple-element.49), channel_id=1, source_target_pairs={{0,1},{1,0},{2,3},{3,2},{4,5},{5,4},{6,7},{7,6},{8,9},{9,8},{10,11... | collective-permute-start | bytes 417800 | tf_op jit(solution)/shard_map/ppermute | solution.py:368
  34.9 10.1 %collective-permute-start.2 = (bf16[2,272,128]{2,1,0:T(8,128)(2,1)S(1)}, bf16[2,272,128]{2,1,0:T(8,128)(2,1)S(1)}, u32[]{:S(2)}, u32[]{:S(2)}) collective-permute-start(bf16[2,272,128]{2,1,0:T(8,128)(2,1)S(1)} %get-tuple-element.50), channel_id=1, source_target_pairs={{0,2},{1,3},{2,0},{3,1},{4,6},{5,7},{6,4},{7,5},{8,10},{9,11},{10,... | collective-permute-start | bytes 417800 | tf_op jit(solution)/shard_map/ppermute | solution.py:368
  37.7 13.0 %collective-permute-start.3 = (bf16[2,272,128]{2,1,0:T(8,128)(2,1)S(1)}, bf16[2,272,128]{2,1,0:T(8,128)(2,1)S(1)}, u32[]{:S(2)}, u32[]{:S(2)}) collective-permute-start(bf16[2,272,128]{2,1,0:T(8,128)(2,1)S(1)} %get-tuple-element.51), channel_id=1, source_target_pairs={{0,3},{1,2},{2,1},{3,0},{4,7},{5,6},{6,5},{7,4},{8,11},{9,10},{10,... | collective-permute-start | bytes 417800 | tf_op jit(solution)/shard_map/ppermute | solution.py:368
  38.8 13.1 %collective-permute-start.4 = (bf16[2,272,128]{2,1,0:T(8,128)(2,1)S(1)}, bf16[2,272,128]{2,1,0:T(8,128)(2,1)S(1)}, u32[]{:S(2)}, u32[]{:S(2)}) collective-permute-start(bf16[2,272,128]{2,1,0:T(8,128)(2,1)S(1)} %get-tuple-element.52), channel_id=1, source_target_pairs={{0,4},{1,5},{2,6},{3,7},{4,0},{5,1},{6,2},{7,3},{8,12},{9,13},{10,... | collective-permute-start | bytes 417800 | tf_op jit(solution)/shard_map/ppermute | solution.py:368
  42.4 20.3 %collective-permute-start.5 = (bf16[2,272,128]{2,1,0:T(8,128)(2,1)S(1)}, bf16[2,272,128]{2,1,0:T(8,128)(2,1)S(1)}, u32[]{:S(2)}, u32[]{:S(2)}) collective-permute-start(bf16[2,272,128]{2,1,0:T(8,128)(2,1)S(1)} %get-tuple-element.53), channel_id=1, source_target_pairs={{0,5},{1,4},{2,7},{3,6},{4,1},{5,0},{6,3},{7,2},{8,13},{9,12},{10,... | collective-permute-start | bytes 417800 | tf_op jit(solution)/shard_map/ppermute | solution.py:368
  44.9 17.8 %collective-permute-start.6 = (bf16[2,272,128]{2,1,0:T(8,128)(2,1)S(1)}, bf16[2,272,128]{2,1,0:T(8,128)(2,1)S(1)}, u32[]{:S(2)}, u32[]{:S(2)}) collective-permute-start(bf16[2,272,128]{2,1,0:T(8,128)(2,1)S(1)} %get-tuple-element.54), channel_id=1, source_target_pairs={{0,6},{1,7},{2,4},{3,5},{4,2},{5,3},{6,0},{7,1},{8,14},{9,15},{10,... | collective-permute-start | bytes 417800 | tf_op jit(solution)/shard_map/ppermute | solution.py:368
  50.8 12.0 %collective-permute-start.7 = (bf16[2,272,128]{2,1,0:T(8,128)(2,1)S(1)}, bf16[2,272,128]{2,1,0:T(8,128)(2,1)S(1)}, u32[]{:S(2)}, u32[]{:S(2)}) collective-permute-start(bf16[2,272,128]{2,1,0:T(8,128)(2,1)S(1)} %get-tuple-element.55), channel_id=1, source_target_pairs={{0,7},{1,6},{2,5},{3,4},{4,3},{5,2},{6,1},{7,0},{8,15},{9,14},{10,... | collective-permute-start | bytes 417800 | tf_op jit(solution)/shard_map/ppermute | solution.py:368
  81.6 31.0 %collective-permute-start.24 = (bf16[4096,128]{1,0:T(8,128)(2,1)S(1)}, bf16[4096,128]{1,0:T(8,128)(2,1)S(1)}, u32[]{:S(2)}, u32[]{:S(2)}) collective-permute-start(bf16[4096,128]{1,0:T(8,128)(2,1)S(1)} %get-tuple-element.77), channel_id=1, source_target_pairs={{0,8},{8,0},{1,9},{9,1},{2,10},{10,2},{3,11},{11,3},{4,12},{12,4},... | collective-permute-start | bytes 3145736 | tf_op jit(solution)/shard_map/ppermute | solution.py:368
  81.7 10.4 %collective-permute-start.16 = (bf16[2,256,128]{2,1,0:T(8,128)(2,1)S(1)}, bf16[2,256,128]{2,1,0:T(8,128)(2,1)S(1)}, u32[]{:S(2)}, u32[]{:S(2)}) collective-permute-start(bf16[2,256,128]{2,1,0:T(8,128)(2,1)S(1)} %get-tuple-element.65), channel_id=1, source_target_pairs={{0,1},{1,0},{2,3},{3,2},{4,5},{5,4},{6,7},{7,6},{8,9},{9,8},{10,11... | collective-permute-start | bytes 393224 | tf_op jit(solution)/shard_map/ppermute | solution.py:368
  82.8 15.1 %collective-permute-start.17 = (bf16[2,256,128]{2,1,0:T(8,128)(2,1)S(1)}, bf16[2,256,128]{2,1,0:T(8,128)(2,1)S(1)}, u32[]{:S(2)}, u32[]{:S(2)}) collective-permute-start(bf16[2,256,128]{2,1,0:T(8,128)(2,1)S(1)} %get-tuple-element.66), channel_id=1, source_target_pairs={{0,2},{1,3},{2,0},{3,1},{4,6},{5,7},{6,4},{7,5},{8,10},{9,11},{10,... | collective-permute-start | bytes 393224 | tf_op jit(solution)/shard_map/ppermute | solution.py:368
  89.2 11.2 %collective-permute-start.18 = (bf16[2,256,128]{2,1,0:T(8,128)(2,1)S(1)}, bf16[2,256,128]{2,1,0:T(8,128)(2,1)S(1)}, u32[]{:S(2)}, u32[]{:S(2)}) collective-permute-start(bf16[2,256,128]{2,1,0:T(8,128)(2,1)S(1)} %get-tuple-element.67), channel_id=1, source_target_pairs={{0,3},{1,2},{2,1},{3,0},{4,7},{5,6},{6,5},{7,4},{8,11},{9,10},{10,... | collective-permute-start | bytes 393224 | tf_op jit(solution)/shard_map/ppermute | solution.py:368
  89.3 14.0 %collective-permute-start.19 = (bf16[2,256,128]{2,1,0:T(8,128)(2,1)S(1)}, bf16[2,256,128]{2,1,0:T(8,128)(2,1)S(1)}, u32[]{:S(2)}, u32[]{:S(2)}) collective-permute-start(bf16[2,256,128]{2,1,0:T(8,128)(2,1)S(1)} %get-tuple-element.68), channel_id=1, source_target_pairs={{0,4},{1,5},{2,6},{3,7},{4,0},{5,1},{6,2},{7,3},{8,12},{9,13},{10,... | collective-permute-start | bytes 393224 | tf_op jit(solution)/shard_map/ppermute | solution.py:368
  92.2 18.9 %collective-permute-start.20 = (bf16[2,256,128]{2,1,0:T(8,128)(2,1)S(1)}, bf16[2,256,128]{2,1,0:T(8,128)(2,1)S(1)}, u32[]{:S(2)}, u32[]{:S(2)}) collective-permute-start(bf16[2,256,128]{2,1,0:T(8,128)(2,1)S(1)} %get-tuple-element.69), channel_id=1, source_target_pairs={{0,5},{1,4},{2,7},{3,6},{4,1},{5,0},{6,3},{7,2},{8,13},{9,12},{10,... | collective-permute-start | bytes 393224 | tf_op jit(solution)/shard_map/ppermute | solution.py:368
  97.8 13.2 %collective-permute-start.21 = (bf16[2,256,128]{2,1,0:T(8,128)(2,1)S(1)}, bf16[2,256,128]{2,1,0:T(8,128)(2,1)S(1)}, u32[]{:S(2)}, u32[]{:S(2)}) collective-permute-start(bf16[2,256,128]{2,1,0:T(8,128)(2,1)S(1)} %get-tuple-element.70), channel_id=1, source_target_pairs={{0,6},{1,7},{2,4},{3,5},{4,2},{5,3},{6,0},{7,1},{8,14},{9,15},{10,... | collective-permute-start | bytes 393224 | tf_op jit(solution)/shard_map/ppermute | solution.py:368
  100.4 10.6 %collective-permute-start.22 = (bf16[2,256,128]{2,1,0:T(8,128)(2,1)S(1)}, bf16[2,256,128]{2,1,0:T(8,128)(2,1)S(1)}, u32[]{:S(2)}, u32[]{:S(2)}) collective-permute-start(bf16[2,256,128]{2,1,0:T(8,128)(2,1)S(1)} %get-tuple-element.71), channel_id=1, source_target_pairs={{0,7},{1,6},{2,5},{3,4},{4,3},{5,2},{6,1},{7,0},{8,15},{9,14},{10,... | collective-permute-start | bytes 393224 | tf_op jit(solution)/shard_map/ppermute | solution.py:368
  111.1 12.0 %collective-permute-start.23 = (bf16[8,256,128]{2,1,0:T(8,128)(2,1)S(1)}, bf16[8,256,128]{2,1,0:T(8,128)(2,1)S(1)}, u32[]{:S(2)}, u32[]{:S(2)}) collective-permute-start(bf16[8,256,128]{2,1,0:T(8,128)(2,1)S(1)} %get-tuple-element.73), channel_id=1, source_target_pairs={{0,16},{16,0},{1,17},{17,1},{2,18},{18,2},{3,19},{19,3},{4,20},{20... | collective-permute-start | bytes 1572872 | tf_op jit(solution)/shard_map/ppermute | solution.py:368
  113.5 17.9 %collective-permute-start.25 = (bf16[512,128]{1,0:T(8,128)(2,1)S(1)}, bf16[512,128]{1,0:T(8,128)(2,1)S(1)}, u32[]{:S(2)}, u32[]{:S(2)}) collective-permute-start(bf16[512,128]{1,0:T(8,128)(2,1)S(1)} %get-tuple-element.78), channel_id=1, source_target_pairs={{0,0},{1,1},{2,2},{3,3},{4,12},{5,13},{6,14},{7,15},{8,4},{9,5},{1... | collective-permute-start | bytes 393224 | tf_op jit(solution)/shard_map/ppermute | solution.py:402
  114.2 18.0 %collective-permute-start.26 = (bf16[512,128]{1,0:T(8,128)(2,1)S(1)}, bf16[512,128]{1,0:T(8,128)(2,1)S(1)}, u32[]{:S(2)}, u32[]{:S(2)}) collective-permute-start(bf16[512,128]{1,0:T(8,128)(2,1)S(1)} %get-tuple-element.79), channel_id=1, source_target_pairs={{0,1},{1,0},{2,3},{3,2},{4,13},{5,12},{6,15},{7,14},{8,5},{9,4},{1... | collective-permute-start | bytes 393224 | tf_op jit(solution)/shard_map/ppermute | solution.py:402
  115.7 17.7 %collective-permute-start.27 = (bf16[512,128]{1,0:T(8,128)(2,1)S(1)}, bf16[512,128]{1,0:T(8,128)(2,1)S(1)}, u32[]{:S(2)}, u32[]{:S(2)}) collective-permute-start(bf16[512,128]{1,0:T(8,128)(2,1)S(1)} %get-tuple-element.80), channel_id=1, source_target_pairs={{0,2},{1,3},{2,0},{3,1},{4,14},{5,15},{6,12},{7,13},{8,6},{9,7},{1... | collective-permute-start | bytes 393224 | tf_op jit(solution)/shard_map/ppermute | solution.py:402
  120.4 17.8 %collective-permute-start.28 = (bf16[512,128]{1,0:T(8,128)(2,1)S(1)}, bf16[512,128]{1,0:T(8,128)(2,1)S(1)}, u32[]{:S(2)}, u32[]{:S(2)}) collective-permute-start(bf16[512,128]{1,0:T(8,128)(2,1)S(1)} %get-tuple-element.81), channel_id=1, source_target_pairs={{0,3},{1,2},{2,1},{3,0},{4,15},{5,14},{6,13},{7,12},{8,7},{9,6},{1... | collective-permute-start | bytes 393224 | tf_op jit(solution)/shard_map/ppermute | solution.py:402
  123.2 15.0 %collective-permute-start.29 = (bf16[512,128]{1,0:T(8,128)(2,1)S(1)}, bf16[512,128]{1,0:T(8,128)(2,1)S(1)}, u32[]{:S(2)}, u32[]{:S(2)}) collective-permute-start(bf16[512,128]{1,0:T(8,128)(2,1)S(1)} %get-tuple-element.82), channel_id=1, source_target_pairs={{0,4},{1,5},{2,6},{3,7},{4,8},{5,9},{6,10},{7,11},{8,0},{9,1},{10,... | collective-permute-start | bytes 393224 | tf_op jit(solution)/shard_map/ppermute | solution.py:402
  131.4 6.8 %collective-permute-start.30 = (bf16[512,128]{1,0:T(8,128)(2,1)S(1)}, bf16[512,128]{1,0:T(8,128)(2,1)S(1)}, u32[]{:S(2)}, u32[]{:S(2)}) collective-permute-start(bf16[512,128]{1,0:T(8,128)(2,1)S(1)} %get-tuple-element.83), channel_id=1, source_target_pairs={{0,5},{1,4},{2,7},{3,6},{4,9},{5,8},{6,11},{7,10},{8,1},{9,0},{10,... | collective-permute-start | bytes 393224 | tf_op jit(solution)/shard_map/ppermute | solution.py:402
  132.2 7.3 %collective-permute-start.31 = (bf16[512,128]{1,0:T(8,128)(2,1)S(1)}, bf16[512,128]{1,0:T(8,128)(2,1)S(1)}, u32[]{:S(2)}, u32[]{:S(2)}) collective-permute-start(bf16[512,128]{1,0:T(8,128)(2,1)S(1)} %get-tuple-element.84), channel_id=1, source_target_pairs={{0,6},{1,7},{2,4},{3,5},{4,10},{5,11},{6,8},{7,9},{8,2},{9,3},{10,... | collective-permute-start | bytes 393224 | tf_op jit(solution)/shard_map/ppermute | solution.py:402
  133.4 9.5 %collective-permute-start.32 = (bf16[512,128]{1,0:T(8,128)(2,1)S(1)}, bf16[512,128]{1,0:T(8,128)(2,1)S(1)}, u32[]{:S(2)}, u32[]{:S(2)}) collective-permute-start(bf16[512,128]{1,0:T(8,128)(2,1)S(1)} %get-tuple-element.85), channel_id=1, source_target_pairs={{0,7},{1,6},{2,5},{3,4},{4,11},{5,10},{6,9},{7,8},{8,3},{9,2},{10,... | collective-permute-start | bytes 393224 | tf_op jit(solution)/shard_map/ppermute | solution.py:402

commit v3 on v2

--- a/solution.py
+++ b/solution.py
@@ -17,10 +17,12 @@
 NEG_FILL = -1e30
 PEAK = 1.15e9
 MIB = 1024 * 1024
-ATTEND_COST = 20
-SPLIT_COST = 2
+BATCHES = ((0, 4, 0), (4, 8, 0))
+SPLIT_COST = 0
+UNPACK_FACT = 2
+PLANES = 4
 STACK_COST = 2
-UNPACK_COST = 3
+UNPACK_COST = 5
 
 SMEM = pl.BlockSpec(memory_space=pltpu.SMEM)
 VMEM = pl.BlockSpec(memory_space=pltpu.VMEM)
@@ -101,7 +103,7 @@
             out_specs=[pl.BlockSpec((rows, LANES), lambda _, p: (0, 0))] * dims,
         ),
         out_shape=[bf16(rows, LANES)] * dims,
-        compiler_params=pltpu.CompilerParams(vmem_limit_bytes=24 * MIB),
+        compiler_params=pltpu.CompilerParams(vmem_limit_bytes=60 * MIB),
         name="pack_dimension",
     )(place, *([key_rows] * pairs), *([value_rows] * pairs))
 
@@ -111,16 +113,13 @@
     tiles, slots = block_lists.shape
     parts = HEADS // dims
 
-    def kernel(place, queries, cotangent, block_lists, tile_lengths, *outs):
+    def kernel(place, queries, cotangent, block_lists, tile_lengths, *refs):
+        *outs, words = refs
         odd = (place[2] & 1) == 1
-        row = lax.broadcasted_iota(jnp.int32, (META_ROWS, LANES), 0)
-        lane = lax.broadcasted_iota(jnp.int32, (META_ROWS, LANES), 1)
-        words = jnp.zeros((META_ROWS, LANES), jnp.int32)
-        for t in range(tiles):
-            for j in range(slots):
-                words = jnp.where((row == t) & (lane == j), block_lists[t, j], words)
-            words = jnp.where((row == t) & (lane == slots), tile_lengths[t], words)
-        meta = words.astype(jnp.float32).astype(jnp.bfloat16)
+        words[...] = jnp.zeros_like(words)
+        words[:tiles, :slots] = block_lists[...]
+        words[:tiles, slots : slots + 1] = tile_lengths[...]
+        meta = words[...].astype(jnp.float32).astype(jnp.bfloat16)
         for k in range(parts):
             base = (place[0] ^ k) * (dims // 2)
             for i in range(dims // 2):
@@ -134,9 +133,10 @@
         kernel,
         "pack_fact",
         [bf16(dims, rows + META_ROWS, LANES)] * parts,
-        [SMEM, VMEM, VMEM, SMEM, SMEM],
-        cost=4,
-    )(place, queries, cotangent, block_lists, tile_lengths)
+        [SMEM, VMEM, VMEM, VMEM, VMEM],
+        cost=1,
+        scratch_shapes=[pltpu.VMEM((META_ROWS, LANES), jnp.int32)],
+    )(place, queries, cotangent, block_lists, tile_lengths[:, None])
 
 
 def merge_fact(parts):
@@ -156,40 +156,57 @@
     rows = chunks[0].shape[0]
 
     def kernel(*refs):
-        for r in range(len(chunks)):
-            refs[-1][r * rows : (r + 1) * rows, :] = refs[r][...]
+        for r, chunk in enumerate(refs[:-1]):
+            refs[-1][r * rows : (r + 1) * rows, :] = chunk[...]
 
     return call(
         kernel, "stack_chunks", bf16(len(chunks) * rows, LANES), [VMEM] * len(chunks), cost=cost
     )(*chunks)
 
 
-def attend(place, facts, tables, rows, slots):
-    dims, shares = len(facts), len(tables)
+def attend(place, facts, tables, total, rows, slots, dims, shares, ys, last, cost):
+    count = len(facts)
     parts = facts[0].shape[0]
-    sources = dims * parts
-    table_rows = tables[0].shape[0]
+    sources = count * parts
+    table_rows = sum(t.shape[0] for t in tables) // shares
     owner_blocks = table_rows // TILE // dims
     tiles_each = rows // TILE
+    begin = total is None
 
     def kernel(place, *refs):
-        facts_in, tables_in = refs[:dims], refs[dims : dims + shares]
-        fact_outs = refs[dims + shares : 2 * dims + shares]
-        own_out = refs[2 * dims + shares]
-        share_outs = refs[2 * dims + shares + 1 : 2 * dims + 2 * shares]
-        fact, fact_out, table, total, words, meta, sem = refs[2 * dims + 2 * shares :]
+        refs = list(refs)
+
+        def take(n):
+            taken = refs[:n]
+            del refs[:n]
+            return taken
+
+        facts_in = take(count)
+        tables_in = take(len(tables))
+        (total_in,) = take(1) if not begin else (None,)
+        fact_outs = take(count // ys)
+        if last:
+            (own_out,), share_outs = take(1), take(shares - 1)
+        else:
+            (sums_out,) = take(1)
+        (table,) = take(1) if begin else tables_in
+        (sums,) = take(1) if last else (sums_out,)
+        fact, fact_out, words, meta, sem = refs
         odd = place[2] & 1
-        for r in range(dims):
+        for r in range(count):
             words[r * parts : (r + 1) * parts] = (
                 facts_in[r][:, rows:, :].astype(jnp.float32).astype(jnp.int32)
             )
         copy = pltpu.make_async_copy(words, meta, sem)
         copy.start()
-        for r in range(dims):
+        for r in range(count):
             fact[r * parts : (r + 1) * parts] = facts_in[r][:, :rows, :]
-        for k in range(shares):
-            table[k * table_rows : (k + 1) * table_rows, :] = tables_in[k][...]
-        total[...] = jnp.zeros_like(total)
+        if begin:
+            for k in range(shares):
+                table[k * table_rows : (k + 1) * table_rows, :] = tables_in[k][...]
+            sums[...] = jnp.zeros_like(sums)
+        else:
+            sums[...] = total_in[...]
         copy.wait()
         first = lane_is((TILE, LANES), odd)
 
@@ -244,7 +261,7 @@
                 ).astype(jnp.bfloat16)
                 grads = jnp.dot(pairs[tile], left[tile], preferred_element_type=jnp.float32)
                 for j, at in enumerate(places[tile]):
-                    total[pl.ds(at, TILE), :] += grads[j * TILE : (j + 1) * TILE]
+                    sums[pl.ds(at, TILE), :] += grads[j * TILE : (j + 1) * TILE]
 
         def source_step(source, carry):
             lengths = [meta[source, tile, slots] for tile in range(tiles_each)]
@@ -254,71 +271,82 @@
             return carry
 
         lax.fori_loop(0, sources, source_step, 0)
-        for r in range(dims):
-            fact_outs[r][...] = fact_out[r * parts : (r + 1) * parts]
-        factor = jnp.where(lane_is((table_rows, LANES), odd), SCALE, 1.0)
-        own_out[...] = total[:table_rows] * factor
-        for k in range(1, shares):
-            share_outs[k - 1][...] = (
-                total[k * table_rows : (k + 1) * table_rows] * factor
-            ).astype(jnp.bfloat16)
-
+        for r in range(count):
+            for i in range(parts):
+                fact_outs[r // ys][i * ys + r % ys] = fact_out[r * parts + i]
+        if last:
+            factor = jnp.where(lane_is((table_rows, LANES), odd), SCALE, 1.0)
+            own_out[...] = sums[:table_rows] * factor
+            for k in range(1, shares):
+                share_outs[k - 1][...] = (
+                    sums[k * table_rows : (k + 1) * table_rows] * factor
+                ).astype(jnp.bfloat16)
+
+    outs = [bf16(parts * ys, rows, LANES)] * (count // ys)
+    wide = jax.ShapeDtypeStruct((shares * table_rows, LANES), jnp.float32)
+    scratch = []
+    if last:
+        outs += [jax.ShapeDtypeStruct((table_rows, LANES), jnp.float32)]
+        outs += [bf16(table_rows, LANES)] * (shares - 1)
+    else:
+        outs += [wide]
+    if begin:
+        if last:
+            scratch += [pltpu.VMEM((shares * table_rows, LANES), jnp.bfloat16)]
+        else:
+            outs += [bf16(shares * table_rows, LANES)]
+    if last:
+        scratch += [pltpu.VMEM(wide.shape, wide.dtype)]
+    sums_in = [] if begin else [total]
     results = call(
         kernel,
         "attend",
-        [bf16(parts, rows, LANES)] * dims
-        + [jax.ShapeDtypeStruct((table_rows, LANES), jnp.float32)]
-        + [bf16(table_rows, LANES)] * (shares - 1),
-        [SMEM] + [VMEM] * (dims + shares),
-        cost=ATTEND_COST,
-        vmem=40,
-        scratch_shapes=[
+        outs,
+        [SMEM] + [VMEM] * (count + len(tables) + len(sums_in)),
+        cost=cost,
+        vmem=32,
+        scratch_shapes=scratch
+        + [
             pltpu.VMEM((sources, rows, LANES), jnp.bfloat16),
             pltpu.VMEM((sources, rows, LANES), jnp.bfloat16),
-            pltpu.VMEM((shares * table_rows, LANES), jnp.bfloat16),
-            pltpu.VMEM((shares * table_rows, LANES), jnp.float32),
             pltpu.VMEM((sources, META_ROWS, LANES), jnp.int32),
             pltpu.SMEM((sources, META_ROWS, LANES), jnp.int32),
             pltpu.SemaphoreType.DMA,
         ],
-    )(place, *facts, *tables)
-    return results[:dims], results[dims], results[dims + 1 :]
-
-
-def split_fact(chunks):
-    parts, rows, _ = chunks[0].shape
-    dims = len(chunks)
-
-    def kernel(*refs):
-        for k in range(parts):
-            for r in range(dims):
-                refs[dims + k][r] = refs[r][k]
-
-    return call(
-        kernel, "split_fact", [bf16(dims, rows, LANES)] * parts, [VMEM] * dims, cost=SPLIT_COST
-    )(*chunks)
-
-
-def unpack_fact(place, parts):
-    dims, rows, _ = parts[0].shape
+    )(place, *facts, *tables, *sums_in)
+    return results[: count // ys], results[count // ys :]
+
+
+def join_planes(place, chunks, xs, cost):
+    zs, (count, rows, _) = len(chunks), chunks[0].shape
+    ys = count // xs
 
     def kernel(place, *refs):
-        attended, query_grad = refs[len(parts) :]
-        odd = (place[2] & 1) == 1
-        for k in range(len(parts)):
-            base = (place[0] ^ k) * (dims // 2)
-            for i in range(dims // 2):
-                span = pair_lanes(base, place, i)
-                pair = in_order(odd, (refs[k][2 * i], refs[k][2 * i + 1]))
-                query_grad[:, span], attended[:, span] = separate(*pair)
-
-    return call(
-        kernel,
-        "unpack_fact",
-        [bf16(rows, HEADS * HEAD_DIM)] * 2,
-        [SMEM] + [VMEM] * len(parts),
-        cost=2.4,
-    )(place, *parts)
+        for k in range(zs):
+            for n in range(count):
+                i, j = divmod(n, ys)
+                m = (place[0] ^ i) * ys + (place[4] ^ j)
+                refs[zs][m, place[3] ^ k] = refs[zs - 1 - k][n]
+
+    return call(
+        kernel, "join_planes", bf16(count, zs, rows, LANES), [SMEM] + [VMEM] * zs, cost=cost
+    )(place, *chunks[::-1])
+
+
+def unpack_fact(parts, xs):
+    planes, zs, rows, _ = parts.shape
+    ys = planes // xs
+
+    def kernel(parts, attended, query_grad):
+        for p in range(HEADS // 2):
+            span = slice(p * LANES, (p + 1) * LANES)
+            x, dim = divmod(2 * p, zs * ys)
+            m, z = x * ys + dim % ys, dim // ys
+            query_grad[:, span], attended[:, span] = separate(parts[m, z], parts[m + 1, z])
+
+    return call(
+        kernel, "unpack_fact", [bf16(rows, HEADS * HEAD_DIM)] * 2, [VMEM], cost=UNPACK_FACT
+    )(parts)
 
 
 def sum_shares(place, own, others, dims, per_fact):
@@ -344,6 +372,7 @@
 
     def kernel(place, *refs):
         key_grad, value_grad = refs[dims:]
+        refs = refs[dims - 1 :: -1]
         odd = (place[2] & 1) == 1
         for i in range(dims // 2):
             source = place[2] ^ (2 * i)
@@ -359,7 +388,7 @@
         [bf16(shares * rows, per_fact * HEAD_DIM)] * 2,
         [SMEM] + [VMEM] * dims,
         cost=UNPACK_COST,
-    )(place, *chunks)
+    )(place, *reversed(chunks))
 
 
 def by_xor(part, axis, index, count):
@@ -368,38 +397,72 @@
     return lax.ppermute(part, axis, [(i, i ^ index) for i in range(count)])
 
 
-def body(xs, shares, dims, queries, key_rows, value_rows, cotangent, block_lists, tile_lengths):
+def exchange(chunks, send):
+    moved = list(chunks)
+    for r in range(len(chunks)):
+        moved[r] = send(chunks[r], r)
+    return moved
+
+
+def body(xs, shares, zs, ys, queries, key_rows, value_rows, cotangent, block_lists, tile_lengths):
+    dims = zs * ys
     per_fact = dims // shares
     rows, slots = queries.shape[0], block_lists.shape[1]
-    place = jnp.stack([lax.axis_index(a) for a in ("x", "share", "dim")]).astype(jnp.int32)
-
-    chunks = pack_dimension(place, key_rows, value_rows, dims, shares)
-    chunks = [by_xor(chunk, "dim", r, dims) for r, chunk in enumerate(chunks)]
-    table = stack_chunks(chunks, STACK_COST)
-    tables = [by_xor(table, "share", k, shares) for k in range(shares)]
-
-    parts = pack_fact(place, queries, cotangent, block_lists, tile_lengths, dims)
-    parts = [by_xor(part, "x", k, xs) for k, part in enumerate(parts)]
-    facts = merge_fact(parts)
-    facts = [by_xor(chunk, "dim", r, dims) for r, chunk in enumerate(facts)]
-
-    fact_outs, own, others = attend(place, facts, tables, rows, slots)
-
-    fact_outs = [by_xor(chunk, "dim", r, dims) for r, chunk in enumerate(fact_outs)]
-    parts = split_fact(fact_outs)
-    parts = [by_xor(part, "x", k, xs) for k, part in enumerate(parts)]
-    attended, query_grad = unpack_fact(place, parts)
-
-    others = [by_xor(other, "share", k + 1, shares) for k, other in enumerate(others)]
-    chunks = sum_shares(place, own, others, dims, per_fact)
-    grads = []
-    for r, chunk in enumerate(chunks):
+    x, share, z, y = (lax.axis_index(a) for a in ("x", "share", "z", "y"))
+    place = jnp.stack([x, share, z * ys + y, z, y]).astype(jnp.int32)
+
+    def over_dim(chunk, r):
+        return by_xor(chunk, ("z", "y"), r, dims)
+
+    def to_columns(chunk, r):
         pairs = [
             (c * dims + d, (d // per_fact) * dims + (d ^ r ^ (c * per_fact)))
             for c in range(shares)
             for d in range(dims)
         ]
-        grads.append(lax.ppermute(chunk, ("share", "dim"), pairs))
+        return lax.ppermute(chunk, ("share", "z", "y"), pairs)
+
+    chunks = pack_dimension(place, key_rows, value_rows, dims, shares)
+    chunks = exchange(chunks, over_dim)
+    table = stack_chunks(chunks, STACK_COST)
+    tables = [by_xor(table, "share", k, shares) for k in range(shares)]
+
+    parts = pack_fact(place, queries, cotangent, block_lists, tile_lengths, dims)
+    parts = [by_xor(part, "x", k, xs) for k, part in enumerate(parts)]
+    facts = merge_fact(parts)
+    facts = exchange(facts, over_dim)
+
+    fact_outs, total = [], None
+    for start, stop, cost in BATCHES:
+        stop = min(stop * dims // 8, dims)
+        outs, rest = attend(
+            place,
+            facts[start * dims // 8 : stop],
+            tables,
+            total,
+            rows,
+            slots,
+            dims,
+            shares,
+            ys,
+            stop == dims,
+            cost,
+        )
+        fact_outs += outs
+        if stop < dims:
+            total = rest[0]
+            tables = rest[1:] or tables
+    own, others = rest[0], rest[1:]
+
+    fact_outs = [by_xor(chunk, "z", k, zs) for k, chunk in enumerate(fact_outs)]
+    others = [by_xor(other, "share", k + 1, shares) for k, other in enumerate(others)]
+    chunks = sum_shares(place, own, others, dims, per_fact)
+    fact_outs[0], *chunks = lax.optimization_barrier((fact_outs[0], *chunks))
+    fact_out = join_planes(place, fact_outs, xs, SPLIT_COST)
+    fact_out = lax.all_to_all(fact_out, ("x", "y"), split_axis=0, concat_axis=0, tiled=True)
+    attended, query_grad = unpack_fact(fact_out, xs)
+
+    grads = exchange(chunks, to_columns)
     key_grad, value_grad = unpack_dimension(place, grads, shares, per_fact)
     return attended, query_grad, key_grad, value_grad
 
@@ -408,12 +471,14 @@
     facts, dims = mesh.shape["fact"], mesh.shape["dim"]
     xs = HEADS // dims
     shares = facts // xs
-    fine = Mesh(mesh.devices.reshape(xs, shares, dims), ("x", "share", "dim"))
-    every = ("x", "share", "dim")
+    ys = dims // PLANES
+    every = ("x", "share", "z", "y")
+    fine = Mesh(mesh.devices.reshape(xs, shares, PLANES, ys), every)
+    owner, columns = ("z", "y"), ("x", "share")
     in_specs = (
         P(every, None),
-        P("dim", None),
-        P("dim", None),
+        P(owner, None),
+        P(owner, None),
         P(every, None),
         P(every, None),
         P(every),
@@ -421,11 +486,11 @@
     out_specs = (
         P(every, None),
         P(every, None),
-        P("dim", ("x", "share")),
-        P("dim", ("x", "share")),
+        P(owner, columns),
+        P(owner, columns),
     )
     return jax.shard_map(
-        functools.partial(body, xs, shares, dims),
+        functools.partial(body, xs, shares, PLANES, ys),
         mesh=fine,
         in_specs=in_specs,
         out_specs=out_specs,

time: 145 us -> 132 us (0.910)
  starting transfers between devices: 71.6 us -> 62.7 us
  waiting for transfers between devices: 43.6 us -> 38.7 us
  Pallas kernels: 25.4 us -> 28.9 us
  local copies, waits for them, and re-layouts: 3.2 us -> 0.71 us
    ppermute x25 -> x20, starting transfers between devices: 51 us -> 37 us  [by_xor(): return lax.ppermute(part, axis, [(i, i ^ index) for i in range(count)])]
    ppermute x25 -> x20, waiting for transfers between devices: 38.8 us -> 25.6 us  [by_xor(): return lax.ppermute(part, axis, [(i, i ^ index) for i in range(count)])]
    ppermute x8, waiting for transfers between devices: 4.73 us -> 13.1 us  [to_columns(): return lax.ppermute(chunk, ('share', 'z', 'y'), pairs)]
    all_to_all x0 -> x1, starting transfers between devices: none -> 3.51 us  [body(): lax.all_to_all(fact_out, ('x', 'y'), split_axis=0, concat_axis=0, tiled=T...]
    unnamed x12, local copies, waits for them, and re-layouts: 3.2 us -> 0.03 us
    pallas_call x1, Pallas kernels: 1.05 us -> 3.22 us  [pack_dimension(): pl.pallas_call(kernel, grid_spec=pltpu.PrefetchScalarGridSpec(num_scalar_...]
    ppermute x8, starting transfers between devices: 20.6 us -> 22.2 us  [to_columns(): return lax.ppermute(chunk, ('share', 'z', 'y'), pairs)]
    pallas_call x3 -> x4, Pallas kernels: 20.7 us -> 22 us  [the longest x2 19.3 us: attend(): call(kernel, 'attend', outs, [SMEM] + [VMEM] * (count + len(tables) + len...]
  transfers between devices with their start and end apart: 33 -> 29, of which waited for: 10 -> 9; matrix products, arithmetic and copies ran while one was open for 0% -> 0% of each run, Pallas kernels for 3% -> 11%
where the time goes in v3:
time: 132 us
  starting transfers between devices  62.7 us (48%)
  waiting for transfers between devices  38.7 us (29%)
  Pallas kernels  28.9 us (22%)
    ppermute x20, starting transfers between devices, by_xor(): return lax.ppermute(part, axis, [(i, i ^ index) for i in range(count)])  37 us
    ppermute x20, waiting for transfers between devices, by_xor(): return lax.ppermute(part, axis, [(i, i ^ index) for i in range(count)])  25.6 us
    ppermute x8, starting transfers between devices, to_columns(): return lax.ppermute(chunk, ('share', 'z', 'y'), pairs)  22.2 us
    pallas_call x2, Pallas kernels, attend(): call(kernel, 'attend', outs, [SMEM] + [VMEM] * (count + len(tables) + len...  19.3 us
    ppermute x8, waiting for transfers between devices, to_columns(): return lax.ppermute(chunk, ('share', 'z', 'y'), pairs)  13.1 us
    all_to_all x1, starting transfers between devices, body(): lax.all_to_all(fact_out, ('x', 'y'), split_axis=0, concat_axis=0, tiled=T...  3.51 us
    pallas_call x1, Pallas kernels, pack_dimension(): pl.pallas_call(kernel, grid_spec=pltpu.PrefetchScalarGridSpec(num_scalar_...  3.22 us
  transfers between devices with their start and end apart: 29, of which 9 were waited for; matrix products, arithmetic and copies ran while one was open for 0% of the time, Pallas kernels for 11%

profile of v3, /device:TPU:0, one launch (start us, length us, event | category | flops | bytes accessed | tf_op | source)
XLA Modules:
  0.0 131.8 jit_solution(14289450898219793508)
XLA Ops:
  0.6 0.6 stack.23.place
  1.3 3.2 %pack_dimension.1 = (bf16[512,128]{1,0:T(8,128)(2,1)}, bf16[512,128]{1,0:T(8,128)(2,1)}, bf16[512,128]{1,0:T(8,128)(2,1)}, bf16[512,128]{1,0:T(8,128)(2,1)}, bf1...) custom-call(s32[5]{0:T(128)} %stack.23.place, ...), custom_call_target="tpu_custom_call" | custom-call | tf_op jit(solution)/shard_map/pack_dimension/pallas_call | solution.py:97
  4.5 3.0 %collective-permute-start.8 = (bf16[512,128]{1,0:T(8,128)(2,1)}, bf16[512,128]{1,0:T(8,128)(2,1)S(1)}, u32[]{:S(2)}, u32[]{:S(2)}) collective-permute-start(bf16[512,128]{1,0:T(8,128)(2,1)} %get-tuple-element.62), channel_id=1, source_target_pairs={{0,1},{1,0},{2,3},{3,2},{4,5},{5,4},{6,7},{7,6},{8,9},{9,8},{10,11... | collective-permute-start | bytes 393224 | tf_op jit(solution)/shard_map/ppermute | solution.py:397
  7.4 1.6 %collective-permute-start.9 = (bf16[512,128]{1,0:T(8,128)(2,1)}, bf16[512,128]{1,0:T(8,128)(2,1)S(1)}, u32[]{:S(2)}, u32[]{:S(2)}) collective-permute-start(bf16[512,128]{1,0:T(8,128)(2,1)} %get-tuple-element.63), channel_id=1, source_target_pairs={{0,2},{1,3},{2,0},{3,1},{4,6},{5,7},{6,4},{7,5},{8,10},{9,11},{10,... | collective-permute-start | bytes 393224 | tf_op jit(solution)/shard_map/ppermute | solution.py:397
  9.0 3.0 %collective-permute-start.11 = (bf16[512,128]{1,0:T(8,128)(2,1)}, bf16[512,128]{1,0:T(8,128)(2,1)S(1)}, u32[]{:S(2)}, u32[]{:S(2)}) collective-permute-start(bf16[512,128]{1,0:T(8,128)(2,1)} %get-tuple-element.65), channel_id=1, source_target_pairs={{0,4},{1,5},{2,6},{3,7},{4,0},{5,1},{6,2},{7,3},{8,12},{9,13},{10,... | collective-permute-start | bytes 393224 | tf_op jit(solution)/shard_map/ppermute | solution.py:397
  12.0 1.3 collective-permute-start.12
  13.3 3.6 %collective-permute-start.13 = (bf16[512,128]{1,0:T(8,128)(2,1)}, bf16[512,128]{1,0:T(8,128)(2,1)S(1)}, u32[]{:S(2)}, u32[]{:S(2)}) collective-permute-start(bf16[512,128]{1,0:T(8,128)(2,1)} %get-tuple-element.67), channel_id=1, source_target_pairs={{0,6},{1,7},{2,4},{3,5},{4,2},{5,3},{6,0},{7,1},{8,14},{9,15},{10,... | collective-permute-start | bytes 393224 | tf_op jit(solution)/shard_map/ppermute | solution.py:397
  16.9 1.5 %collective-permute-done.9.refs_2_ = bf16[512,128]{1,0:T(8,128)(2,1)S(1)} collective-permute-done((bf16[512,128]{1,0:T(8,128)(2,1)}, bf16[512,128]{1,0:T(8,128)(2,1)S(1)}, u32[]{:S(2)}, u32[]{:S(2)}) %collective-permute-start.9) | collective-permute-done | bytes 131104 | tf_op jit(solution)/shard_map/ppermute | solution.py:397
  18.4 0.7 collective-permute-start.14
  19.0 0.1 copy.10.tile_lengths
  19.2 1.0 pack_fact.1
  20.2 1.6 %collective-permute-start = (bf16[8,272,128]{2,1,0:T(8,128)(2,1)S(1)}, bf16[8,272,128]{2,1,0:T(8,128)(2,1)S(1)}, u32[]{:S(2)}, u32[]{:S(2)}) collective-permute-start(bf16[8,272,128]{2,1,0:T(8,128)(2,1)S(1)} %get-tuple-element.52), channel_id=1, source_target_pairs={{0,16},{16,0},{1,17},{17,1},{2,18},{18,2},{3,19},{19,3},{4,20},{20... | collective-permute-start | bytes 1671176 | tf_op jit(solution)/shard_map/ppermute | solution.py:397
  21.7 9.9 %collective-permute-done.12.refs_5_ = bf16[512,128]{1,0:T(8,128)(2,1)S(1)} collective-permute-done((bf16[512,128]{1,0:T(8,128)(2,1)}, bf16[512,128]{1,0:T(8,128)(2,1)S(1)}, u32[]{:S(2)}, u32[]{:S(2)}) %collective-permute-start.12) | collective-permute-done | bytes 131104 | tf_op jit(solution)/shard_map/ppermute | solution.py:397
  31.7 0.1 stack_chunks.1.refs_4_
  31.8 0.1 collective-permute-start.15
  31.8 0.8 collective-permute-done.refs_1_
  32.6 0.1 merge_fact.1
  32.7 1.8 %collective-permute-start.5 = (bf16[2,272,128]{2,1,0:T(8,128)(2,1)S(1)}, bf16[2,272,128]{2,1,0:T(8,128)(2,1)S(1)}, u32[]{:S(2)}, u32[]{:S(2)}) collective-permute-start(bf16[2,272,128]{2,1,0:T(8,128)(2,1)S(1)} %get-tuple-element.58), channel_id=1, source_target_pairs={{0,1},{1,0},{2,3},{3,2},{4,5},{5,4},{6,7},{7,6},{8,9},{9,8},{10,11... | collective-permute-start | bytes 417800 | tf_op jit(solution)/shard_map/ppermute | solution.py:397
  34.5 2.8 %collective-permute-start.6 = (bf16[2,272,128]{2,1,0:T(8,128)(2,1)S(1)}, bf16[2,272,128]{2,1,0:T(8,128)(2,1)S(1)}, u32[]{:S(2)}, u32[]{:S(2)}) collective-permute-start(bf16[2,272,128]{2,1,0:T(8,128)(2,1)S(1)} %get-tuple-element.59), channel_id=1, source_target_pairs={{0,2},{1,3},{2,0},{3,1},{4,6},{5,7},{6,4},{7,5},{8,10},{9,11},{10,... | collective-permute-start | bytes 417800 | tf_op jit(solution)/shard_map/ppermute | solution.py:397
  37.4 1.1 collective-permute-start.7
  38.5 3.5 %collective-permute-start.1 = (bf16[2,272,128]{2,1,0:T(8,128)(2,1)S(1)}, bf16[2,272,128]{2,1,0:T(8,128)(2,1)S(1)}, u32[]{:S(2)}, u32[]{:S(2)}) collective-permute-start(bf16[2,272,128]{2,1,0:T(8,128)(2,1)S(1)} %get-tuple-element.53), channel_id=1, source_target_pairs={{0,4},{1,5},{2,6},{3,7},{4,0},{5,1},{6,2},{7,3},{8,12},{9,13},{10,... | collective-permute-start | bytes 417800 | tf_op jit(solution)/shard_map/ppermute | solution.py:397
  42.0 2.6 %collective-permute-start.2 = (bf16[2,272,128]{2,1,0:T(8,128)(2,1)S(1)}, bf16[2,272,128]{2,1,0:T(8,128)(2,1)S(1)}, u32[]{:S(2)}, u32[]{:S(2)}) collective-permute-start(bf16[2,272,128]{2,1,0:T(8,128)(2,1)S(1)} %get-tuple-element.54), channel_id=1, source_target_pairs={{0,5},{1,4},{2,7},{3,6},{4,1},{5,0},{6,3},{7,2},{8,13},{9,12},{10,... | collective-permute-start | bytes 417800 | tf_op jit(solution)/shard_map/ppermute | solution.py:397
  44.6 2.8 %collective-permute-start.3 = (bf16[2,272,128]{2,1,0:T(8,128)(2,1)S(1)}, bf16[2,272,128]{2,1,0:T(8,128)(2,1)S(1)}, u32[]{:S(2)}, u32[]{:S(2)}) collective-permute-start(bf16[2,272,128]{2,1,0:T(8,128)(2,1)S(1)} %get-tuple-element.55), channel_id=1, source_target_pairs={{0,6},{1,7},{2,4},{3,5},{4,2},{5,3},{6,0},{7,1},{8,14},{9,15},{10,... | collective-permute-start | bytes 417800 | tf_op jit(solution)/shard_map/ppermute | solution.py:397
  47.4 3.0 %collective-permute-done.7.refs_3_ = bf16[2,272,128]{2,1,0:T(8,128)(2,1)S(1)} collective-permute-done((bf16[2,272,128]{2,1,0:T(8,128)(2,1)S(1)}, bf16[2,272,128]{2,1,0:T(8,128)(2,1)S(1)}, u32[]{:S(2)}, u32[]{:S(2)}) %collective-permute-start.7) | collective-permute-done | bytes 139296 | tf_op jit(solution)/shard_map/ppermute | solution.py:397
  50.4 1.2 collective-permute-start.4
  51.6 9.2 %attend.2 = (bf16[4,256,128]{2,1,0:T(8,128)(2,1)S(1)}, bf16[4,256,128]{2,1,0:T(8,128)(2,1)S(1)}, f32[8192,128]{1,0:T(8,128)S(1)}, bf16[8192,128]{1,0:T(8,128)(2,1)S(1)}) custom-call(s32[5]{0:T(128)S(1)} %copy-done, bf16[2,272,128]{2,1,0:T(8,128)(2,1)S(1)} %get-tuple-element.57.refs_0_, bf16[2,272,128]{2,1,0:T(8,128)(2,1)S(1)} %collective-permute-done.5.refs_1_, ...), custom_call_target="tpu_custom_call" | custom-call | tf_op jit(solution)/shard_map/attend/pallas_call | solution.py:301
  60.8 1.6 %collective-permute-done.2.refs_1_ = bf16[2,272,128]{2,1,0:T(8,128)(2,1)S(1)} collective-permute-done((bf16[2,272,128]{2,1,0:T(8,128)(2,1)S(1)}, bf16[2,272,128]{2,1,0:T(8,128)(2,1)S(1)}, u32[]{:S(2)}, u32[]{:S(2)}) %collective-permute-start.2) | collective-permute-done | bytes 139296 | tf_op jit(solution)/shard_map/ppermute | solution.py:397
  62.4 10.1 %attend.3 = (bf16[4,256,128]{2,1,0:T(8,128)(2,1)S(1)}, bf16[4,256,128]{2,1,0:T(8,128)(2,1)S(1)}, f32[4096,128]{1,0:T(8,128)S(1)}, bf16[4096,128]{1,0:T(8,128)(2,1)S(1)}) custom-call(s32[5]{0:T(128)S(1)} %copy-done, bf16[2,272,128]{2,1,0:T(8,128)(2,1)S(1)} %collective-permute-done.1.refs_0_, bf16[2,272,128]{2,1,0:T(8,128)(2,1)S(1)} %collective-permute-done.2.refs_1_, ...), custom_call_target="tpu_custom_call" | custom-call | tf_op jit(solution)/shard_map/attend/pallas_call | solution.py:301
  72.5 0.1 collective-permute-start.19
  72.5 1.1 collective-permute-start.16
  73.6 5.3 %collective-permute-start.17 = (bf16[4,256,128]{2,1,0:T(8,128)(2,1)S(1)}, bf16[4,256,128]{2,1,0:T(8,128)(2,1)S(1)}, u32[]{:S(2)}, u32[]{:S(2)}) collective-permute-start(bf16[4,256,128]{2,1,0:T(8,128)(2,1)S(1)} %get-tuple-element.72), channel_id=1, source_target_pairs={{0,4},{2,6},{4,0},{6,2},{1,5},{3,7},{5,1},{7,3},{8,12},{10,14},{12... | collective-permute-start | bytes 786440 | tf_op jit(solution)/shard_map/ppermute | solution.py:397
  78.9 0.8 sum_shares.1
  79.8 2.6 %collective-permute-start.20 = (bf16[512,128]{1,0:T(8,128)(2,1)S(1)}, bf16[512,128]{1,0:T(8,128)(2,1)S(1)}, u32[]{:S(2)}, u32[]{:S(2)}) collective-permute-start(bf16[512,128]{1,0:T(8,128)(2,1)S(1)} %get-tuple-element.88), channel_id=1, source_target_pairs={{0,7},{1,6},{2,5},{3,4},{4,11},{5,10},{6,9},{7,8},{8,3},{9,2},{10,... | collective-permute-start | bytes 393224 | tf_op jit(solution)/shard_map/ppermute | solution.py:423
  82.4 1.4 %collective-permute-start.21 = (bf16[512,128]{1,0:T(8,128)(2,1)S(1)}, bf16[512,128]{1,0:T(8,128)(2,1)S(1)}, u32[]{:S(2)}, u32[]{:S(2)}) collective-permute-start(bf16[512,128]{1,0:T(8,128)(2,1)S(1)} %get-tuple-element.89), channel_id=1, source_target_pairs={{0,6},{1,7},{2,4},{3,5},{4,10},{5,11},{6,8},{7,9},{8,2},{9,3},{10,... | collective-permute-start | bytes 393224 | tf_op jit(solution)/shard_map/ppermute | solution.py:423
  83.8 11.7 %collective-permute-start.22 = (bf16[512,128]{1,0:T(8,128)(2,1)S(1)}, bf16[512,128]{1,0:T(8,128)(2,1)S(1)}, u32[]{:S(2)}, u32[]{:S(2)}) collective-permute-start(bf16[512,128]{1,0:T(8,128)(2,1)S(1)} %get-tuple-element.90), channel_id=1, source_target_pairs={{0,5},{1,4},{2,7},{3,6},{4,9},{5,8},{6,11},{7,10},{8,1},{9,0},{10,... | collective-permute-start | bytes 393224 | tf_op jit(solution)/shard_map/ppermute | solution.py:423
  95.4 8.7 %collective-permute-done.17.refs_1_ = bf16[4,256,128]{2,1,0:T(8,128)(2,1)S(1)} collective-permute-done((bf16[4,256,128]{2,1,0:T(8,128)(2,1)S(1)}, bf16[4,256,128]{2,1,0:T(8,128)(2,1)S(1)}, u32[]{:S(2)}, u32[]{:S(2)}) %collective-permute-start.17) | collective-permute-done | bytes 262176 | tf_op jit(solution)/shard_map/ppermute | solution.py:397
  104.1 1.6 %join_planes.1 = bf16[4,4,256,128]{3,2,1,0:T(8,128)(2,1)} custom-call(s32[5]{0:T(128)S(1)} %copy-done, bf16[4,256,128]{2,1,0:T(8,128)(2,1)S(1)} %collective-permute-done.16.refs_0_, bf16[4,256,128]{2,1,0:T(8,128)(2,1)S(1)} %collective-permute-done.17.refs_1_, bf16[4,256,128]{2,1,0:T(8,128)(2,1)S(1)} %collective-permute-done.18.refs_2_, ...), custom_call_target="tpu_custom_call" | custom-call | tf_op jit(solution)/shard_map/join_planes/pallas_call | solution.py:331
  105.7 3.5 %all-to-all-start = ((bf16[4,4,256,128]{3,2,1,0:T(8,128)(2,1)}), bf16[4,4,256,128]{3,2,1,0:T(8,128)(2,1)S(1)}, u32[]{:S(2)}, u32[]{:S(2)}) async-start(bf16[4,4,256,128]{3,2,1,0:T(8,128)(2,1)} %join_planes.1), calls=%async_computation | async-start | bytes 2097152 | tf_op jit(solution)/shard_map/all_to_all | solution.py:462
  109.3 1.9 %collective-permute-start.23 = (bf16[512,128]{1,0:T(8,128)(2,1)S(1)}, bf16[512,128]{1,0:T(8,128)(2,1)S(1)}, u32[]{:S(2)}, u32[]{:S(2)}) collective-permute-start(bf16[512,128]{1,0:T(8,128)(2,1)S(1)} %get-tuple-element.91), channel_id=1, source_target_pairs={{0,4},{1,5},{2,6},{3,7},{4,8},{5,9},{6,10},{7,11},{8,0},{9,1},{10,... | collective-permute-start | bytes 393224 | tf_op jit(solution)/shard_map/ppermute | solution.py:423
  111.2 3.3 %collective-permute-start.24 = (bf16[512,128]{1,0:T(8,128)(2,1)S(1)}, bf16[512,128]{1,0:T(8,128)(2,1)S(1)}, u32[]{:S(2)}, u32[]{:S(2)}) collective-permute-start(bf16[512,128]{1,0:T(8,128)(2,1)S(1)} %get-tuple-element.92), channel_id=1, source_target_pairs={{0,3},{1,2},{2,1},{3,0},{4,15},{5,14},{6,13},{7,12},{8,7},{9,6},{1... | collective-permute-start | bytes 393224 | tf_op jit(solution)/shard_map/ppermute | solution.py:423
  114.5 0.2 collective-permute-start.25
  114.7 0.4 collective-permute-start.26
  115.1 0.7 collective-permute-start.27
  115.8 5.7 %collective-permute-done.24.refs_4_ = bf16[512,128]{1,0:T(8,128)(2,1)S(1)} collective-permute-done((bf16[512,128]{1,0:T(8,128)(2,1)S(1)}, bf16[512,128]{1,0:T(8,128)(2,1)S(1)}, u32[]{:S(2)}, u32[]{:S(2)}) %collective-permute-start.24) | collective-permute-done | bytes 131104 | tf_op jit(solution)/shard_map/ppermute | solution.py:423
  121.5 1.8 %collective-permute-done.25.refs_5_ = bf16[512,128]{1,0:T(8,128)(2,1)S(1)} collective-permute-done((bf16[512,128]{1,0:T(8,128)(2,1)S(1)}, bf16[512,128]{1,0:T(8,128)(2,1)S(1)}, u32[]{:S(2)}, u32[]{:S(2)}) %collective-permute-start.25) | collective-permute-done | bytes 131104 | tf_op jit(solution)/shard_map/ppermute | solution.py:423
  123.4 5.6 %collective-permute-done.26.refs_6_ = bf16[512,128]{1,0:T(8,128)(2,1)S(1)} collective-permute-done((bf16[512,128]{1,0:T(8,128)(2,1)S(1)}, bf16[512,128]{1,0:T(8,128)(2,1)S(1)}, u32[]{:S(2)}, u32[]{:S(2)}) %collective-permute-start.26) | collective-permute-done | bytes 131104 | tf_op jit(solution)/shard_map/ppermute | solution.py:423
  128.9 1.7 %unpack_dimension.1 = (bf16[1024,256]{1,0:T(8,128)(2,1)}, bf16[1024,256]{1,0:T(8,128)(2,1)}) custom-call(s32[5]{0:T(128)S(1)} %copy-done, bf16[512,128]{1,0:T(8,128)(2,1)S(1)} %collective-permute-done.20.refs_0_, bf16[512,128]{1,0:T(8,128)(2,1)S(1)} %collective-permute-done.21.refs_1_, bf16[512,128]{1,0:T(8,128)(2,1)S(1)} %collective-permute-done.22.refs_2_, ...), custom_call_target="tpu_custom_call" | custom-call | flops 5750000128 | tf_op jit(solution)/shard_map/unpack_dimension/pallas_call | solution.py:385
  130.7 1.1 unpack_fact.1
  (34 shorter events, 0.1 us)
Async XLA Ops:
  1.2 17.8 %copy-start.5 = (s32[2]{0:T(128)S(1)}, s32[2]{0:T(128)}, u32[]{:S(2)}) copy-start(s32[2]{0:T(128)} %param.11) | copy-start | bytes 28
  1.2 17.9 %copy-start = (s32[5]{0:T(128)S(1)}, s32[5]{0:T(128)}, u32[]{:S(2)}) copy-start(s32[5]{0:T(128)} %stack.23.place) | copy-start | bytes 64
  1.2 17.9 %copy-start.1 = (bf16[256,1024]{1,0:T(8,128)(2,1)S(1)}, bf16[256,1024]{1,0:T(8,128)(2,1)}, u32[]{:S(2)}) copy-start(bf16[256,1024]{1,0:T(8,128)(2,1)} %queries.1) | copy-start | bytes 1572868
  1.2 17.9 %copy-start.2 = (bf16[256,1024]{1,0:T(8,128)(2,1)S(1)}, bf16[256,1024]{1,0:T(8,128)(2,1)}, u32[]{:S(2)}) copy-start(bf16[256,1024]{1,0:T(8,128)(2,1)} %cotangent.1) | copy-start | bytes 1572868
  1.2 17.9 %copy-start.4 = (s32[2,8]{1,0:T(2,128)S(1)}, s32[2,8]{1,0:T(2,128)}, u32[]{:S(2)}) copy-start(s32[2,8]{1,0:T(2,128)} %block_lists.1) | copy-start | bytes 196
  4.5 8.8 %collective-permute-start.8 = (bf16[512,128]{1,0:T(8,128)(2,1)}, bf16[512,128]{1,0:T(8,128)(2,1)S(1)}, u32[]{:S(2)}, u32[]{:S(2)}) collective-permute-start(bf16[512,128]{1,0:T(8,128)(2,1)} %get-tuple-element.62), channel_id=1, source_target_pairs={{0,1},{1,0},{2,3},{3,2},{4,5},{5,4},{6,7},{7,6},{8,9},{9,8},{10,11... | collective-permute-start | bytes 393224 | tf_op jit(solution)/shard_map/ppermute | solution.py:397
  7.4 10.9 %collective-permute-start.9 = (bf16[512,128]{1,0:T(8,128)(2,1)}, bf16[512,128]{1,0:T(8,128)(2,1)S(1)}, u32[]{:S(2)}, u32[]{:S(2)}) collective-permute-start(bf16[512,128]{1,0:T(8,128)(2,1)} %get-tuple-element.63), channel_id=1, source_target_pairs={{0,2},{1,3},{2,0},{3,1},{4,6},{5,7},{6,4},{7,5},{8,10},{9,11},{10,... | collective-permute-start | bytes 393224 | tf_op jit(solution)/shard_map/ppermute | solution.py:397
  9.0 11.1 %collective-permute-start.10 = (bf16[512,128]{1,0:T(8,128)(2,1)}, bf16[512,128]{1,0:T(8,128)(2,1)S(1)}, u32[]{:S(2)}, u32[]{:S(2)}) collective-permute-start(bf16[512,128]{1,0:T(8,128)(2,1)} %get-tuple-element.64), channel_id=1, source_target_pairs={{0,3},{1,2},{2,1},{3,0},{4,7},{5,6},{6,5},{7,4},{8,11},{9,10},{10,... | collective-permute-start | bytes 393224 | tf_op jit(solution)/shard_map/ppermute | solution.py:397
  9.0 12.7 %collective-permute-start.11 = (bf16[512,128]{1,0:T(8,128)(2,1)}, bf16[512,128]{1,0:T(8,128)(2,1)S(1)}, u32[]{:S(2)}, u32[]{:S(2)}) collective-permute-start(bf16[512,128]{1,0:T(8,128)(2,1)} %get-tuple-element.65), channel_id=1, source_target_pairs={{0,4},{1,5},{2,6},{3,7},{4,0},{5,1},{6,2},{7,3},{8,12},{9,13},{10,... | collective-permute-start | bytes 393224 | tf_op jit(solution)/shard_map/ppermute | solution.py:397
  12.0 19.7 %collective-permute-start.12 = (bf16[512,128]{1,0:T(8,128)(2,1)}, bf16[512,128]{1,0:T(8,128)(2,1)S(1)}, u32[]{:S(2)}, u32[]{:S(2)}) collective-permute-start(bf16[512,128]{1,0:T(8,128)(2,1)} %get-tuple-element.66), channel_id=1, source_target_pairs={{0,5},{1,4},{2,7},{3,6},{4,1},{5,0},{6,3},{7,2},{8,13},{9,12},{10,... | collective-permute-start | bytes 393224 | tf_op jit(solution)/shard_map/ppermute | solution.py:397
  13.3 18.4 %collective-permute-start.13 = (bf16[512,128]{1,0:T(8,128)(2,1)}, bf16[512,128]{1,0:T(8,128)(2,1)S(1)}, u32[]{:S(2)}, u32[]{:S(2)}) collective-permute-start(bf16[512,128]{1,0:T(8,128)(2,1)} %get-tuple-element.67), channel_id=1, source_target_pairs={{0,6},{1,7},{2,4},{3,5},{4,2},{5,3},{6,0},{7,1},{8,14},{9,15},{10,... | collective-permute-start | bytes 393224 | tf_op jit(solution)/shard_map/ppermute | solution.py:397
  18.4 13.3 %collective-permute-start.14 = (bf16[512,128]{1,0:T(8,128)(2,1)}, bf16[512,128]{1,0:T(8,128)(2,1)S(1)}, u32[]{:S(2)}, u32[]{:S(2)}) collective-permute-start(bf16[512,128]{1,0:T(8,128)(2,1)} %get-tuple-element.68), channel_id=1, source_target_pairs={{0,7},{1,6},{2,5},{3,4},{4,3},{5,2},{6,1},{7,0},{8,15},{9,14},{10,... | collective-permute-start | bytes 393224 | tf_op jit(solution)/shard_map/ppermute | solution.py:397
  19.2 12.5 %copy-start.3 = (bf16[512,128]{1,0:T(8,128)(2,1)S(1)}, bf16[512,128]{1,0:T(8,128)(2,1)}, u32[]{:S(2)}) copy-start(bf16[512,128]{1,0:T(8,128)(2,1)} %get-tuple-element.61.refs_0_) | copy-start | bytes 393220
  20.2 12.5 %collective-permute-start = (bf16[8,272,128]{2,1,0:T(8,128)(2,1)S(1)}, bf16[8,272,128]{2,1,0:T(8,128)(2,1)S(1)}, u32[]{:S(2)}, u32[]{:S(2)}) collective-permute-start(bf16[8,272,128]{2,1,0:T(8,128)(2,1)S(1)} %get-tuple-element.52), channel_id=1, source_target_pairs={{0,16},{16,0},{1,17},{17,1},{2,18},{18,2},{3,19},{19,3},{4,20},{20... | collective-permute-start | bytes 1671176 | tf_op jit(solution)/shard_map/ppermute | solution.py:397
  31.8 19.9 %collective-permute-start.15 = (bf16[4096,128]{1,0:T(8,128)(2,1)S(1)}, bf16[4096,128]{1,0:T(8,128)(2,1)S(1)}, u32[]{:S(2)}, u32[]{:S(2)}) collective-permute-start(bf16[4096,128]{1,0:T(8,128)(2,1)S(1)} %stack_chunks.1.refs_4_), channel_id=1, source_target_pairs={{0,8},{8,0},{1,9},{9,1},{2,10},{10,2},{3,11},{11,3},{4,12},{12,4},... | collective-permute-start | bytes 3145736 | tf_op jit(solution)/shard_map/ppermute | solution.py:397
  32.7 9.3 %collective-permute-start.5 = (bf16[2,272,128]{2,1,0:T(8,128)(2,1)S(1)}, bf16[2,272,128]{2,1,0:T(8,128)(2,1)S(1)}, u32[]{:S(2)}, u32[]{:S(2)}) collective-permute-start(bf16[2,272,128]{2,1,0:T(8,128)(2,1)S(1)} %get-tuple-element.58), channel_id=1, source_target_pairs={{0,1},{1,0},{2,3},{3,2},{4,5},{5,4},{6,7},{7,6},{8,9},{9,8},{10,11... | collective-permute-start | bytes 417800 | tf_op jit(solution)/shard_map/ppermute | solution.py:397
  34.5 10.1 %collective-permute-start.6 = (bf16[2,272,128]{2,1,0:T(8,128)(2,1)S(1)}, bf16[2,272,128]{2,1,0:T(8,128)(2,1)S(1)}, u32[]{:S(2)}, u32[]{:S(2)}) collective-permute-start(bf16[2,272,128]{2,1,0:T(8,128)(2,1)S(1)} %get-tuple-element.59), channel_id=1, source_target_pairs={{0,2},{1,3},{2,0},{3,1},{4,6},{5,7},{6,4},{7,5},{8,10},{9,11},{10,... | collective-permute-start | bytes 417800 | tf_op jit(solution)/shard_map/ppermute | solution.py:397
  37.4 13.0 %collective-permute-start.7 = (bf16[2,272,128]{2,1,0:T(8,128)(2,1)S(1)}, bf16[2,272,128]{2,1,0:T(8,128)(2,1)S(1)}, u32[]{:S(2)}, u32[]{:S(2)}) collective-permute-start(bf16[2,272,128]{2,1,0:T(8,128)(2,1)S(1)} %get-tuple-element.60), channel_id=1, source_target_pairs={{0,3},{1,2},{2,1},{3,0},{4,7},{5,6},{6,5},{7,4},{8,11},{9,10},{10,... | collective-permute-start | bytes 417800 | tf_op jit(solution)/shard_map/ppermute | solution.py:397
  38.5 22.3 %collective-permute-start.1 = (bf16[2,272,128]{2,1,0:T(8,128)(2,1)S(1)}, bf16[2,272,128]{2,1,0:T(8,128)(2,1)S(1)}, u32[]{:S(2)}, u32[]{:S(2)}) collective-permute-start(bf16[2,272,128]{2,1,0:T(8,128)(2,1)S(1)} %get-tuple-element.53), channel_id=1, source_target_pairs={{0,4},{1,5},{2,6},{3,7},{4,0},{5,1},{6,2},{7,3},{8,12},{9,13},{10,... | collective-permute-start | bytes 417800 | tf_op jit(solution)/shard_map/ppermute | solution.py:397
  42.0 20.3 %collective-permute-start.2 = (bf16[2,272,128]{2,1,0:T(8,128)(2,1)S(1)}, bf16[2,272,128]{2,1,0:T(8,128)(2,1)S(1)}, u32[]{:S(2)}, u32[]{:S(2)}) collective-permute-start(bf16[2,272,128]{2,1,0:T(8,128)(2,1)S(1)} %get-tuple-element.54), channel_id=1, source_target_pairs={{0,5},{1,4},{2,7},{3,6},{4,1},{5,0},{6,3},{7,2},{8,13},{9,12},{10,... | collective-permute-start | bytes 417800 | tf_op jit(solution)/shard_map/ppermute | solution.py:397
  44.6 17.8 %collective-permute-start.3 = (bf16[2,272,128]{2,1,0:T(8,128)(2,1)S(1)}, bf16[2,272,128]{2,1,0:T(8,128)(2,1)S(1)}, u32[]{:S(2)}, u32[]{:S(2)}) collective-permute-start(bf16[2,272,128]{2,1,0:T(8,128)(2,1)S(1)} %get-tuple-element.55), channel_id=1, source_target_pairs={{0,6},{1,7},{2,4},{3,5},{4,2},{5,3},{6,0},{7,1},{8,14},{9,15},{10,... | collective-permute-start | bytes 417800 | tf_op jit(solution)/shard_map/ppermute | solution.py:397
  50.4 12.0 %collective-permute-start.4 = (bf16[2,272,128]{2,1,0:T(8,128)(2,1)S(1)}, bf16[2,272,128]{2,1,0:T(8,128)(2,1)S(1)}, u32[]{:S(2)}, u32[]{:S(2)}) collective-permute-start(bf16[2,272,128]{2,1,0:T(8,128)(2,1)S(1)} %get-tuple-element.56), channel_id=1, source_target_pairs={{0,7},{1,6},{2,5},{3,4},{4,3},{5,2},{6,1},{7,0},{8,15},{9,14},{10,... | collective-permute-start | bytes 417800 | tf_op jit(solution)/shard_map/ppermute | solution.py:397
  72.5 6.5 %collective-permute-start.19 = (bf16[4096,128]{1,0:T(8,128)(2,1)S(1)}, bf16[4096,128]{1,0:T(8,128)(2,1)S(1)}, u32[]{:S(2)}, u32[]{:S(2)}) collective-permute-start(bf16[4096,128]{1,0:T(8,128)(2,1)S(1)} %get-tuple-element.76), channel_id=1, source_target_pairs={{0,8},{8,0},{1,9},{9,1},{2,10},{10,2},{3,11},{11,3},{4,12},{12,4},... | collective-permute-start | bytes 3145736 | tf_op jit(solution)/shard_map/ppermute | solution.py:397
  72.5 11.2 %collective-permute-start.16 = (bf16[4,256,128]{2,1,0:T(8,128)(2,1)S(1)}, bf16[4,256,128]{2,1,0:T(8,128)(2,1)S(1)}, u32[]{:S(2)}, u32[]{:S(2)}) collective-permute-start(bf16[4,256,128]{2,1,0:T(8,128)(2,1)S(1)} %get-tuple-element.71), channel_id=1, source_target_pairs={{0,6},{2,4},{4,2},{6,0},{1,7},{3,5},{5,3},{7,1},{8,14},{10,12},{12... | collective-permute-start | bytes 786440 | tf_op jit(solution)/shard_map/ppermute | solution.py:397
  73.6 30.5 %collective-permute-start.17 = (bf16[4,256,128]{2,1,0:T(8,128)(2,1)S(1)}, bf16[4,256,128]{2,1,0:T(8,128)(2,1)S(1)}, u32[]{:S(2)}, u32[]{:S(2)}) collective-permute-start(bf16[4,256,128]{2,1,0:T(8,128)(2,1)S(1)} %get-tuple-element.72), channel_id=1, source_target_pairs={{0,4},{2,6},{4,0},{6,2},{1,5},{3,7},{5,1},{7,3},{8,12},{10,14},{12... | collective-permute-start | bytes 786440 | tf_op jit(solution)/shard_map/ppermute | solution.py:397
  78.9 25.2 %collective-permute-start.18 = (bf16[4,256,128]{2,1,0:T(8,128)(2,1)S(1)}, bf16[4,256,128]{2,1,0:T(8,128)(2,1)S(1)}, u32[]{:S(2)}, u32[]{:S(2)}) collective-permute-start(bf16[4,256,128]{2,1,0:T(8,128)(2,1)S(1)} %get-tuple-element.73), channel_id=1, source_target_pairs={{0,2},{2,0},{4,6},{6,4},{1,3},{3,1},{5,7},{7,5},{8,10},{10,8},{12,... | collective-permute-start | bytes 786440 | tf_op jit(solution)/shard_map/ppermute | solution.py:397
  79.8 34.7 %collective-permute-start.20 = (bf16[512,128]{1,0:T(8,128)(2,1)S(1)}, bf16[512,128]{1,0:T(8,128)(2,1)S(1)}, u32[]{:S(2)}, u32[]{:S(2)}) collective-permute-start(bf16[512,128]{1,0:T(8,128)(2,1)S(1)} %get-tuple-element.88), channel_id=1, source_target_pairs={{0,7},{1,6},{2,5},{3,4},{4,11},{5,10},{6,9},{7,8},{8,3},{9,2},{10,... | collective-permute-start | bytes 393224 | tf_op jit(solution)/shard_map/ppermute | solution.py:423
  82.4 32.3 %collective-permute-start.21 = (bf16[512,128]{1,0:T(8,128)(2,1)S(1)}, bf16[512,128]{1,0:T(8,128)(2,1)S(1)}, u32[]{:S(2)}, u32[]{:S(2)}) collective-permute-start(bf16[512,128]{1,0:T(8,128)(2,1)S(1)} %get-tuple-element.89), channel_id=1, source_target_pairs={{0,6},{1,7},{2,4},{3,5},{4,10},{5,11},{6,8},{7,9},{8,2},{9,3},{10,... | collective-permute-start | bytes 393224 | tf_op jit(solution)/shard_map/ppermute | solution.py:423
  83.8 31.3 %collective-permute-start.22 = (bf16[512,128]{1,0:T(8,128)(2,1)S(1)}, bf16[512,128]{1,0:T(8,128)(2,1)S(1)}, u32[]{:S(2)}, u32[]{:S(2)}) collective-permute-start(bf16[512,128]{1,0:T(8,128)(2,1)S(1)} %get-tuple-element.90), channel_id=1, source_target_pairs={{0,5},{1,4},{2,7},{3,6},{4,9},{5,8},{6,11},{7,10},{8,1},{9,0},{10,... | collective-permute-start | bytes 393224 | tf_op jit(solution)/shard_map/ppermute | solution.py:423
  105.7 24.9 %all-to-all-start = ((bf16[4,4,256,128]{3,2,1,0:T(8,128)(2,1)}), bf16[4,4,256,128]{3,2,1,0:T(8,128)(2,1)S(1)}, u32[]{:S(2)}, u32[]{:S(2)}) async-start(bf16[4,4,256,128]{3,2,1,0:T(8,128)(2,1)} %join_planes.1), calls=%async_computation | async-start | bytes 2097152 | tf_op jit(solution)/shard_map/all_to_all | solution.py:462
  109.3 6.5 %collective-permute-start.23 = (bf16[512,128]{1,0:T(8,128)(2,1)S(1)}, bf16[512,128]{1,0:T(8,128)(2,1)S(1)}, u32[]{:S(2)}, u32[]{:S(2)}) collective-permute-start(bf16[512,128]{1,0:T(8,128)(2,1)S(1)} %get-tuple-element.91), channel_id=1, source_target_pairs={{0,4},{1,5},{2,6},{3,7},{4,8},{5,9},{6,10},{7,11},{8,0},{9,1},{10,... | collective-permute-start | bytes 393224 | tf_op jit(solution)/shard_map/ppermute | solution.py:423
  111.2 10.3 %collective-permute-start.24 = (bf16[512,128]{1,0:T(8,128)(2,1)S(1)}, bf16[512,128]{1,0:T(8,128)(2,1)S(1)}, u32[]{:S(2)}, u32[]{:S(2)}) collective-permute-start(bf16[512,128]{1,0:T(8,128)(2,1)S(1)} %get-tuple-element.92), channel_id=1, source_target_pairs={{0,3},{1,2},{2,1},{3,0},{4,15},{5,14},{6,13},{7,12},{8,7},{9,6},{1... | collective-permute-start | bytes 393224 | tf_op jit(solution)/shard_map/ppermute | solution.py:423
  114.5 8.9 %collective-permute-start.25 = (bf16[512,128]{1,0:T(8,128)(2,1)S(1)}, bf16[512,128]{1,0:T(8,128)(2,1)S(1)}, u32[]{:S(2)}, u32[]{:S(2)}) collective-permute-start(bf16[512,128]{1,0:T(8,128)(2,1)S(1)} %get-tuple-element.93), channel_id=1, source_target_pairs={{0,2},{1,3},{2,0},{3,1},{4,14},{5,15},{6,12},{7,13},{8,6},{9,7},{1... | collective-permute-start | bytes 393224 | tf_op jit(solution)/shard_map/ppermute | solution.py:423
  114.7 14.3 %collective-permute-start.26 = (bf16[512,128]{1,0:T(8,128)(2,1)S(1)}, bf16[512,128]{1,0:T(8,128)(2,1)S(1)}, u32[]{:S(2)}, u32[]{:S(2)}) collective-permute-start(bf16[512,128]{1,0:T(8,128)(2,1)S(1)} %get-tuple-element.94), channel_id=1, source_target_pairs={{0,1},{1,0},{2,3},{3,2},{4,13},{5,12},{6,15},{7,14},{8,5},{9,4},{1... | collective-permute-start | bytes 393224 | tf_op jit(solution)/shard_map/ppermute | solution.py:423
  115.1 13.8 %collective-permute-start.27 = (bf16[512,128]{1,0:T(8,128)(2,1)S(1)}, bf16[512,128]{1,0:T(8,128)(2,1)S(1)}, u32[]{:S(2)}, u32[]{:S(2)}) collective-permute-start(bf16[512,128]{1,0:T(8,128)(2,1)S(1)} %get-tuple-element.95), channel_id=1, source_target_pairs={{0,0},{1,1},{2,2},{3,3},{4,12},{5,13},{6,14},{7,15},{8,4},{9,5},{1... | collective-permute-start | bytes 393224 | tf_op jit(solution)/shard_map/ppermute | solution.py:423

commit v4 on v3

--- a/solution.py
+++ b/solution.py
@@ -17,7 +17,7 @@
 NEG_FILL = -1e30
 PEAK = 1.15e9
 MIB = 1024 * 1024
-BATCHES = ((0, 4, 0), (4, 8, 0))
+BATCHES = ((0, 4, 0), (4, 6, 0), (6, 8, 60))
 SPLIT_COST = 0
 UNPACK_FACT = 2
 PLANES = 4

time: 132 us -> 129 us (0.977)
  waiting for transfers between devices: 38.7 us -> 36.9 us
  starting transfers between devices: 62.7 us -> 61.2 us
    ppermute x20, waiting for transfers between devices: 25.6 us -> 23.6 us  [by_xor(): return lax.ppermute(part, axis, [(i, i ^ index) for i in range(count)])]
    ppermute x20, starting transfers between devices: 37 us -> 35.3 us  [by_xor(): return lax.ppermute(part, axis, [(i, i ^ index) for i in range(count)])]
    pallas_call x2 -> x3, Pallas kernels: 19.3 us -> 20.2 us  [attend(): call(kernel, 'attend', outs, [SMEM] + [VMEM] * (count + len(tables) + len...]
  transfers between devices with their start and end apart: 29 -> 29, of which waited for: 9 -> 10; matrix products, arithmetic and copies ran while one was open for 0% -> 0% of each run, Pallas kernels for 11% -> 16%
where the time goes in v4:
time: 129 us
  starting transfers between devices  61.2 us (47%)
  waiting for transfers between devices  36.9 us (29%)
  Pallas kernels  29.7 us (23%)
    ppermute x20, starting transfers between devices, by_xor(): return lax.ppermute(part, axis, [(i, i ^ index) for i in range(count)])  35.3 us
    ppermute x20, waiting for transfers between devices, by_xor(): return lax.ppermute(part, axis, [(i, i ^ index) for i in range(count)])  23.6 us
    ppermute x8, starting transfers between devices, to_columns(): return lax.ppermute(chunk, ('share', 'z', 'y'), pairs)  22.3 us
    pallas_call x3, Pallas kernels, attend(): call(kernel, 'attend', outs, [SMEM] + [VMEM] * (count + len(tables) + len...  20.2 us
    ppermute x8, waiting for transfers between devices, to_columns(): return lax.ppermute(chunk, ('share', 'z', 'y'), pairs)  13.3 us
    all_to_all x1, starting transfers between devices, body(): lax.all_to_all(fact_out, ('x', 'y'), split_axis=0, concat_axis=0, tiled=T...  3.51 us
    pallas_call x1, Pallas kernels, pack_dimension(): pl.pallas_call(kernel, grid_spec=pltpu.PrefetchScalarGridSpec(num_scalar_...  3.22 us
  transfers between devices with their start and end apart: 29, of which 10 were waited for; matrix products, arithmetic and copies ran while one was open for 0% of the time, Pallas kernels for 16%

profile of v4, /device:TPU:0, one launch (start us, length us, event | category | flops | bytes accessed | tf_op | source)
XLA Modules:
  0.0 129.5 jit_solution(11271808000051506900)
XLA Ops:
  0.6 0.7 stack.23.place
  1.3 3.2 %pack_dimension.1 = (bf16[512,128]{1,0:T(8,128)(2,1)}, bf16[512,128]{1,0:T(8,128)(2,1)}, bf16[512,128]{1,0:T(8,128)(2,1)}, bf16[512,128]{1,0:T(8,128)(2,1)}, bf1...) custom-call(s32[5]{0:T(128)} %stack.23.place, ...), custom_call_target="tpu_custom_call" | custom-call | tf_op jit(solution)/shard_map/pack_dimension/pallas_call | solution.py:97
  4.6 3.0 %collective-permute-start.6 = (bf16[512,128]{1,0:T(8,128)(2,1)}, bf16[512,128]{1,0:T(8,128)(2,1)S(1)}, u32[]{:S(2)}, u32[]{:S(2)}) collective-permute-start(bf16[512,128]{1,0:T(8,128)(2,1)} %get-tuple-element.61), channel_id=1, source_target_pairs={{0,1},{1,0},{2,3},{3,2},{4,5},{5,4},{6,7},{7,6},{8,9},{9,8},{10,11... | collective-permute-start | bytes 393224 | tf_op jit(solution)/shard_map/ppermute | solution.py:397
  7.5 1.6 %collective-permute-start.7 = (bf16[512,128]{1,0:T(8,128)(2,1)}, bf16[512,128]{1,0:T(8,128)(2,1)S(1)}, u32[]{:S(2)}, u32[]{:S(2)}) collective-permute-start(bf16[512,128]{1,0:T(8,128)(2,1)} %get-tuple-element.62), channel_id=1, source_target_pairs={{0,2},{1,3},{2,0},{3,1},{4,6},{5,7},{6,4},{7,5},{8,10},{9,11},{10,... | collective-permute-start | bytes 393224 | tf_op jit(solution)/shard_map/ppermute | solution.py:397
  9.1 3.0 %collective-permute-start.9 = (bf16[512,128]{1,0:T(8,128)(2,1)}, bf16[512,128]{1,0:T(8,128)(2,1)S(1)}, u32[]{:S(2)}, u32[]{:S(2)}) collective-permute-start(bf16[512,128]{1,0:T(8,128)(2,1)} %get-tuple-element.64), channel_id=1, source_target_pairs={{0,4},{1,5},{2,6},{3,7},{4,0},{5,1},{6,2},{7,3},{8,12},{9,13},{10,... | collective-permute-start | bytes 393224 | tf_op jit(solution)/shard_map/ppermute | solution.py:397
  12.1 1.3 collective-permute-start.10
  13.4 3.6 %collective-permute-start.11 = (bf16[512,128]{1,0:T(8,128)(2,1)}, bf16[512,128]{1,0:T(8,128)(2,1)S(1)}, u32[]{:S(2)}, u32[]{:S(2)}) collective-permute-start(bf16[512,128]{1,0:T(8,128)(2,1)} %get-tuple-element.66), channel_id=1, source_target_pairs={{0,6},{1,7},{2,4},{3,5},{4,2},{5,3},{6,0},{7,1},{8,14},{9,15},{10,... | collective-permute-start | bytes 393224 | tf_op jit(solution)/shard_map/ppermute | solution.py:397
  17.0 1.5 %collective-permute-done.7.refs_2_ = bf16[512,128]{1,0:T(8,128)(2,1)S(1)} collective-permute-done((bf16[512,128]{1,0:T(8,128)(2,1)}, bf16[512,128]{1,0:T(8,128)(2,1)S(1)}, u32[]{:S(2)}, u32[]{:S(2)}) %collective-permute-start.7) | collective-permute-done | bytes 131104 | tf_op jit(solution)/shard_map/ppermute | solution.py:397
  18.5 0.7 collective-permute-start.12
  19.1 0.1 copy.10.tile_lengths
  19.3 1.0 pack_fact.1
  20.2 1.6 %collective-permute-start = (bf16[8,272,128]{2,1,0:T(8,128)(2,1)S(1)}, bf16[8,272,128]{2,1,0:T(8,128)(2,1)S(1)}, u32[]{:S(2)}, u32[]{:S(2)}) collective-permute-start(bf16[8,272,128]{2,1,0:T(8,128)(2,1)S(1)} %get-tuple-element.53), channel_id=1, source_target_pairs={{0,16},{16,0},{1,17},{17,1},{2,18},{18,2},{3,19},{19,3},{4,20},{20... | collective-permute-start | bytes 1671176 | tf_op jit(solution)/shard_map/ppermute | solution.py:397
  21.8 9.9 %collective-permute-done.10.refs_5_ = bf16[512,128]{1,0:T(8,128)(2,1)S(1)} collective-permute-done((bf16[512,128]{1,0:T(8,128)(2,1)}, bf16[512,128]{1,0:T(8,128)(2,1)S(1)}, u32[]{:S(2)}, u32[]{:S(2)}) %collective-permute-start.10) | collective-permute-done | bytes 131104 | tf_op jit(solution)/shard_map/ppermute | solution.py:397
  31.8 0.1 stack_chunks.1.refs_4_
  31.9 0.8 collective-permute-done.refs_1_
  32.7 0.1 merge_fact.1
  32.8 1.8 %collective-permute-start.3 = (bf16[2,272,128]{2,1,0:T(8,128)(2,1)S(1)}, bf16[2,272,128]{2,1,0:T(8,128)(2,1)S(1)}, u32[]{:S(2)}, u32[]{:S(2)}) collective-permute-start(bf16[2,272,128]{2,1,0:T(8,128)(2,1)S(1)} %get-tuple-element.57), channel_id=1, source_target_pairs={{0,1},{1,0},{2,3},{3,2},{4,5},{5,4},{6,7},{7,6},{8,9},{9,8},{10,11... | collective-permute-start | bytes 417800 | tf_op jit(solution)/shard_map/ppermute | solution.py:397
  34.6 2.8 %collective-permute-start.4 = (bf16[2,272,128]{2,1,0:T(8,128)(2,1)S(1)}, bf16[2,272,128]{2,1,0:T(8,128)(2,1)S(1)}, u32[]{:S(2)}, u32[]{:S(2)}) collective-permute-start(bf16[2,272,128]{2,1,0:T(8,128)(2,1)S(1)} %get-tuple-element.58), channel_id=1, source_target_pairs={{0,2},{1,3},{2,0},{3,1},{4,6},{5,7},{6,4},{7,5},{8,10},{9,11},{10,... | collective-permute-start | bytes 417800 | tf_op jit(solution)/shard_map/ppermute | solution.py:397
  37.5 1.1 collective-permute-start.5
  38.6 3.5 %collective-permute-start.14 = (bf16[2,272,128]{2,1,0:T(8,128)(2,1)S(1)}, bf16[2,272,128]{2,1,0:T(8,128)(2,1)S(1)}, u32[]{:S(2)}, u32[]{:S(2)}) collective-permute-start(bf16[2,272,128]{2,1,0:T(8,128)(2,1)S(1)} %get-tuple-element.69), channel_id=1, source_target_pairs={{0,4},{1,5},{2,6},{3,7},{4,0},{5,1},{6,2},{7,3},{8,12},{9,13},{10,... | collective-permute-start | bytes 417800 | tf_op jit(solution)/shard_map/ppermute | solution.py:397
  42.1 2.6 %collective-permute-start.15 = (bf16[2,272,128]{2,1,0:T(8,128)(2,1)S(1)}, bf16[2,272,128]{2,1,0:T(8,128)(2,1)S(1)}, u32[]{:S(2)}, u32[]{:S(2)}) collective-permute-start(bf16[2,272,128]{2,1,0:T(8,128)(2,1)S(1)} %get-tuple-element.70), channel_id=1, source_target_pairs={{0,5},{1,4},{2,7},{3,6},{4,1},{5,0},{6,3},{7,2},{8,13},{9,12},{10,... | collective-permute-start | bytes 417800 | tf_op jit(solution)/shard_map/ppermute | solution.py:397
  44.7 2.8 %collective-permute-start.1 = (bf16[2,272,128]{2,1,0:T(8,128)(2,1)S(1)}, bf16[2,272,128]{2,1,0:T(8,128)(2,1)S(1)}, u32[]{:S(2)}, u32[]{:S(2)}) collective-permute-start(bf16[2,272,128]{2,1,0:T(8,128)(2,1)S(1)} %get-tuple-element.54), channel_id=1, source_target_pairs={{0,6},{1,7},{2,4},{3,5},{4,2},{5,3},{6,0},{7,1},{8,14},{9,15},{10,... | collective-permute-start | bytes 417800 | tf_op jit(solution)/shard_map/ppermute | solution.py:397
  47.5 3.0 %collective-permute-done.5.refs_3_ = bf16[2,272,128]{2,1,0:T(8,128)(2,1)S(1)} collective-permute-done((bf16[2,272,128]{2,1,0:T(8,128)(2,1)S(1)}, bf16[2,272,128]{2,1,0:T(8,128)(2,1)S(1)}, u32[]{:S(2)}, u32[]{:S(2)}) %collective-permute-start.5) | collective-permute-done | bytes 139296 | tf_op jit(solution)/shard_map/ppermute | solution.py:397
  50.5 1.2 collective-permute-start.2
  51.7 10.4 %attend.3 = (bf16[4,256,128]{2,1,0:T(8,128)(2,1)S(1)}, bf16[4,256,128]{2,1,0:T(8,128)(2,1)S(1)}, f32[8192,128]{1,0:T(8,128)S(1)}, bf16[8192,128]{1,0:T(8,128)(2,1)S(1)}) custom-call(s32[5]{0:T(128)S(1)} %copy-done, bf16[2,272,128]{2,1,0:T(8,128)(2,1)S(1)} %get-tuple-element.56.refs_0_, bf16[2,272,128]{2,1,0:T(8,128)(2,1)S(1)} %collective-permute-done.3.refs_1_, ...), custom_call_target="tpu_custom_call" | custom-call | tf_op jit(solution)/shard_map/attend/pallas_call | solution.py:301
  62.1 0.3 collective-permute-done.15.refs_1_
  62.5 4.7 %attend.4 = (bf16[4,256,128]{2,1,0:T(8,128)(2,1)S(1)}, f32[8192,128]{1,0:T(8,128)S(1)}) custom-call(s32[5]{0:T(128)S(1)} %copy-done, bf16[2,272,128]{2,1,0:T(8,128)(2,1)S(1)} %collective-permute-done.14.refs_0_, bf16[2,272,128]{2,1,0:T(8,128)(2,1)S(1)} %collective-permute-done.15.refs_1_, bf16[8192,128]{1,0:T(8,128)(2,1)S(1)} %get-tuple-element.68.refs_2_, ...), custom_call_target="tpu_custom_call" | custom-call | tf_op jit(solution)/shard_map/attend/pallas_call | solution.py:301
  67.2 5.1 %attend.5 = (bf16[4,256,128]{2,1,0:T(8,128)(2,1)S(1)}, f32[4096,128]{1,0:T(8,128)S(1)}, bf16[4096,128]{1,0:T(8,128)(2,1)S(1)}) custom-call(s32[5]{0:T(128)S(1)} %copy-done, bf16[2,272,128]{2,1,0:T(8,128)(2,1)S(1)} %collective-permute-done.1.refs_0_, bf16[2,272,128]{2,1,0:T(8,128)(2,1)S(1)} %collective-permute-done.2.refs_1_, ...), custom_call_target="tpu_custom_call" | custom-call | flops 69000003584 | tf_op jit(solution)/shard_map/attend/pallas_call | solution.py:301
  72.3 0.4 collective-permute-start.19
  72.7 3.5 %collective-permute-start.16 = (bf16[4,256,128]{2,1,0:T(8,128)(2,1)S(1)}, bf16[4,256,128]{2,1,0:T(8,128)(2,1)S(1)}, u32[]{:S(2)}, u32[]{:S(2)}) collective-permute-start(bf16[4,256,128]{2,1,0:T(8,128)(2,1)S(1)} %get-tuple-element.73), channel_id=1, source_target_pairs={{0,6},{2,4},{4,2},{6,0},{1,7},{3,5},{5,3},{7,1},{8,14},{10,12},{12... | collective-permute-start | bytes 786440 | tf_op jit(solution)/shard_map/ppermute | solution.py:397
  76.3 0.8 collective-permute-start.18
  77.1 0.7 sum_shares.1
  77.9 4.5 %collective-permute-start.20 = (bf16[512,128]{1,0:T(8,128)(2,1)S(1)}, bf16[512,128]{1,0:T(8,128)(2,1)S(1)}, u32[]{:S(2)}, u32[]{:S(2)}) collective-permute-start(bf16[512,128]{1,0:T(8,128)(2,1)S(1)} %get-tuple-element.90), channel_id=1, source_target_pairs={{0,7},{1,6},{2,5},{3,4},{4,11},{5,10},{6,9},{7,8},{8,3},{9,2},{10,... | collective-permute-start | bytes 393224 | tf_op jit(solution)/shard_map/ppermute | solution.py:423
  82.3 0.3 collective-permute-start.21
  82.6 1.2 collective-permute-done.16.refs_0_
  83.8 11.5 %collective-permute-start.22 = (bf16[512,128]{1,0:T(8,128)(2,1)S(1)}, bf16[512,128]{1,0:T(8,128)(2,1)S(1)}, u32[]{:S(2)}, u32[]{:S(2)}) collective-permute-start(bf16[512,128]{1,0:T(8,128)(2,1)S(1)} %get-tuple-element.92), channel_id=1, source_target_pairs={{0,5},{1,4},{2,7},{3,6},{4,9},{5,8},{6,11},{7,10},{8,1},{9,0},{10,... | collective-permute-start | bytes 393224 | tf_op jit(solution)/shard_map/ppermute | solution.py:423
  95.3 6.7 %collective-permute-done.17.refs_1_ = bf16[4,256,128]{2,1,0:T(8,128)(2,1)S(1)} collective-permute-done((bf16[4,256,128]{2,1,0:T(8,128)(2,1)S(1)}, bf16[4,256,128]{2,1,0:T(8,128)(2,1)S(1)}, u32[]{:S(2)}, u32[]{:S(2)}) %collective-permute-start.17) | collective-permute-done | bytes 262176 | tf_op jit(solution)/shard_map/ppermute | solution.py:397
  102.0 1.6 %join_planes.1 = bf16[4,4,256,128]{3,2,1,0:T(8,128)(2,1)} custom-call(s32[5]{0:T(128)S(1)} %copy-done, bf16[4,256,128]{2,1,0:T(8,128)(2,1)S(1)} %collective-permute-done.16.refs_0_, bf16[4,256,128]{2,1,0:T(8,128)(2,1)S(1)} %collective-permute-done.17.refs_1_, bf16[4,256,128]{2,1,0:T(8,128)(2,1)S(1)} %collective-permute-done.18.refs_2_, ...), custom_call_target="tpu_custom_call" | custom-call | tf_op jit(solution)/shard_map/join_planes/pallas_call | solution.py:331
  103.6 3.5 %all-to-all-start = ((bf16[4,4,256,128]{3,2,1,0:T(8,128)(2,1)}), bf16[4,4,256,128]{3,2,1,0:T(8,128)(2,1)S(1)}, u32[]{:S(2)}, u32[]{:S(2)}) async-start(bf16[4,4,256,128]{3,2,1,0:T(8,128)(2,1)} %join_planes.1), calls=%async_computation | async-start | bytes 2097152 | tf_op jit(solution)/shard_map/all_to_all | solution.py:462
  107.1 1.9 %collective-permute-start.23 = (bf16[512,128]{1,0:T(8,128)(2,1)S(1)}, bf16[512,128]{1,0:T(8,128)(2,1)S(1)}, u32[]{:S(2)}, u32[]{:S(2)}) collective-permute-start(bf16[512,128]{1,0:T(8,128)(2,1)S(1)} %get-tuple-element.93), channel_id=1, source_target_pairs={{0,4},{1,5},{2,6},{3,7},{4,8},{5,9},{6,10},{7,11},{8,0},{9,1},{10,... | collective-permute-start | bytes 393224 | tf_op jit(solution)/shard_map/ppermute | solution.py:423
  109.1 2.7 %collective-permute-start.24 = (bf16[512,128]{1,0:T(8,128)(2,1)S(1)}, bf16[512,128]{1,0:T(8,128)(2,1)S(1)}, u32[]{:S(2)}, u32[]{:S(2)}) collective-permute-start(bf16[512,128]{1,0:T(8,128)(2,1)S(1)} %get-tuple-element.94), channel_id=1, source_target_pairs={{0,3},{1,2},{2,1},{3,0},{4,15},{5,14},{6,13},{7,12},{8,7},{9,6},{1... | collective-permute-start | bytes 393224 | tf_op jit(solution)/shard_map/ppermute | solution.py:423
  111.8 0.8 collective-permute-start.25
  112.6 0.7 collective-permute-start.27
  113.3 5.9 %collective-permute-done.24.refs_4_ = bf16[512,128]{1,0:T(8,128)(2,1)S(1)} collective-permute-done((bf16[512,128]{1,0:T(8,128)(2,1)S(1)}, bf16[512,128]{1,0:T(8,128)(2,1)S(1)}, u32[]{:S(2)}, u32[]{:S(2)}) %collective-permute-start.24) | collective-permute-done | bytes 131104 | tf_op jit(solution)/shard_map/ppermute | solution.py:423
  119.2 2.0 %collective-permute-done.25.refs_5_ = bf16[512,128]{1,0:T(8,128)(2,1)S(1)} collective-permute-done((bf16[512,128]{1,0:T(8,128)(2,1)S(1)}, bf16[512,128]{1,0:T(8,128)(2,1)S(1)}, u32[]{:S(2)}, u32[]{:S(2)}) %collective-permute-start.25) | collective-permute-done | bytes 131104 | tf_op jit(solution)/shard_map/ppermute | solution.py:423
  121.1 5.5 %collective-permute-done.26.refs_6_ = bf16[512,128]{1,0:T(8,128)(2,1)S(1)} collective-permute-done((bf16[512,128]{1,0:T(8,128)(2,1)S(1)}, bf16[512,128]{1,0:T(8,128)(2,1)S(1)}, u32[]{:S(2)}, u32[]{:S(2)}) %collective-permute-start.26) | collective-permute-done | bytes 131104 | tf_op jit(solution)/shard_map/ppermute | solution.py:423
  126.6 1.7 %unpack_dimension.1 = (bf16[1024,256]{1,0:T(8,128)(2,1)}, bf16[1024,256]{1,0:T(8,128)(2,1)}) custom-call(s32[5]{0:T(128)S(1)} %copy-done, bf16[512,128]{1,0:T(8,128)(2,1)S(1)} %collective-permute-done.20.refs_0_, bf16[512,128]{1,0:T(8,128)(2,1)S(1)} %collective-permute-done.21.refs_1_, bf16[512,128]{1,0:T(8,128)(2,1)S(1)} %collective-permute-done.22.refs_2_, ...), custom_call_target="tpu_custom_call" | custom-call | flops 5750000128 | tf_op jit(solution)/shard_map/unpack_dimension/pallas_call | solution.py:385
  128.3 1.1 unpack_fact.1
  (35 shorter events, 0.2 us)
Async XLA Ops:
  1.3 17.8 %copy-start.5 = (s32[2]{0:T(128)S(1)}, s32[2]{0:T(128)}, u32[]{:S(2)}) copy-start(s32[2]{0:T(128)} %param.11) | copy-start | bytes 28
  1.3 17.9 %copy-start = (s32[5]{0:T(128)S(1)}, s32[5]{0:T(128)}, u32[]{:S(2)}) copy-start(s32[5]{0:T(128)} %stack.23.place) | copy-start | bytes 64
  1.3 17.9 %copy-start.1 = (bf16[256,1024]{1,0:T(8,128)(2,1)S(1)}, bf16[256,1024]{1,0:T(8,128)(2,1)}, u32[]{:S(2)}) copy-start(bf16[256,1024]{1,0:T(8,128)(2,1)} %queries.1) | copy-start | bytes 1572868
  1.3 17.9 %copy-start.2 = (bf16[256,1024]{1,0:T(8,128)(2,1)S(1)}, bf16[256,1024]{1,0:T(8,128)(2,1)}, u32[]{:S(2)}) copy-start(bf16[256,1024]{1,0:T(8,128)(2,1)} %cotangent.1) | copy-start | bytes 1572868
  1.3 17.9 %copy-start.4 = (s32[2,8]{1,0:T(2,128)S(1)}, s32[2,8]{1,0:T(2,128)}, u32[]{:S(2)}) copy-start(s32[2,8]{1,0:T(2,128)} %block_lists.1) | copy-start | bytes 196
  4.6 8.8 %collective-permute-start.6 = (bf16[512,128]{1,0:T(8,128)(2,1)}, bf16[512,128]{1,0:T(8,128)(2,1)S(1)}, u32[]{:S(2)}, u32[]{:S(2)}) collective-permute-start(bf16[512,128]{1,0:T(8,128)(2,1)} %get-tuple-element.61), channel_id=1, source_target_pairs={{0,1},{1,0},{2,3},{3,2},{4,5},{5,4},{6,7},{7,6},{8,9},{9,8},{10,11... | collective-permute-start | bytes 393224 | tf_op jit(solution)/shard_map/ppermute | solution.py:397
  7.5 10.9 %collective-permute-start.7 = (bf16[512,128]{1,0:T(8,128)(2,1)}, bf16[512,128]{1,0:T(8,128)(2,1)S(1)}, u32[]{:S(2)}, u32[]{:S(2)}) collective-permute-start(bf16[512,128]{1,0:T(8,128)(2,1)} %get-tuple-element.62), channel_id=1, source_target_pairs={{0,2},{1,3},{2,0},{3,1},{4,6},{5,7},{6,4},{7,5},{8,10},{9,11},{10,... | collective-permute-start | bytes 393224 | tf_op jit(solution)/shard_map/ppermute | solution.py:397
  9.1 11.1 %collective-permute-start.8 = (bf16[512,128]{1,0:T(8,128)(2,1)}, bf16[512,128]{1,0:T(8,128)(2,1)S(1)}, u32[]{:S(2)}, u32[]{:S(2)}) collective-permute-start(bf16[512,128]{1,0:T(8,128)(2,1)} %get-tuple-element.63), channel_id=1, source_target_pairs={{0,3},{1,2},{2,1},{3,0},{4,7},{5,6},{6,5},{7,4},{8,11},{9,10},{10,... | collective-permute-start | bytes 393224 | tf_op jit(solution)/shard_map/ppermute | solution.py:397
  9.1 12.7 %collective-permute-start.9 = (bf16[512,128]{1,0:T(8,128)(2,1)}, bf16[512,128]{1,0:T(8,128)(2,1)S(1)}, u32[]{:S(2)}, u32[]{:S(2)}) collective-permute-start(bf16[512,128]{1,0:T(8,128)(2,1)} %get-tuple-element.64), channel_id=1, source_target_pairs={{0,4},{1,5},{2,6},{3,7},{4,0},{5,1},{6,2},{7,3},{8,12},{9,13},{10,... | collective-permute-start | bytes 393224 | tf_op jit(solution)/shard_map/ppermute | solution.py:397
  12.1 19.7 %collective-permute-start.10 = (bf16[512,128]{1,0:T(8,128)(2,1)}, bf16[512,128]{1,0:T(8,128)(2,1)S(1)}, u32[]{:S(2)}, u32[]{:S(2)}) collective-permute-start(bf16[512,128]{1,0:T(8,128)(2,1)} %get-tuple-element.65), channel_id=1, source_target_pairs={{0,5},{1,4},{2,7},{3,6},{4,1},{5,0},{6,3},{7,2},{8,13},{9,12},{10,... | collective-permute-start | bytes 393224 | tf_op jit(solution)/shard_map/ppermute | solution.py:397
  13.4 18.4 %collective-permute-start.11 = (bf16[512,128]{1,0:T(8,128)(2,1)}, bf16[512,128]{1,0:T(8,128)(2,1)S(1)}, u32[]{:S(2)}, u32[]{:S(2)}) collective-permute-start(bf16[512,128]{1,0:T(8,128)(2,1)} %get-tuple-element.66), channel_id=1, source_target_pairs={{0,6},{1,7},{2,4},{3,5},{4,2},{5,3},{6,0},{7,1},{8,14},{9,15},{10,... | collective-permute-start | bytes 393224 | tf_op jit(solution)/shard_map/ppermute | solution.py:397
  18.5 13.3 %collective-permute-start.12 = (bf16[512,128]{1,0:T(8,128)(2,1)}, bf16[512,128]{1,0:T(8,128)(2,1)S(1)}, u32[]{:S(2)}, u32[]{:S(2)}) collective-permute-start(bf16[512,128]{1,0:T(8,128)(2,1)} %get-tuple-element.67), channel_id=1, source_target_pairs={{0,7},{1,6},{2,5},{3,4},{4,3},{5,2},{6,1},{7,0},{8,15},{9,14},{10,... | collective-permute-start | bytes 393224 | tf_op jit(solution)/shard_map/ppermute | solution.py:397
  19.2 12.5 %copy-start.3 = (bf16[512,128]{1,0:T(8,128)(2,1)S(1)}, bf16[512,128]{1,0:T(8,128)(2,1)}, u32[]{:S(2)}) copy-start(bf16[512,128]{1,0:T(8,128)(2,1)} %get-tuple-element.60.refs_0_) | copy-start | bytes 393220
  20.2 12.5 %collective-permute-start = (bf16[8,272,128]{2,1,0:T(8,128)(2,1)S(1)}, bf16[8,272,128]{2,1,0:T(8,128)(2,1)S(1)}, u32[]{:S(2)}, u32[]{:S(2)}) collective-permute-start(bf16[8,272,128]{2,1,0:T(8,128)(2,1)S(1)} %get-tuple-element.53), channel_id=1, source_target_pairs={{0,16},{16,0},{1,17},{17,1},{2,18},{18,2},{3,19},{19,3},{4,20},{20... | collective-permute-start | bytes 1671176 | tf_op jit(solution)/shard_map/ppermute | solution.py:397
  31.8 19.9 %collective-permute-start.13 = (bf16[4096,128]{1,0:T(8,128)(2,1)S(1)}, bf16[4096,128]{1,0:T(8,128)(2,1)S(1)}, u32[]{:S(2)}, u32[]{:S(2)}) collective-permute-start(bf16[4096,128]{1,0:T(8,128)(2,1)S(1)} %stack_chunks.1.refs_4_), channel_id=1, source_target_pairs={{0,8},{8,0},{1,9},{9,1},{2,10},{10,2},{3,11},{11,3},{4,12},{12,4},... | collective-permute-start | bytes 3145736 | tf_op jit(solution)/shard_map/ppermute | solution.py:397
  32.8 9.3 %collective-permute-start.3 = (bf16[2,272,128]{2,1,0:T(8,128)(2,1)S(1)}, bf16[2,272,128]{2,1,0:T(8,128)(2,1)S(1)}, u32[]{:S(2)}, u32[]{:S(2)}) collective-permute-start(bf16[2,272,128]{2,1,0:T(8,128)(2,1)S(1)} %get-tuple-element.57), channel_id=1, source_target_pairs={{0,1},{1,0},{2,3},{3,2},{4,5},{5,4},{6,7},{7,6},{8,9},{9,8},{10,11... | collective-permute-start | bytes 417800 | tf_op jit(solution)/shard_map/ppermute | solution.py:397
  34.6 10.1 %collective-permute-start.4 = (bf16[2,272,128]{2,1,0:T(8,128)(2,1)S(1)}, bf16[2,272,128]{2,1,0:T(8,128)(2,1)S(1)}, u32[]{:S(2)}, u32[]{:S(2)}) collective-permute-start(bf16[2,272,128]{2,1,0:T(8,128)(2,1)S(1)} %get-tuple-element.58), channel_id=1, source_target_pairs={{0,2},{1,3},{2,0},{3,1},{4,6},{5,7},{6,4},{7,5},{8,10},{9,11},{10,... | collective-permute-start | bytes 417800 | tf_op jit(solution)/shard_map/ppermute | solution.py:397
  37.5 13.0 %collective-permute-start.5 = (bf16[2,272,128]{2,1,0:T(8,128)(2,1)S(1)}, bf16[2,272,128]{2,1,0:T(8,128)(2,1)S(1)}, u32[]{:S(2)}, u32[]{:S(2)}) collective-permute-start(bf16[2,272,128]{2,1,0:T(8,128)(2,1)S(1)} %get-tuple-element.59), channel_id=1, source_target_pairs={{0,3},{1,2},{2,1},{3,0},{4,7},{5,6},{6,5},{7,4},{8,11},{9,10},{10,... | collective-permute-start | bytes 417800 | tf_op jit(solution)/shard_map/ppermute | solution.py:397
  38.6 23.5 %collective-permute-start.14 = (bf16[2,272,128]{2,1,0:T(8,128)(2,1)S(1)}, bf16[2,272,128]{2,1,0:T(8,128)(2,1)S(1)}, u32[]{:S(2)}, u32[]{:S(2)}) collective-permute-start(bf16[2,272,128]{2,1,0:T(8,128)(2,1)S(1)} %get-tuple-element.69), channel_id=1, source_target_pairs={{0,4},{1,5},{2,6},{3,7},{4,0},{5,1},{6,2},{7,3},{8,12},{9,13},{10,... | collective-permute-start | bytes 417800 | tf_op jit(solution)/shard_map/ppermute | solution.py:397
  42.1 20.3 %collective-permute-start.15 = (bf16[2,272,128]{2,1,0:T(8,128)(2,1)S(1)}, bf16[2,272,128]{2,1,0:T(8,128)(2,1)S(1)}, u32[]{:S(2)}, u32[]{:S(2)}) collective-permute-start(bf16[2,272,128]{2,1,0:T(8,128)(2,1)S(1)} %get-tuple-element.70), channel_id=1, source_target_pairs={{0,5},{1,4},{2,7},{3,6},{4,1},{5,0},{6,3},{7,2},{8,13},{9,12},{10,... | collective-permute-start | bytes 417800 | tf_op jit(solution)/shard_map/ppermute | solution.py:397
  44.7 22.5 %collective-permute-start.1 = (bf16[2,272,128]{2,1,0:T(8,128)(2,1)S(1)}, bf16[2,272,128]{2,1,0:T(8,128)(2,1)S(1)}, u32[]{:S(2)}, u32[]{:S(2)}) collective-permute-start(bf16[2,272,128]{2,1,0:T(8,128)(2,1)S(1)} %get-tuple-element.54), channel_id=1, source_target_pairs={{0,6},{1,7},{2,4},{3,5},{4,2},{5,3},{6,0},{7,1},{8,14},{9,15},{10,... | collective-permute-start | bytes 417800 | tf_op jit(solution)/shard_map/ppermute | solution.py:397
  50.5 16.7 %collective-permute-start.2 = (bf16[2,272,128]{2,1,0:T(8,128)(2,1)S(1)}, bf16[2,272,128]{2,1,0:T(8,128)(2,1)S(1)}, u32[]{:S(2)}, u32[]{:S(2)}) collective-permute-start(bf16[2,272,128]{2,1,0:T(8,128)(2,1)S(1)} %get-tuple-element.55), channel_id=1, source_target_pairs={{0,7},{1,6},{2,5},{3,4},{4,3},{5,2},{6,1},{7,0},{8,15},{9,14},{10,... | collective-permute-start | bytes 417800 | tf_op jit(solution)/shard_map/ppermute | solution.py:397
  72.3 4.8 %collective-permute-start.19 = (bf16[4096,128]{1,0:T(8,128)(2,1)S(1)}, bf16[4096,128]{1,0:T(8,128)(2,1)S(1)}, u32[]{:S(2)}, u32[]{:S(2)}) collective-permute-start(bf16[4096,128]{1,0:T(8,128)(2,1)S(1)} %get-tuple-element.78), channel_id=1, source_target_pairs={{0,8},{8,0},{1,9},{9,1},{2,10},{10,2},{3,11},{11,3},{4,12},{12,4},... | collective-permute-start | bytes 3145736 | tf_op jit(solution)/shard_map/ppermute | solution.py:397
  72.7 11.1 %collective-permute-start.16 = (bf16[4,256,128]{2,1,0:T(8,128)(2,1)S(1)}, bf16[4,256,128]{2,1,0:T(8,128)(2,1)S(1)}, u32[]{:S(2)}, u32[]{:S(2)}) collective-permute-start(bf16[4,256,128]{2,1,0:T(8,128)(2,1)S(1)} %get-tuple-element.73), channel_id=1, source_target_pairs={{0,6},{2,4},{4,2},{6,0},{1,7},{3,5},{5,3},{7,1},{8,14},{10,12},{12... | collective-permute-start | bytes 786440 | tf_op jit(solution)/shard_map/ppermute | solution.py:397
  76.3 25.7 %collective-permute-start.17 = (bf16[4,256,128]{2,1,0:T(8,128)(2,1)S(1)}, bf16[4,256,128]{2,1,0:T(8,128)(2,1)S(1)}, u32[]{:S(2)}, u32[]{:S(2)}) collective-permute-start(bf16[4,256,128]{2,1,0:T(8,128)(2,1)S(1)} %get-tuple-element.74), channel_id=1, source_target_pairs={{0,4},{2,6},{4,0},{6,2},{1,5},{3,7},{5,1},{7,3},{8,12},{10,14},{12... | collective-permute-start | bytes 786440 | tf_op jit(solution)/shard_map/ppermute | solution.py:397
  76.3 25.7 %collective-permute-start.18 = (bf16[4,256,128]{2,1,0:T(8,128)(2,1)S(1)}, bf16[4,256,128]{2,1,0:T(8,128)(2,1)S(1)}, u32[]{:S(2)}, u32[]{:S(2)}) collective-permute-start(bf16[4,256,128]{2,1,0:T(8,128)(2,1)S(1)} %get-tuple-element.75), channel_id=1, source_target_pairs={{0,2},{2,0},{4,6},{6,4},{1,3},{3,1},{5,7},{7,5},{8,10},{10,8},{12,... | collective-permute-start | bytes 786440 | tf_op jit(solution)/shard_map/ppermute | solution.py:397
  77.9 33.9 %collective-permute-start.20 = (bf16[512,128]{1,0:T(8,128)(2,1)S(1)}, bf16[512,128]{1,0:T(8,128)(2,1)S(1)}, u32[]{:S(2)}, u32[]{:S(2)}) collective-permute-start(bf16[512,128]{1,0:T(8,128)(2,1)S(1)} %get-tuple-element.90), channel_id=1, source_target_pairs={{0,7},{1,6},{2,5},{3,4},{4,11},{5,10},{6,9},{7,8},{8,3},{9,2},{10,... | collective-permute-start | bytes 393224 | tf_op jit(solution)/shard_map/ppermute | solution.py:423
  82.3 30.2 %collective-permute-start.21 = (bf16[512,128]{1,0:T(8,128)(2,1)S(1)}, bf16[512,128]{1,0:T(8,128)(2,1)S(1)}, u32[]{:S(2)}, u32[]{:S(2)}) collective-permute-start(bf16[512,128]{1,0:T(8,128)(2,1)S(1)} %get-tuple-element.91), channel_id=1, source_target_pairs={{0,6},{1,7},{2,4},{3,5},{4,10},{5,11},{6,8},{7,9},{8,2},{9,3},{10,... | collective-permute-start | bytes 393224 | tf_op jit(solution)/shard_map/ppermute | solution.py:423
  83.8 28.8 %collective-permute-start.22 = (bf16[512,128]{1,0:T(8,128)(2,1)S(1)}, bf16[512,128]{1,0:T(8,128)(2,1)S(1)}, u32[]{:S(2)}, u32[]{:S(2)}) collective-permute-start(bf16[512,128]{1,0:T(8,128)(2,1)S(1)} %get-tuple-element.92), channel_id=1, source_target_pairs={{0,5},{1,4},{2,7},{3,6},{4,9},{5,8},{6,11},{7,10},{8,1},{9,0},{10,... | collective-permute-start | bytes 393224 | tf_op jit(solution)/shard_map/ppermute | solution.py:423
  103.6 24.7 %all-to-all-start = ((bf16[4,4,256,128]{3,2,1,0:T(8,128)(2,1)}), bf16[4,4,256,128]{3,2,1,0:T(8,128)(2,1)S(1)}, u32[]{:S(2)}, u32[]{:S(2)}) async-start(bf16[4,4,256,128]{3,2,1,0:T(8,128)(2,1)} %join_planes.1), calls=%async_computation | async-start | bytes 2097152 | tf_op jit(solution)/shard_map/all_to_all | solution.py:462
  107.1 6.1 %collective-permute-start.23 = (bf16[512,128]{1,0:T(8,128)(2,1)S(1)}, bf16[512,128]{1,0:T(8,128)(2,1)S(1)}, u32[]{:S(2)}, u32[]{:S(2)}) collective-permute-start(bf16[512,128]{1,0:T(8,128)(2,1)S(1)} %get-tuple-element.93), channel_id=1, source_target_pairs={{0,4},{1,5},{2,6},{3,7},{4,8},{5,9},{6,10},{7,11},{8,0},{9,1},{10,... | collective-permute-start | bytes 393224 | tf_op jit(solution)/shard_map/ppermute | solution.py:423
  109.1 10.1 %collective-permute-start.24 = (bf16[512,128]{1,0:T(8,128)(2,1)S(1)}, bf16[512,128]{1,0:T(8,128)(2,1)S(1)}, u32[]{:S(2)}, u32[]{:S(2)}) collective-permute-start(bf16[512,128]{1,0:T(8,128)(2,1)S(1)} %get-tuple-element.94), channel_id=1, source_target_pairs={{0,3},{1,2},{2,1},{3,0},{4,15},{5,14},{6,13},{7,12},{8,7},{9,6},{1... | collective-permute-start | bytes 393224 | tf_op jit(solution)/shard_map/ppermute | solution.py:423
  111.8 9.4 %collective-permute-start.25 = (bf16[512,128]{1,0:T(8,128)(2,1)S(1)}, bf16[512,128]{1,0:T(8,128)(2,1)S(1)}, u32[]{:S(2)}, u32[]{:S(2)}) collective-permute-start(bf16[512,128]{1,0:T(8,128)(2,1)S(1)} %get-tuple-element.95), channel_id=1, source_target_pairs={{0,2},{1,3},{2,0},{3,1},{4,14},{5,15},{6,12},{7,13},{8,6},{9,7},{1... | collective-permute-start | bytes 393224 | tf_op jit(solution)/shard_map/ppermute | solution.py:423
  112.6 14.0 %collective-permute-start.26 = (bf16[512,128]{1,0:T(8,128)(2,1)S(1)}, bf16[512,128]{1,0:T(8,128)(2,1)S(1)}, u32[]{:S(2)}, u32[]{:S(2)}) collective-permute-start(bf16[512,128]{1,0:T(8,128)(2,1)S(1)} %get-tuple-element.96), channel_id=1, source_target_pairs={{0,1},{1,0},{2,3},{3,2},{4,13},{5,12},{6,15},{7,14},{8,5},{9,4},{1... | collective-permute-start | bytes 393224 | tf_op jit(solution)/shard_map/ppermute | solution.py:423
  112.6 14.0 %collective-permute-start.27 = (bf16[512,128]{1,0:T(8,128)(2,1)S(1)}, bf16[512,128]{1,0:T(8,128)(2,1)S(1)}, u32[]{:S(2)}, u32[]{:S(2)}) collective-permute-start(bf16[512,128]{1,0:T(8,128)(2,1)S(1)} %get-tuple-element.97), channel_id=1, source_target_pairs={{0,0},{1,1},{2,2},{3,3},{4,12},{5,13},{6,14},{7,15},{8,4},{9,5},{1... | collective-permute-start | bytes 393224 | tf_op jit(solution)/shard_map/ppermute | solution.py:423

commit v5 on v4

--- a/solution.py
+++ b/solution.py
@@ -21,6 +21,8 @@
 SPLIT_COST = 0
 UNPACK_FACT = 2
 PLANES = 4
+COUNTS = (1, 2, 3, 5, 8)
+GROUP = 4
 STACK_COST = 2
 UNPACK_COST = 5
 
@@ -79,33 +81,45 @@
     return pl.ds(pl.multiple_of((base + ((place[2] >> 1) ^ i)) * LANES, LANES), LANES)
 
 
-def pack_dimension(place, key_rows, value_rows, dims, shares):
+def pack_dimension(key_rows, value_rows, dims, shares, ys):
     rows = key_rows.shape[0] // shares
     pairs = dims // 2
 
-    def kernel(place, *refs):
-        keys, values, outs = refs[:pairs], refs[pairs : 2 * pairs], refs[2 * pairs :]
+    def kernel(keys_in, values_in, *refs):
+        outs, (keys, values, sems) = refs[:dims], refs[dims:]
+        x, share, z, y = (lax.axis_index(a) for a in ("x", "share", "z", "y"))
+        place = (x, share, z * ys + y)
         odd = (place[2] & 1) == 1
+        at = pl.ds(pl.multiple_of(place[1] * rows, rows), rows)
+
+        def copies(i):
+            span = pair_lanes(place[0] * pairs, place, i)
+            return (
+                pltpu.make_async_copy(keys_in.at[at, span], keys.at[i], sems.at[0, i]),
+                pltpu.make_async_copy(values_in.at[at, span], values.at[i], sems.at[1, i]),
+            )
+
         for i in range(pairs):
+            for copy in copies(i):
+                copy.start()
+        for i in range(pairs):
+            for copy in copies(i):
+                copy.wait()
             outs[2 * i][...], outs[2 * i + 1][...] = in_order(
-                odd, interleave(keys[i][...], values[i][...])
+                odd, interleave(keys[i], values[i])
             )
 
-    def spec(i):
-        return pl.BlockSpec((rows, LANES), lambda _, p: (p[1], p[0] * pairs + ((p[2] >> 1) ^ i)))
-
-    return pl.pallas_call(
+    anywhere = pl.BlockSpec(memory_space=pl.ANY)
+    block = pltpu.VMEM((pairs, rows, LANES), jnp.bfloat16)
+    return call(
         kernel,
-        grid_spec=pltpu.PrefetchScalarGridSpec(
-            num_scalar_prefetch=1,
-            grid=(1,),
-            in_specs=[spec(i) for i in range(pairs)] * 2,
-            out_specs=[pl.BlockSpec((rows, LANES), lambda _, p: (0, 0))] * dims,
-        ),
-        out_shape=[bf16(rows, LANES)] * dims,
-        compiler_params=pltpu.CompilerParams(vmem_limit_bytes=60 * MIB),
-        name="pack_dimension",
-    )(place, *([key_rows] * pairs), *([value_rows] * pairs))
+        "pack_dimension",
+        [bf16(rows, LANES)] * dims,
+        [anywhere, anywhere],
+        cost=0,
+        vmem=60,
+        scratch_shapes=[block, block, pltpu.SemaphoreType.DMA((2, pairs))],
+    )(key_rows, value_rows)
 
 
 def pack_fact(place, queries, cotangent, block_lists, tile_lengths, dims):
@@ -191,7 +205,7 @@
             (sums_out,) = take(1)
         (table,) = take(1) if begin else tables_in
         (sums,) = take(1) if last else (sums_out,)
-        fact, fact_out, words, meta, sem = refs
+        fact, fact_out, words, meta, order, sem = refs
         odd = place[2] & 1
         for r in range(count):
             words[r * parts : (r + 1) * parts] = (
@@ -216,28 +230,48 @@
             index = ((share ^ place[1]) * dims + (owner ^ place[2])) * owner_blocks + at
             return pl.multiple_of(index * TILE, TILE)
 
-        def step(source, lengths, count):
-            left, places, kept, pairs = [], [], [], []
-            for tile in range(tiles_each):
-                both = fact[source, tile * TILE : (tile + 1) * TILE, :]
+        tiles = sources * tiles_each
+        lengths = [meta[t // tiles_each, t % tiles_each, slots] for t in range(tiles)]
+        ranks = [jnp.int32(0)] * tiles
+        for t in range(tiles):
+            for u in range(t):
+                ahead = (lengths[u] >= lengths[t]).astype(jnp.int32)
+                ranks[t] += ahead
+                ranks[u] += 1 - ahead
+        for t in range(tiles):
+            order[ranks[t]] = t
+
+        def step(index, longest):
+            chosen = [order[index * GROUP + g] for g in range(GROUP)]
+            spots = [(t // tiles_each, pl.multiple_of(t % tiles_each * TILE, TILE)) for t in chosen]
+            left, places, live, pairs = [], [], [], []
+            for t, (source, start) in zip(chosen, spots):
+                both = fact[source, pl.ds(start, TILE), :]
                 zero = jnp.zeros_like(both)
                 left.append(
                     jnp.concatenate(
                         [jnp.where(first, both, zero), jnp.where(first, zero, both)], axis=0
                     )
                 )
-                places.append([row_of(meta[source, tile, j]) for j in range(count)])
-            for tile in range(tiles_each):
-                kv = jnp.concatenate([table[pl.ds(at, TILE), :] for at in places[tile]], axis=0)
+                tile = t % tiles_each
+                places.append([row_of(meta[source, tile, j]) for j in range(longest)])
+                live.append(meta[source, tile, slots])
+            kept = []
+            for g in range(GROUP):
+                kv = jnp.concatenate([table[pl.ds(at, TILE), :] for at in places[g]], axis=0)
                 products = lax.dot_general(
-                    kv, left[tile], (((1,), (1,)), ((), ())), preferred_element_type=jnp.float32
+                    kv, left[g], (((1,), (1,)), ((), ())), preferred_element_type=jnp.float32
                 )
                 scores = products[:, :TILE] * (SCALE * LOG2E)
-                live = [scores[:TILE]] + [
-                    jnp.where(lengths[tile] > j, scores[j * TILE : (j + 1) * TILE], NEG_FILL)
-                    for j in range(1, count)
-                ]
-                scores = jnp.concatenate(live, axis=0)
+                if longest > 1:
+                    scores = jnp.concatenate(
+                        [scores[:TILE]]
+                        + [
+                            jnp.where(live[g] > j, scores[j * TILE : (j + 1) * TILE], NEG_FILL)
+                            for j in range(1, longest)
+                        ],
+                        axis=0,
+                    )
                 dweights = products[:, TILE:]
                 terms = jnp.exp2(scores - jnp.max(scores, axis=0, keepdims=True))
                 weights = terms * (1.0 / jnp.sum(terms, axis=0, keepdims=True))
@@ -249,28 +283,27 @@
                         [dscores.astype(jnp.bfloat16), weights.astype(jnp.bfloat16)], axis=1
                     )
                 )
-            for tile in range(tiles_each):
+            for g, (source, start) in enumerate(spots):
                 out = lax.dot_general(
-                    pairs[tile],
-                    kept[tile],
-                    (((0,), (0,)), ((), ())),
-                    preferred_element_type=jnp.float32,
+                    pairs[g], kept[g], (((0,), (0,)), ((), ())), preferred_element_type=jnp.float32
                 )
-                fact_out[source, tile * TILE : (tile + 1) * TILE, :] = jnp.where(
+                fact_out[source, pl.ds(start, TILE), :] = jnp.where(
                     first, out[:TILE] * SCALE, out[TILE:]
                 ).astype(jnp.bfloat16)
-                grads = jnp.dot(pairs[tile], left[tile], preferred_element_type=jnp.float32)
-                for j, at in enumerate(places[tile]):
+                grads = jnp.dot(pairs[g], left[g], preferred_element_type=jnp.float32)
+                for j, at in enumerate(places[g]):
                     sums[pl.ds(at, TILE), :] += grads[j * TILE : (j + 1) * TILE]
 
-        def source_step(source, carry):
-            lengths = [meta[source, tile, slots] for tile in range(tiles_each)]
-            longest = functools.reduce(jnp.maximum, lengths)
-            for count in range(1, slots + 1):
-                pl.when(longest == count)(functools.partial(step, source, lengths, count))
+        def group_step(index, carry):
+            first_tile = order[index * GROUP]
+            longest = meta[first_tile // tiles_each, first_tile % tiles_each, slots]
+            for below, length in zip((0,) + COUNTS, COUNTS):
+                pl.when((longest > below) & (longest <= length))(
+                    functools.partial(step, index, length)
+                )
             return carry
 
-        lax.fori_loop(0, sources, source_step, 0)
+        lax.fori_loop(0, tiles // GROUP, group_step, 0)
         for r in range(count):
             for i in range(parts):
                 fact_outs[r // ys][i * ys + r % ys] = fact_out[r * parts + i]
@@ -311,6 +344,7 @@
             pltpu.VMEM((sources, rows, LANES), jnp.bfloat16),
             pltpu.VMEM((sources, META_ROWS, LANES), jnp.int32),
             pltpu.SMEM((sources, META_ROWS, LANES), jnp.int32),
+            pltpu.SMEM((sources * tiles_each,), jnp.int32),
             pltpu.SemaphoreType.DMA,
         ],
     )(place, *facts, *tables, *sums_in)
@@ -422,7 +456,7 @@
         ]
         return lax.ppermute(chunk, ("share", "z", "y"), pairs)
 
-    chunks = pack_dimension(place, key_rows, value_rows, dims, shares)
+    chunks = pack_dimension(key_rows, value_rows, dims, shares, ys)
     chunks = exchange(chunks, over_dim)
     table = stack_chunks(chunks, STACK_COST)
     tables = [by_xor(table, "share", k, shares) for k in range(shares)]

time: 129 us -> 127 us (0.984); the launches traced: 129 us -> 126 us
  Pallas kernels: 29.7 us -> 28.4 us
  waiting for transfers between devices: 36.9 us -> 35.6 us
    ppermute x8, waiting for transfers between devices: 13.3 us -> 9.36 us  [to_columns(): return lax.ppermute(chunk, ('share', 'z', 'y'), pairs)]
    ppermute x20, waiting for transfers between devices: 23.6 us -> 26.3 us  [by_xor(): return lax.ppermute(part, axis, [(i, i ^ index) for i in range(count)])]
    ppermute x8, starting transfers between devices: 22.3 us -> 20 us  [to_columns(): return lax.ppermute(chunk, ('share', 'z', 'y'), pairs)]
    all_to_all x1, starting transfers between devices: 3.51 us -> 5.71 us  [body(): lax.all_to_all(fact_out, ('x', 'y'), split_axis=0, concat_axis=0, tiled=T...]
  transfers between devices with their start and end apart: 29 -> 29, of which waited for: 10 -> 10; matrix products, arithmetic and copies ran while one was open for 0% -> 0% of each run, Pallas kernels for 16% -> 15%
where the time goes in v5:
time: 127 us; the launch traced here: 126 us
  starting transfers between devices  60.8 us (48%)
  waiting for transfers between devices  35.6 us (28%)
  Pallas kernels  28.4 us (22%)
    ppermute x20, starting transfers between devices, by_xor(): return lax.ppermute(part, axis, [(i, i ^ index) for i in range(count)])  35.1 us
    ppermute x20, waiting for transfers between devices, by_xor(): return lax.ppermute(part, axis, [(i, i ^ index) for i in range(count)])  26.3 us
    ppermute x8, starting transfers between devices, to_columns(): return lax.ppermute(chunk, ('share', 'z', 'y'), pairs)  20 us
    pallas_call x3, Pallas kernels, attend(): call(kernel, 'attend', outs, [SMEM] + [VMEM] * (count + len(tables) + len...  19.7 us
    ppermute x8, waiting for transfers between devices, to_columns(): return lax.ppermute(chunk, ('share', 'z', 'y'), pairs)  9.36 us
    all_to_all x1, starting transfers between devices, body(): lax.all_to_all(fact_out, ('x', 'y'), split_axis=0, concat_axis=0, tiled=T...  5.71 us
  transfers between devices with their start and end apart: 29, of which 10 were waited for; matrix products, arithmetic and copies ran while one was open for 0% of the time, Pallas kernels for 15%

profile of v5, /device:TPU:0, one launch (start us, length us, event | category | flops | bytes accessed | tf_op | source)
XLA Modules:
  0.0 125.9 jit_solution(17929858355733998309)
XLA Ops:
  0.7 2.5 %pack_dimension.1 = (bf16[512,128]{1,0:T(8,128)(2,1)}, bf16[512,128]{1,0:T(8,128)(2,1)}, bf16[512,128]{1,0:T(8,128)(2,1)}, bf16[512,128]{1,0:T(8,128)(2,1)}, bf1...) custom-call(bf16[1024,1024]{1,0:T(8,128)(2,1)} %keys_in.1, ...), custom_call_target="tpu_custom_call" | custom-call | tf_op jit(solution)/shard_map/pack_dimension/pallas_call | solution.py:114
  3.2 3.0 %collective-permute-start.6 = (bf16[512,128]{1,0:T(8,128)(2,1)}, bf16[512,128]{1,0:T(8,128)(2,1)S(1)}, u32[]{:S(2)}, u32[]{:S(2)}) collective-permute-start(bf16[512,128]{1,0:T(8,128)(2,1)} %get-tuple-element.61), channel_id=1, source_target_pairs={{0,1},{1,0},{2,3},{3,2},{4,5},{5,4},{6,7},{7,6},{8,9},{9,8},{10,11... | collective-permute-start | bytes 393224 | tf_op jit(solution)/shard_map/ppermute | solution.py:431
  6.2 1.6 %collective-permute-start.7 = (bf16[512,128]{1,0:T(8,128)(2,1)}, bf16[512,128]{1,0:T(8,128)(2,1)S(1)}, u32[]{:S(2)}, u32[]{:S(2)}) collective-permute-start(bf16[512,128]{1,0:T(8,128)(2,1)} %get-tuple-element.62), channel_id=1, source_target_pairs={{0,2},{1,3},{2,0},{3,1},{4,6},{5,7},{6,4},{7,5},{8,10},{9,11},{10,... | collective-permute-start | bytes 393224 | tf_op jit(solution)/shard_map/ppermute | solution.py:431
  7.8 3.0 %collective-permute-start.9 = (bf16[512,128]{1,0:T(8,128)(2,1)}, bf16[512,128]{1,0:T(8,128)(2,1)S(1)}, u32[]{:S(2)}, u32[]{:S(2)}) collective-permute-start(bf16[512,128]{1,0:T(8,128)(2,1)} %get-tuple-element.64), channel_id=1, source_target_pairs={{0,4},{1,5},{2,6},{3,7},{4,0},{5,1},{6,2},{7,3},{8,12},{9,13},{10,... | collective-permute-start | bytes 393224 | tf_op jit(solution)/shard_map/ppermute | solution.py:431
  10.8 1.3 %collective-permute-start.10 = (bf16[512,128]{1,0:T(8,128)(2,1)}, bf16[512,128]{1,0:T(8,128)(2,1)S(1)}, u32[]{:S(2)}, u32[]{:S(2)}) collective-permute-start(bf16[512,128]{1,0:T(8,128)(2,1)} %get-tuple-element.65), channel_id=1, source_target_pairs={{0,5},{1,4},{2,7},{3,6},{4,1},{5,0},{6,3},{7,2},{8,13},{9,12},{10,... | collective-permute-start | bytes 393224 | tf_op jit(solution)/shard_map/ppermute | solution.py:431
  12.1 3.6 %collective-permute-start.11 = (bf16[512,128]{1,0:T(8,128)(2,1)}, bf16[512,128]{1,0:T(8,128)(2,1)S(1)}, u32[]{:S(2)}, u32[]{:S(2)}) collective-permute-start(bf16[512,128]{1,0:T(8,128)(2,1)} %get-tuple-element.66), channel_id=1, source_target_pairs={{0,6},{1,7},{2,4},{3,5},{4,2},{5,3},{6,0},{7,1},{8,14},{9,15},{10,... | collective-permute-start | bytes 393224 | tf_op jit(solution)/shard_map/ppermute | solution.py:431
  15.7 1.5 %collective-permute-done.7.refs_2_ = bf16[512,128]{1,0:T(8,128)(2,1)S(1)} collective-permute-done((bf16[512,128]{1,0:T(8,128)(2,1)}, bf16[512,128]{1,0:T(8,128)(2,1)S(1)}, u32[]{:S(2)}, u32[]{:S(2)}) %collective-permute-start.7) | collective-permute-done | bytes 131104 | tf_op jit(solution)/shard_map/ppermute | solution.py:431
  17.2 0.7 collective-permute-start.12
  17.8 0.1 copy.10.tile_lengths
  17.9 0.1 stack.23.place
  18.0 1.0 pack_fact.1
  19.0 1.6 %collective-permute-start = (bf16[8,272,128]{2,1,0:T(8,128)(2,1)S(1)}, bf16[8,272,128]{2,1,0:T(8,128)(2,1)S(1)}, u32[]{:S(2)}, u32[]{:S(2)}) collective-permute-start(bf16[8,272,128]{2,1,0:T(8,128)(2,1)S(1)} %get-tuple-element.53), channel_id=1, source_target_pairs={{0,16},{16,0},{1,17},{17,1},{2,18},{18,2},{3,19},{19,3},{4,20},{20... | collective-permute-start | bytes 1671176 | tf_op jit(solution)/shard_map/ppermute | solution.py:431
  20.6 9.9 %collective-permute-done.10.refs_5_ = bf16[512,128]{1,0:T(8,128)(2,1)S(1)} collective-permute-done((bf16[512,128]{1,0:T(8,128)(2,1)}, bf16[512,128]{1,0:T(8,128)(2,1)S(1)}, u32[]{:S(2)}, u32[]{:S(2)}) %collective-permute-start.10) | collective-permute-done | bytes 131104 | tf_op jit(solution)/shard_map/ppermute | solution.py:431
  30.5 0.1 stack_chunks.1.refs_4_
  30.5 0.1 collective-permute-start.13
  30.6 0.8 collective-permute-done.refs_1_
  31.4 0.1 merge_fact.1
  31.5 1.8 %collective-permute-start.3 = (bf16[2,272,128]{2,1,0:T(8,128)(2,1)S(1)}, bf16[2,272,128]{2,1,0:T(8,128)(2,1)S(1)}, u32[]{:S(2)}, u32[]{:S(2)}) collective-permute-start(bf16[2,272,128]{2,1,0:T(8,128)(2,1)S(1)} %get-tuple-element.57), channel_id=1, source_target_pairs={{0,1},{1,0},{2,3},{3,2},{4,5},{5,4},{6,7},{7,6},{8,9},{9,8},{10,11... | collective-permute-start | bytes 417800 | tf_op jit(solution)/shard_map/ppermute | solution.py:431
  33.3 2.8 %collective-permute-start.4 = (bf16[2,272,128]{2,1,0:T(8,128)(2,1)S(1)}, bf16[2,272,128]{2,1,0:T(8,128)(2,1)S(1)}, u32[]{:S(2)}, u32[]{:S(2)}) collective-permute-start(bf16[2,272,128]{2,1,0:T(8,128)(2,1)S(1)} %get-tuple-element.58), channel_id=1, source_target_pairs={{0,2},{1,3},{2,0},{3,1},{4,6},{5,7},{6,4},{7,5},{8,10},{9,11},{10,... | collective-permute-start | bytes 417800 | tf_op jit(solution)/shard_map/ppermute | solution.py:431
  36.2 1.1 collective-permute-start.5
  37.3 3.5 %collective-permute-start.14 = (bf16[2,272,128]{2,1,0:T(8,128)(2,1)S(1)}, bf16[2,272,128]{2,1,0:T(8,128)(2,1)S(1)}, u32[]{:S(2)}, u32[]{:S(2)}) collective-permute-start(bf16[2,272,128]{2,1,0:T(8,128)(2,1)S(1)} %get-tuple-element.69), channel_id=1, source_target_pairs={{0,4},{1,5},{2,6},{3,7},{4,0},{5,1},{6,2},{7,3},{8,12},{9,13},{10,... | collective-permute-start | bytes 417800 | tf_op jit(solution)/shard_map/ppermute | solution.py:431
  40.8 2.6 %collective-permute-start.15 = (bf16[2,272,128]{2,1,0:T(8,128)(2,1)S(1)}, bf16[2,272,128]{2,1,0:T(8,128)(2,1)S(1)}, u32[]{:S(2)}, u32[]{:S(2)}) collective-permute-start(bf16[2,272,128]{2,1,0:T(8,128)(2,1)S(1)} %get-tuple-element.70), channel_id=1, source_target_pairs={{0,5},{1,4},{2,7},{3,6},{4,1},{5,0},{6,3},{7,2},{8,13},{9,12},{10,... | collective-permute-start | bytes 417800 | tf_op jit(solution)/shard_map/ppermute | solution.py:431
  43.4 2.8 %collective-permute-start.1 = (bf16[2,272,128]{2,1,0:T(8,128)(2,1)S(1)}, bf16[2,272,128]{2,1,0:T(8,128)(2,1)S(1)}, u32[]{:S(2)}, u32[]{:S(2)}) collective-permute-start(bf16[2,272,128]{2,1,0:T(8,128)(2,1)S(1)} %get-tuple-element.54), channel_id=1, source_target_pairs={{0,6},{1,7},{2,4},{3,5},{4,2},{5,3},{6,0},{7,1},{8,14},{9,15},{10,... | collective-permute-start | bytes 417800 | tf_op jit(solution)/shard_map/ppermute | solution.py:431
  46.1 3.0 %collective-permute-done.5.refs_3_ = bf16[2,272,128]{2,1,0:T(8,128)(2,1)S(1)} collective-permute-done((bf16[2,272,128]{2,1,0:T(8,128)(2,1)S(1)}, bf16[2,272,128]{2,1,0:T(8,128)(2,1)S(1)}, u32[]{:S(2)}, u32[]{:S(2)}) %collective-permute-start.5) | collective-permute-done | bytes 139296 | tf_op jit(solution)/shard_map/ppermute | solution.py:431
  49.2 1.2 collective-permute-start.2
  50.4 7.9 %attend.3 = (bf16[4,256,128]{2,1,0:T(8,128)(2,1)S(1)}, bf16[4,256,128]{2,1,0:T(8,128)(2,1)S(1)}, f32[8192,128]{1,0:T(8,128)S(1)}, bf16[8192,128]{1,0:T(8,128)(2,1)S(1)}) custom-call(s32[5]{0:T(128)S(1)} %stack.23.place, bf16[2,272,128]{2,1,0:T(8,128)(2,1)S(1)} %get-tuple-element.56.refs_0_, bf16[2,272,128]{2,1,0:T(8,128)(2,1)S(1)} %collective-permute-done.3.refs_1_, ...), custom_call_target="tpu_custom_call" | custom-call | tf_op jit(solution)/shard_map/attend/pallas_call | solution.py:334
  58.3 2.9 %collective-permute-done.15.refs_1_ = bf16[2,272,128]{2,1,0:T(8,128)(2,1)S(1)} collective-permute-done((bf16[2,272,128]{2,1,0:T(8,128)(2,1)S(1)}, bf16[2,272,128]{2,1,0:T(8,128)(2,1)S(1)}, u32[]{:S(2)}, u32[]{:S(2)}) %collective-permute-start.15) | collective-permute-done | bytes 139296 | tf_op jit(solution)/shard_map/ppermute | solution.py:431
  61.2 5.8 %attend.4 = (bf16[4,256,128]{2,1,0:T(8,128)(2,1)S(1)}, f32[8192,128]{1,0:T(8,128)S(1)}) custom-call(s32[5]{0:T(128)S(1)} %stack.23.place, bf16[2,272,128]{2,1,0:T(8,128)(2,1)S(1)} %collective-permute-done.14.refs_0_, bf16[2,272,128]{2,1,0:T(8,128)(2,1)S(1)} %collective-permute-done.15.refs_1_, bf16[8192,128]{1,0:T(8,128)(2,1)S(1)} %get-tuple-element.68.refs_2_, ...), custom_call_target="tpu_custom_call" | custom-call | tf_op jit(solution)/shard_map/attend/pallas_call | solution.py:334
  67.0 6.0 %attend.5 = (bf16[4,256,128]{2,1,0:T(8,128)(2,1)S(1)}, f32[4096,128]{1,0:T(8,128)S(1)}, bf16[4096,128]{1,0:T(8,128)(2,1)S(1)}) custom-call(s32[5]{0:T(128)S(1)} %stack.23.place, bf16[2,272,128]{2,1,0:T(8,128)(2,1)S(1)} %collective-permute-done.1.refs_0_, bf16[2,272,128]{2,1,0:T(8,128)(2,1)S(1)} %collective-permute-done.2.refs_1_, ...), custom_call_target="tpu_custom_call" | custom-call | flops 69000003584 | tf_op jit(solution)/shard_map/attend/pallas_call | solution.py:334
  73.1 0.5 collective-permute-start.17
  73.6 3.9 %collective-permute-start.18 = (bf16[4,256,128]{2,1,0:T(8,128)(2,1)S(1)}, bf16[4,256,128]{2,1,0:T(8,128)(2,1)S(1)}, u32[]{:S(2)}, u32[]{:S(2)}) collective-permute-start(bf16[4,256,128]{2,1,0:T(8,128)(2,1)S(1)} %get-tuple-element.75), channel_id=1, source_target_pairs={{0,2},{2,0},{4,6},{6,4},{1,3},{3,1},{5,7},{7,5},{8,10},{10,8},{12,... | collective-permute-start | bytes 786440 | tf_op jit(solution)/shard_map/ppermute | solution.py:431
  77.5 0.7 sum_shares.1
  78.2 0.7 collective-permute-start.20
  78.9 2.4 %collective-permute-start.21 = (bf16[512,128]{1,0:T(8,128)(2,1)S(1)}, bf16[512,128]{1,0:T(8,128)(2,1)S(1)}, u32[]{:S(2)}, u32[]{:S(2)}) collective-permute-start(bf16[512,128]{1,0:T(8,128)(2,1)S(1)} %get-tuple-element.91), channel_id=1, source_target_pairs={{0,6},{1,7},{2,4},{3,5},{4,10},{5,11},{6,8},{7,9},{8,2},{9,3},{10,... | collective-permute-start | bytes 393224 | tf_op jit(solution)/shard_map/ppermute | solution.py:457
  81.3 2.9 %collective-permute-done.16.refs_0_ = bf16[4,256,128]{2,1,0:T(8,128)(2,1)S(1)} collective-permute-done((bf16[4,256,128]{2,1,0:T(8,128)(2,1)S(1)}, bf16[4,256,128]{2,1,0:T(8,128)(2,1)S(1)}, u32[]{:S(2)}, u32[]{:S(2)}) %collective-permute-start.16) | collective-permute-done | bytes 262176 | tf_op jit(solution)/shard_map/ppermute | solution.py:431
  84.1 9.6 %collective-permute-start.22 = (bf16[512,128]{1,0:T(8,128)(2,1)S(1)}, bf16[512,128]{1,0:T(8,128)(2,1)S(1)}, u32[]{:S(2)}, u32[]{:S(2)}) collective-permute-start(bf16[512,128]{1,0:T(8,128)(2,1)S(1)} %get-tuple-element.92), channel_id=1, source_target_pairs={{0,5},{1,4},{2,7},{3,6},{4,9},{5,8},{6,11},{7,10},{8,1},{9,0},{10,... | collective-permute-start | bytes 393224 | tf_op jit(solution)/shard_map/ppermute | solution.py:457
  93.8 5.3 %collective-permute-done.17.refs_1_ = bf16[4,256,128]{2,1,0:T(8,128)(2,1)S(1)} collective-permute-done((bf16[4,256,128]{2,1,0:T(8,128)(2,1)S(1)}, bf16[4,256,128]{2,1,0:T(8,128)(2,1)S(1)}, u32[]{:S(2)}, u32[]{:S(2)}) %collective-permute-start.17) | collective-permute-done | bytes 262176 | tf_op jit(solution)/shard_map/ppermute | solution.py:431
  99.0 1.6 %join_planes.1 = bf16[4,4,256,128]{3,2,1,0:T(8,128)(2,1)} custom-call(s32[5]{0:T(128)S(1)} %stack.23.place, bf16[4,256,128]{2,1,0:T(8,128)(2,1)S(1)} %collective-permute-done.16.refs_0_, bf16[4,256,128]{2,1,0:T(8,128)(2,1)S(1)} %collective-permute-done.17.refs_1_, bf16[4,256,128]{2,1,0:T(8,128)(2,1)S(1)} %collective-permute-done.18.refs_2_, ...), custom_call_target="tpu_custom_call" | custom-call | tf_op jit(solution)/shard_map/join_planes/pallas_call | solution.py:365
  100.7 5.7 %all-to-all-start = ((bf16[4,4,256,128]{3,2,1,0:T(8,128)(2,1)}), bf16[4,4,256,128]{3,2,1,0:T(8,128)(2,1)S(1)}, u32[]{:S(2)}, u32[]{:S(2)}) async-start(bf16[4,4,256,128]{3,2,1,0:T(8,128)(2,1)} %join_planes.1), calls=%async_computation | async-start | bytes 2097152 | tf_op jit(solution)/shard_map/all_to_all | solution.py:496
  106.4 1.9 %collective-permute-start.23 = (bf16[512,128]{1,0:T(8,128)(2,1)S(1)}, bf16[512,128]{1,0:T(8,128)(2,1)S(1)}, u32[]{:S(2)}, u32[]{:S(2)}) collective-permute-start(bf16[512,128]{1,0:T(8,128)(2,1)S(1)} %get-tuple-element.93), channel_id=1, source_target_pairs={{0,4},{1,5},{2,6},{3,7},{4,8},{5,9},{6,10},{7,11},{8,0},{9,1},{10,... | collective-permute-start | bytes 393224 | tf_op jit(solution)/shard_map/ppermute | solution.py:457
  108.3 4.1 %collective-permute-start.24 = (bf16[512,128]{1,0:T(8,128)(2,1)S(1)}, bf16[512,128]{1,0:T(8,128)(2,1)S(1)}, u32[]{:S(2)}, u32[]{:S(2)}) collective-permute-start(bf16[512,128]{1,0:T(8,128)(2,1)S(1)} %get-tuple-element.94), channel_id=1, source_target_pairs={{0,3},{1,2},{2,1},{3,0},{4,15},{5,14},{6,13},{7,12},{8,7},{9,6},{1... | collective-permute-start | bytes 393224 | tf_op jit(solution)/shard_map/ppermute | solution.py:457
  112.4 0.6 collective-permute-start.26
  113.0 0.7 collective-permute-start.27
  113.7 6.2 %collective-permute-done.24.refs_4_ = bf16[512,128]{1,0:T(8,128)(2,1)S(1)} collective-permute-done((bf16[512,128]{1,0:T(8,128)(2,1)S(1)}, bf16[512,128]{1,0:T(8,128)(2,1)S(1)}, u32[]{:S(2)}, u32[]{:S(2)}) %collective-permute-start.24) | collective-permute-done | bytes 131104 | tf_op jit(solution)/shard_map/ppermute | solution.py:457
  119.9 0.9 collective-permute-done.25.refs_5_
  120.8 2.3 %collective-permute-done.26.refs_6_ = bf16[512,128]{1,0:T(8,128)(2,1)S(1)} collective-permute-done((bf16[512,128]{1,0:T(8,128)(2,1)S(1)}, bf16[512,128]{1,0:T(8,128)(2,1)S(1)}, u32[]{:S(2)}, u32[]{:S(2)}) %collective-permute-start.26) | collective-permute-done | bytes 131104 | tf_op jit(solution)/shard_map/ppermute | solution.py:457
  123.1 1.7 %unpack_dimension.1 = (bf16[1024,256]{1,0:T(8,128)(2,1)}, bf16[1024,256]{1,0:T(8,128)(2,1)}) custom-call(s32[5]{0:T(128)S(1)} %stack.23.place, bf16[512,128]{1,0:T(8,128)(2,1)S(1)} %collective-permute-done.20.refs_0_, bf16[512,128]{1,0:T(8,128)(2,1)S(1)} %collective-permute-done.21.refs_1_, bf16[512,128]{1,0:T(8,128)(2,1)S(1)} %collective-permute-done.22.refs_2_, ...), custom_call_target="tpu_custom_call" | custom-call | flops 5750000128 | tf_op jit(solution)/shard_map/unpack_dimension/pallas_call | solution.py:419
  124.8 1.1 unpack_fact.1
  (33 shorter events, 0.2 us)
Async XLA Ops:
  0.6 17.2 %copy-start.4 = (s32[2]{0:T(128)S(1)}, s32[2]{0:T(128)}, u32[]{:S(2)}) copy-start(s32[2]{0:T(128)} %param.11) | copy-start | bytes 28
  0.6 17.4 %copy-start.3 = (s32[2,8]{1,0:T(2,128)S(1)}, s32[2,8]{1,0:T(2,128)}, u32[]{:S(2)}) copy-start(s32[2,8]{1,0:T(2,128)} %block_lists.1) | copy-start | bytes 196
  0.7 17.4 %copy-start.1 = (bf16[256,1024]{1,0:T(8,128)(2,1)S(1)}, bf16[256,1024]{1,0:T(8,128)(2,1)}, u32[]{:S(2)}) copy-start(bf16[256,1024]{1,0:T(8,128)(2,1)} %cotangent.1) | copy-start | bytes 1572868
  0.7 17.4 %copy-start = (bf16[256,1024]{1,0:T(8,128)(2,1)S(1)}, bf16[256,1024]{1,0:T(8,128)(2,1)}, u32[]{:S(2)}) copy-start(bf16[256,1024]{1,0:T(8,128)(2,1)} %queries.1) | copy-start | bytes 1572868
  3.2 8.9 %collective-permute-start.6 = (bf16[512,128]{1,0:T(8,128)(2,1)}, bf16[512,128]{1,0:T(8,128)(2,1)S(1)}, u32[]{:S(2)}, u32[]{:S(2)}) collective-permute-start(bf16[512,128]{1,0:T(8,128)(2,1)} %get-tuple-element.61), channel_id=1, source_target_pairs={{0,1},{1,0},{2,3},{3,2},{4,5},{5,4},{6,7},{7,6},{8,9},{9,8},{10,11... | collective-permute-start | bytes 393224 | tf_op jit(solution)/shard_map/ppermute | solution.py:431
  6.2 10.9 %collective-permute-start.7 = (bf16[512,128]{1,0:T(8,128)(2,1)}, bf16[512,128]{1,0:T(8,128)(2,1)S(1)}, u32[]{:S(2)}, u32[]{:S(2)}) collective-permute-start(bf16[512,128]{1,0:T(8,128)(2,1)} %get-tuple-element.62), channel_id=1, source_target_pairs={{0,2},{1,3},{2,0},{3,1},{4,6},{5,7},{6,4},{7,5},{8,10},{9,11},{10,... | collective-permute-start | bytes 393224 | tf_op jit(solution)/shard_map/ppermute | solution.py:431
  7.8 11.2 %collective-permute-start.8 = (bf16[512,128]{1,0:T(8,128)(2,1)}, bf16[512,128]{1,0:T(8,128)(2,1)S(1)}, u32[]{:S(2)}, u32[]{:S(2)}) collective-permute-start(bf16[512,128]{1,0:T(8,128)(2,1)} %get-tuple-element.63), channel_id=1, source_target_pairs={{0,3},{1,2},{2,1},{3,0},{4,7},{5,6},{6,5},{7,4},{8,11},{9,10},{10,... | collective-permute-start | bytes 393224 | tf_op jit(solution)/shard_map/ppermute | solution.py:431
  7.8 12.8 %collective-permute-start.9 = (bf16[512,128]{1,0:T(8,128)(2,1)}, bf16[512,128]{1,0:T(8,128)(2,1)S(1)}, u32[]{:S(2)}, u32[]{:S(2)}) collective-permute-start(bf16[512,128]{1,0:T(8,128)(2,1)} %get-tuple-element.64), channel_id=1, source_target_pairs={{0,4},{1,5},{2,6},{3,7},{4,0},{5,1},{6,2},{7,3},{8,12},{9,13},{10,... | collective-permute-start | bytes 393224 | tf_op jit(solution)/shard_map/ppermute | solution.py:431
  10.8 19.7 %collective-permute-start.10 = (bf16[512,128]{1,0:T(8,128)(2,1)}, bf16[512,128]{1,0:T(8,128)(2,1)S(1)}, u32[]{:S(2)}, u32[]{:S(2)}) collective-permute-start(bf16[512,128]{1,0:T(8,128)(2,1)} %get-tuple-element.65), channel_id=1, source_target_pairs={{0,5},{1,4},{2,7},{3,6},{4,1},{5,0},{6,3},{7,2},{8,13},{9,12},{10,... | collective-permute-start | bytes 393224 | tf_op jit(solution)/shard_map/ppermute | solution.py:431
  12.1 18.4 %collective-permute-start.11 = (bf16[512,128]{1,0:T(8,128)(2,1)}, bf16[512,128]{1,0:T(8,128)(2,1)S(1)}, u32[]{:S(2)}, u32[]{:S(2)}) collective-permute-start(bf16[512,128]{1,0:T(8,128)(2,1)} %get-tuple-element.66), channel_id=1, source_target_pairs={{0,6},{1,7},{2,4},{3,5},{4,2},{5,3},{6,0},{7,1},{8,14},{9,15},{10,... | collective-permute-start | bytes 393224 | tf_op jit(solution)/shard_map/ppermute | solution.py:431
  17.2 13.3 %collective-permute-start.12 = (bf16[512,128]{1,0:T(8,128)(2,1)}, bf16[512,128]{1,0:T(8,128)(2,1)S(1)}, u32[]{:S(2)}, u32[]{:S(2)}) collective-permute-start(bf16[512,128]{1,0:T(8,128)(2,1)} %get-tuple-element.67), channel_id=1, source_target_pairs={{0,7},{1,6},{2,5},{3,4},{4,3},{5,2},{6,1},{7,0},{8,15},{9,14},{10,... | collective-permute-start | bytes 393224 | tf_op jit(solution)/shard_map/ppermute | solution.py:431
  18.0 12.4 %copy-start.2 = (bf16[512,128]{1,0:T(8,128)(2,1)S(1)}, bf16[512,128]{1,0:T(8,128)(2,1)}, u32[]{:S(2)}) copy-start(bf16[512,128]{1,0:T(8,128)(2,1)} %get-tuple-element.60.refs_0_) | copy-start | bytes 393220
  19.0 12.4 %collective-permute-start = (bf16[8,272,128]{2,1,0:T(8,128)(2,1)S(1)}, bf16[8,272,128]{2,1,0:T(8,128)(2,1)S(1)}, u32[]{:S(2)}, u32[]{:S(2)}) collective-permute-start(bf16[8,272,128]{2,1,0:T(8,128)(2,1)S(1)} %get-tuple-element.53), channel_id=1, source_target_pairs={{0,16},{16,0},{1,17},{17,1},{2,18},{18,2},{3,19},{19,3},{4,20},{20... | collective-permute-start | bytes 1671176 | tf_op jit(solution)/shard_map/ppermute | solution.py:431
  30.5 19.9 %collective-permute-start.13 = (bf16[4096,128]{1,0:T(8,128)(2,1)S(1)}, bf16[4096,128]{1,0:T(8,128)(2,1)S(1)}, u32[]{:S(2)}, u32[]{:S(2)}) collective-permute-start(bf16[4096,128]{1,0:T(8,128)(2,1)S(1)} %stack_chunks.1.refs_4_), channel_id=1, source_target_pairs={{0,8},{8,0},{1,9},{9,1},{2,10},{10,2},{3,11},{11,3},{4,12},{12,4},... | collective-permute-start | bytes 3145736 | tf_op jit(solution)/shard_map/ppermute | solution.py:431
  31.5 9.3 %collective-permute-start.3 = (bf16[2,272,128]{2,1,0:T(8,128)(2,1)S(1)}, bf16[2,272,128]{2,1,0:T(8,128)(2,1)S(1)}, u32[]{:S(2)}, u32[]{:S(2)}) collective-permute-start(bf16[2,272,128]{2,1,0:T(8,128)(2,1)S(1)} %get-tuple-element.57), channel_id=1, source_target_pairs={{0,1},{1,0},{2,3},{3,2},{4,5},{5,4},{6,7},{7,6},{8,9},{9,8},{10,11... | collective-permute-start | bytes 417800 | tf_op jit(solution)/shard_map/ppermute | solution.py:431
  33.3 10.1 %collective-permute-start.4 = (bf16[2,272,128]{2,1,0:T(8,128)(2,1)S(1)}, bf16[2,272,128]{2,1,0:T(8,128)(2,1)S(1)}, u32[]{:S(2)}, u32[]{:S(2)}) collective-permute-start(bf16[2,272,128]{2,1,0:T(8,128)(2,1)S(1)} %get-tuple-element.58), channel_id=1, source_target_pairs={{0,2},{1,3},{2,0},{3,1},{4,6},{5,7},{6,4},{7,5},{8,10},{9,11},{10,... | collective-permute-start | bytes 417800 | tf_op jit(solution)/shard_map/ppermute | solution.py:431
  36.2 13.0 %collective-permute-start.5 = (bf16[2,272,128]{2,1,0:T(8,128)(2,1)S(1)}, bf16[2,272,128]{2,1,0:T(8,128)(2,1)S(1)}, u32[]{:S(2)}, u32[]{:S(2)}) collective-permute-start(bf16[2,272,128]{2,1,0:T(8,128)(2,1)S(1)} %get-tuple-element.59), channel_id=1, source_target_pairs={{0,3},{1,2},{2,1},{3,0},{4,7},{5,6},{6,5},{7,4},{8,11},{9,10},{10,... | collective-permute-start | bytes 417800 | tf_op jit(solution)/shard_map/ppermute | solution.py:431
  37.3 21.0 %collective-permute-start.14 = (bf16[2,272,128]{2,1,0:T(8,128)(2,1)S(1)}, bf16[2,272,128]{2,1,0:T(8,128)(2,1)S(1)}, u32[]{:S(2)}, u32[]{:S(2)}) collective-permute-start(bf16[2,272,128]{2,1,0:T(8,128)(2,1)S(1)} %get-tuple-element.69), channel_id=1, source_target_pairs={{0,4},{1,5},{2,6},{3,7},{4,0},{5,1},{6,2},{7,3},{8,12},{9,13},{10,... | collective-permute-start | bytes 417800 | tf_op jit(solution)/shard_map/ppermute | solution.py:431
  40.8 20.3 %collective-permute-start.15 = (bf16[2,272,128]{2,1,0:T(8,128)(2,1)S(1)}, bf16[2,272,128]{2,1,0:T(8,128)(2,1)S(1)}, u32[]{:S(2)}, u32[]{:S(2)}) collective-permute-start(bf16[2,272,128]{2,1,0:T(8,128)(2,1)S(1)} %get-tuple-element.70), channel_id=1, source_target_pairs={{0,5},{1,4},{2,7},{3,6},{4,1},{5,0},{6,3},{7,2},{8,13},{9,12},{10,... | collective-permute-start | bytes 417800 | tf_op jit(solution)/shard_map/ppermute | solution.py:431
  43.4 23.6 %collective-permute-start.1 = (bf16[2,272,128]{2,1,0:T(8,128)(2,1)S(1)}, bf16[2,272,128]{2,1,0:T(8,128)(2,1)S(1)}, u32[]{:S(2)}, u32[]{:S(2)}) collective-permute-start(bf16[2,272,128]{2,1,0:T(8,128)(2,1)S(1)} %get-tuple-element.54), channel_id=1, source_target_pairs={{0,6},{1,7},{2,4},{3,5},{4,2},{5,3},{6,0},{7,1},{8,14},{9,15},{10,... | collective-permute-start | bytes 417800 | tf_op jit(solution)/shard_map/ppermute | solution.py:431
  49.2 17.8 %collective-permute-start.2 = (bf16[2,272,128]{2,1,0:T(8,128)(2,1)S(1)}, bf16[2,272,128]{2,1,0:T(8,128)(2,1)S(1)}, u32[]{:S(2)}, u32[]{:S(2)}) collective-permute-start(bf16[2,272,128]{2,1,0:T(8,128)(2,1)S(1)} %get-tuple-element.55), channel_id=1, source_target_pairs={{0,7},{1,6},{2,5},{3,4},{4,3},{5,2},{6,1},{7,0},{8,15},{9,14},{10,... | collective-permute-start | bytes 417800 | tf_op jit(solution)/shard_map/ppermute | solution.py:431
  73.0 4.5 %collective-permute-start.19 = (bf16[4096,128]{1,0:T(8,128)(2,1)S(1)}, bf16[4096,128]{1,0:T(8,128)(2,1)S(1)}, u32[]{:S(2)}, u32[]{:S(2)}) collective-permute-start(bf16[4096,128]{1,0:T(8,128)(2,1)S(1)} %get-tuple-element.78), channel_id=1, source_target_pairs={{0,8},{8,0},{1,9},{9,1},{2,10},{10,2},{3,11},{11,3},{4,12},{12,4},... | collective-permute-start | bytes 3145736 | tf_op jit(solution)/shard_map/ppermute | solution.py:431
  73.0 11.1 %collective-permute-start.16 = (bf16[4,256,128]{2,1,0:T(8,128)(2,1)S(1)}, bf16[4,256,128]{2,1,0:T(8,128)(2,1)S(1)}, u32[]{:S(2)}, u32[]{:S(2)}) collective-permute-start(bf16[4,256,128]{2,1,0:T(8,128)(2,1)S(1)} %get-tuple-element.73), channel_id=1, source_target_pairs={{0,6},{2,4},{4,2},{6,0},{1,7},{3,5},{5,3},{7,1},{8,14},{10,12},{12... | collective-permute-start | bytes 786440 | tf_op jit(solution)/shard_map/ppermute | solution.py:431
  73.1 25.9 %collective-permute-start.17 = (bf16[4,256,128]{2,1,0:T(8,128)(2,1)S(1)}, bf16[4,256,128]{2,1,0:T(8,128)(2,1)S(1)}, u32[]{:S(2)}, u32[]{:S(2)}) collective-permute-start(bf16[4,256,128]{2,1,0:T(8,128)(2,1)S(1)} %get-tuple-element.74), channel_id=1, source_target_pairs={{0,4},{2,6},{4,0},{6,2},{1,5},{3,7},{5,1},{7,3},{8,12},{10,14},{12... | collective-permute-start | bytes 786440 | tf_op jit(solution)/shard_map/ppermute | solution.py:431
  73.6 25.4 %collective-permute-start.18 = (bf16[4,256,128]{2,1,0:T(8,128)(2,1)S(1)}, bf16[4,256,128]{2,1,0:T(8,128)(2,1)S(1)}, u32[]{:S(2)}, u32[]{:S(2)}) collective-permute-start(bf16[4,256,128]{2,1,0:T(8,128)(2,1)S(1)} %get-tuple-element.75), channel_id=1, source_target_pairs={{0,2},{2,0},{4,6},{6,4},{1,3},{3,1},{5,7},{7,5},{8,10},{10,8},{12,... | collective-permute-start | bytes 786440 | tf_op jit(solution)/shard_map/ppermute | solution.py:431
  78.2 34.2 %collective-permute-start.20 = (bf16[512,128]{1,0:T(8,128)(2,1)S(1)}, bf16[512,128]{1,0:T(8,128)(2,1)S(1)}, u32[]{:S(2)}, u32[]{:S(2)}) collective-permute-start(bf16[512,128]{1,0:T(8,128)(2,1)S(1)} %get-tuple-element.90), channel_id=1, source_target_pairs={{0,7},{1,6},{2,5},{3,4},{4,11},{5,10},{6,9},{7,8},{8,3},{9,2},{10,... | collective-permute-start | bytes 393224 | tf_op jit(solution)/shard_map/ppermute | solution.py:457
  78.9 33.5 %collective-permute-start.21 = (bf16[512,128]{1,0:T(8,128)(2,1)S(1)}, bf16[512,128]{1,0:T(8,128)(2,1)S(1)}, u32[]{:S(2)}, u32[]{:S(2)}) collective-permute-start(bf16[512,128]{1,0:T(8,128)(2,1)S(1)} %get-tuple-element.91), channel_id=1, source_target_pairs={{0,6},{1,7},{2,4},{3,5},{4,10},{5,11},{6,8},{7,9},{8,2},{9,3},{10,... | collective-permute-start | bytes 393224 | tf_op jit(solution)/shard_map/ppermute | solution.py:457
  84.1 28.9 %collective-permute-start.22 = (bf16[512,128]{1,0:T(8,128)(2,1)S(1)}, bf16[512,128]{1,0:T(8,128)(2,1)S(1)}, u32[]{:S(2)}, u32[]{:S(2)}) collective-permute-start(bf16[512,128]{1,0:T(8,128)(2,1)S(1)} %get-tuple-element.92), channel_id=1, source_target_pairs={{0,5},{1,4},{2,7},{3,6},{4,9},{5,8},{6,11},{7,10},{8,1},{9,0},{10,... | collective-permute-start | bytes 393224 | tf_op jit(solution)/shard_map/ppermute | solution.py:457
  100.7 24.1 %all-to-all-start = ((bf16[4,4,256,128]{3,2,1,0:T(8,128)(2,1)}), bf16[4,4,256,128]{3,2,1,0:T(8,128)(2,1)S(1)}, u32[]{:S(2)}, u32[]{:S(2)}) async-start(bf16[4,4,256,128]{3,2,1,0:T(8,128)(2,1)} %join_planes.1), calls=%async_computation | async-start | bytes 2097152 | tf_op jit(solution)/shard_map/all_to_all | solution.py:496
  106.4 7.3 %collective-permute-start.23 = (bf16[512,128]{1,0:T(8,128)(2,1)S(1)}, bf16[512,128]{1,0:T(8,128)(2,1)S(1)}, u32[]{:S(2)}, u32[]{:S(2)}) collective-permute-start(bf16[512,128]{1,0:T(8,128)(2,1)S(1)} %get-tuple-element.93), channel_id=1, source_target_pairs={{0,4},{1,5},{2,6},{3,7},{4,8},{5,9},{6,10},{7,11},{8,0},{9,1},{10,... | collective-permute-start | bytes 393224 | tf_op jit(solution)/shard_map/ppermute | solution.py:457
  108.3 11.6 %collective-permute-start.24 = (bf16[512,128]{1,0:T(8,128)(2,1)S(1)}, bf16[512,128]{1,0:T(8,128)(2,1)S(1)}, u32[]{:S(2)}, u32[]{:S(2)}) collective-permute-start(bf16[512,128]{1,0:T(8,128)(2,1)S(1)} %get-tuple-element.94), channel_id=1, source_target_pairs={{0,3},{1,2},{2,1},{3,0},{4,15},{5,14},{6,13},{7,12},{8,7},{9,6},{1... | collective-permute-start | bytes 393224 | tf_op jit(solution)/shard_map/ppermute | solution.py:457
  112.4 8.4 %collective-permute-start.25 = (bf16[512,128]{1,0:T(8,128)(2,1)S(1)}, bf16[512,128]{1,0:T(8,128)(2,1)S(1)}, u32[]{:S(2)}, u32[]{:S(2)}) collective-permute-start(bf16[512,128]{1,0:T(8,128)(2,1)S(1)} %get-tuple-element.95), channel_id=1, source_target_pairs={{0,2},{1,3},{2,0},{3,1},{4,14},{5,15},{6,12},{7,13},{8,6},{9,7},{1... | collective-permute-start | bytes 393224 | tf_op jit(solution)/shard_map/ppermute | solution.py:457
  112.4 10.7 %collective-permute-start.26 = (bf16[512,128]{1,0:T(8,128)(2,1)S(1)}, bf16[512,128]{1,0:T(8,128)(2,1)S(1)}, u32[]{:S(2)}, u32[]{:S(2)}) collective-permute-start(bf16[512,128]{1,0:T(8,128)(2,1)S(1)} %get-tuple-element.96), channel_id=1, source_target_pairs={{0,1},{1,0},{2,3},{3,2},{4,13},{5,12},{6,15},{7,14},{8,5},{9,4},{1... | collective-permute-start | bytes 393224 | tf_op jit(solution)/shard_map/ppermute | solution.py:457
  113.0 10.0 %collective-permute-start.27 = (bf16[512,128]{1,0:T(8,128)(2,1)S(1)}, bf16[512,128]{1,0:T(8,128)(2,1)S(1)}, u32[]{:S(2)}, u32[]{:S(2)}) collective-permute-start(bf16[512,128]{1,0:T(8,128)(2,1)S(1)} %get-tuple-element.97), channel_id=1, source_target_pairs={{0,0},{1,1},{2,2},{3,3},{4,12},{5,13},{6,14},{7,15},{8,4},{9,5},{1... | collective-permute-start | bytes 393224 | tf_op jit(solution)/shard_map/ppermute | solution.py:457

commit v6 on v5

--- a/solution.py
+++ b/solution.py
@@ -130,11 +130,12 @@
     def kernel(place, queries, cotangent, block_lists, tile_lengths, *refs):
         *outs, words = refs
         odd = (place[2] & 1) == 1
-        words[...] = jnp.zeros_like(words)
-        words[:tiles, :slots] = block_lists[...]
-        words[:tiles, slots : slots + 1] = tile_lengths[...]
-        meta = words[...].astype(jnp.float32).astype(jnp.bfloat16)
         for k in range(parts):
+            lists = slice(k * tiles, (k + 1) * tiles)
+            words[...] = jnp.zeros_like(words)
+            words[lists, :slots] = block_lists[...]
+            words[lists, slots : slots + 1] = tile_lengths[...]
+            meta = words[...].astype(jnp.float32).astype(jnp.bfloat16)
             base = (place[0] ^ k) * (dims // 2)
             for i in range(dims // 2):
                 span = pair_lanes(base, place, i)
@@ -155,14 +156,23 @@
 
 def merge_fact(parts):
     dims, rows, _ = parts[0].shape
+    rows -= META_ROWS
+    count = len(parts)
 
     def kernel(*refs):
         for r in range(dims):
-            for k in range(len(parts)):
-                refs[len(parts) + r][k] = refs[k][r]
-
-    return call(
-        kernel, "merge_fact", [bf16(len(parts), rows, LANES)] * dims, [VMEM] * len(parts), cost=2
+            out = refs[count + r]
+            for k in range(count):
+                out[k * rows : (k + 1) * rows, :] = refs[k][r, :rows, :]
+            lists = [refs[k][r, rows:, :].astype(jnp.float32) for k in range(count)]
+            out[count * rows :, :] = functools.reduce(jnp.add, lists).astype(jnp.bfloat16)
+
+    return call(
+        kernel,
+        "merge_fact",
+        [bf16(count * rows + META_ROWS, LANES)] * dims,
+        [VMEM] * count,
+        cost=4,
     )(*parts)
 
 
@@ -180,7 +190,7 @@
 
 def attend(place, facts, tables, total, rows, slots, dims, shares, ys, last, cost):
     count = len(facts)
-    parts = facts[0].shape[0]
+    parts = (facts[0].shape[0] - META_ROWS) // rows
     sources = count * parts
     table_rows = sum(t.shape[0] for t in tables) // shares
     owner_blocks = table_rows // TILE // dims
@@ -208,13 +218,12 @@
         fact, fact_out, words, meta, order, sem = refs
         odd = place[2] & 1
         for r in range(count):
-            words[r * parts : (r + 1) * parts] = (
-                facts_in[r][:, rows:, :].astype(jnp.float32).astype(jnp.int32)
-            )
+            words[r] = facts_in[r][parts * rows :, :].astype(jnp.float32).astype(jnp.int32)
         copy = pltpu.make_async_copy(words, meta, sem)
         copy.start()
         for r in range(count):
-            fact[r * parts : (r + 1) * parts] = facts_in[r][:, :rows, :]
+            for i in range(parts):
+                fact[r * parts + i] = facts_in[r][i * rows : (i + 1) * rows, :]
         if begin:
             for k in range(shares):
                 table[k * table_rows : (k + 1) * table_rows, :] = tables_in[k][...]
@@ -231,7 +240,11 @@
             return pl.multiple_of(index * TILE, TILE)
 
         tiles = sources * tiles_each
-        lengths = [meta[t // tiles_each, t % tiles_each, slots] for t in range(tiles)]
+
+        def word(t, j):
+            return meta[t // (parts * tiles_each), t % (parts * tiles_each), j]
+
+        lengths = [word(t, slots) for t in range(tiles)]
         ranks = [jnp.int32(0)] * tiles
         for t in range(tiles):
             for u in range(t):
@@ -253,9 +266,8 @@
                         [jnp.where(first, both, zero), jnp.where(first, zero, both)], axis=0
                     )
                 )
-                tile = t % tiles_each
-                places.append([row_of(meta[source, tile, j]) for j in range(longest)])
-                live.append(meta[source, tile, slots])
+                places.append([row_of(word(t, j)) for j in range(longest)])
+                live.append(word(t, slots))
             kept = []
             for g in range(GROUP):
                 kv = jnp.concatenate([table[pl.ds(at, TILE), :] for at in places[g]], axis=0)
@@ -295,8 +307,7 @@
                     sums[pl.ds(at, TILE), :] += grads[j * TILE : (j + 1) * TILE]
 
         def group_step(index, carry):
-            first_tile = order[index * GROUP]
-            longest = meta[first_tile // tiles_each, first_tile % tiles_each, slots]
+            longest = word(order[index * GROUP], slots)
             for below, length in zip((0,) + COUNTS, COUNTS):
                 pl.when((longest > below) & (longest <= length))(
                     functools.partial(step, index, length)
@@ -342,8 +353,8 @@
         + [
             pltpu.VMEM((sources, rows, LANES), jnp.bfloat16),
             pltpu.VMEM((sources, rows, LANES), jnp.bfloat16),
-            pltpu.VMEM((sources, META_ROWS, LANES), jnp.int32),
-            pltpu.SMEM((sources, META_ROWS, LANES), jnp.int32),
+            pltpu.VMEM((count, META_ROWS, LANES), jnp.int32),
+            pltpu.SMEM((count, META_ROWS, LANES), jnp.int32),
             pltpu.SMEM((sources * tiles_each,), jnp.int32),
             pltpu.SemaphoreType.DMA,
         ],

time: 127 us -> 128 us (level)
  waiting for transfers between devices: 35.6 us -> 37.8 us
    ppermute x8, starting transfers between devices: 20 us -> 23.9 us  [to_columns(): return lax.ppermute(chunk, ('share', 'z', 'y'), pairs)]
    ppermute x20, starting transfers between devices: 35.1 us -> 32.9 us  [by_xor(): return lax.ppermute(part, axis, [(i, i ^ index) for i in range(count)])]
    all_to_all x1, starting transfers between devices: 5.71 us -> 3.66 us  [body(): lax.all_to_all(fact_out, ('x', 'y'), split_axis=0, concat_axis=0, tiled=T...]
    ppermute x8, waiting for transfers between devices: 9.36 us -> 11.4 us  [to_columns(): return lax.ppermute(chunk, ('share', 'z', 'y'), pairs)]
where the time goes in v6:
time: 128 us
  starting transfers between devices  60.5 us (47%)
  waiting for transfers between devices  37.8 us (30%)
  Pallas kernels  28.6 us (22%)
    ppermute x20, starting transfers between devices, by_xor(): return lax.ppermute(part, axis, [(i, i ^ index) for i in range(count)])  32.9 us
    ppermute x20, waiting for transfers between devices, by_xor(): return lax.ppermute(part, axis, [(i, i ^ index) for i in range(count)])  26.4 us
    ppermute x8, starting transfers between devices, to_columns(): return lax.ppermute(chunk, ('share', 'z', 'y'), pairs)  23.9 us
    pallas_call x3, Pallas kernels, attend(): call(kernel, 'attend', outs, [SMEM] + [VMEM] * (count + len(tables) + len...  19.7 us
    ppermute x8, waiting for transfers between devices, to_columns(): return lax.ppermute(chunk, ('share', 'z', 'y'), pairs)  11.4 us
    all_to_all x1, starting transfers between devices, body(): lax.all_to_all(fact_out, ('x', 'y'), split_axis=0, concat_axis=0, tiled=T...  3.66 us
  transfers between devices with their start and end apart: 29, of which 10 were waited for; matrix products, arithmetic and copies ran while one was open for 0% of the time, Pallas kernels for 15%

profile of v6, /device:TPU:0, one launch (start us, length us, event | category | flops | bytes accessed | tf_op | source)
XLA Modules:
  0.0 127.9 jit_solution(4155412662401591443)
XLA Ops:
  0.7 2.5 %pack_dimension.1 = (bf16[512,128]{1,0:T(8,128)(2,1)}, bf16[512,128]{1,0:T(8,128)(2,1)}, bf16[512,128]{1,0:T(8,128)(2,1)}, bf16[512,128]{1,0:T(8,128)(2,1)}, bf1...) custom-call(bf16[1024,1024]{1,0:T(8,128)(2,1)} %keys_in.1, ...), custom_call_target="tpu_custom_call" | custom-call | tf_op jit(solution)/shard_map/pack_dimension/pallas_call | solution.py:114
  3.2 3.0 %collective-permute-start.6 = (bf16[512,128]{1,0:T(8,128)(2,1)}, bf16[512,128]{1,0:T(8,128)(2,1)S(1)}, u32[]{:S(2)}, u32[]{:S(2)}) collective-permute-start(bf16[512,128]{1,0:T(8,128)(2,1)} %get-tuple-element.61), channel_id=1, source_target_pairs={{0,1},{1,0},{2,3},{3,2},{4,5},{5,4},{6,7},{7,6},{8,9},{9,8},{10,11... | collective-permute-start | bytes 393224 | tf_op jit(solution)/shard_map/ppermute | solution.py:442
  6.2 1.6 %collective-permute-start.7 = (bf16[512,128]{1,0:T(8,128)(2,1)}, bf16[512,128]{1,0:T(8,128)(2,1)S(1)}, u32[]{:S(2)}, u32[]{:S(2)}) collective-permute-start(bf16[512,128]{1,0:T(8,128)(2,1)} %get-tuple-element.62), channel_id=1, source_target_pairs={{0,2},{1,3},{2,0},{3,1},{4,6},{5,7},{6,4},{7,5},{8,10},{9,11},{10,... | collective-permute-start | bytes 393224 | tf_op jit(solution)/shard_map/ppermute | solution.py:442
  7.8 3.0 %collective-permute-start.9 = (bf16[512,128]{1,0:T(8,128)(2,1)}, bf16[512,128]{1,0:T(8,128)(2,1)S(1)}, u32[]{:S(2)}, u32[]{:S(2)}) collective-permute-start(bf16[512,128]{1,0:T(8,128)(2,1)} %get-tuple-element.64), channel_id=1, source_target_pairs={{0,4},{1,5},{2,6},{3,7},{4,0},{5,1},{6,2},{7,3},{8,12},{9,13},{10,... | collective-permute-start | bytes 393224 | tf_op jit(solution)/shard_map/ppermute | solution.py:442
  10.8 1.3 %collective-permute-start.10 = (bf16[512,128]{1,0:T(8,128)(2,1)}, bf16[512,128]{1,0:T(8,128)(2,1)S(1)}, u32[]{:S(2)}, u32[]{:S(2)}) collective-permute-start(bf16[512,128]{1,0:T(8,128)(2,1)} %get-tuple-element.65), channel_id=1, source_target_pairs={{0,5},{1,4},{2,7},{3,6},{4,1},{5,0},{6,3},{7,2},{8,13},{9,12},{10,... | collective-permute-start | bytes 393224 | tf_op jit(solution)/shard_map/ppermute | solution.py:442
  12.1 3.6 %collective-permute-start.11 = (bf16[512,128]{1,0:T(8,128)(2,1)}, bf16[512,128]{1,0:T(8,128)(2,1)S(1)}, u32[]{:S(2)}, u32[]{:S(2)}) collective-permute-start(bf16[512,128]{1,0:T(8,128)(2,1)} %get-tuple-element.66), channel_id=1, source_target_pairs={{0,6},{1,7},{2,4},{3,5},{4,2},{5,3},{6,0},{7,1},{8,14},{9,15},{10,... | collective-permute-start | bytes 393224 | tf_op jit(solution)/shard_map/ppermute | solution.py:442
  15.7 1.5 %collective-permute-done.7.refs_2_ = bf16[512,128]{1,0:T(8,128)(2,1)S(1)} collective-permute-done((bf16[512,128]{1,0:T(8,128)(2,1)}, bf16[512,128]{1,0:T(8,128)(2,1)S(1)}, u32[]{:S(2)}, u32[]{:S(2)}) %collective-permute-start.7) | collective-permute-done | bytes 131104 | tf_op jit(solution)/shard_map/ppermute | solution.py:442
  17.2 0.7 collective-permute-start.12
  17.8 0.1 copy.10.tile_lengths
  17.9 0.1 stack.23.place
  18.0 1.0 pack_fact.1
  19.0 1.6 %collective-permute-start = (bf16[8,272,128]{2,1,0:T(8,128)(2,1)S(1)}, bf16[8,272,128]{2,1,0:T(8,128)(2,1)S(1)}, u32[]{:S(2)}, u32[]{:S(2)}) collective-permute-start(bf16[8,272,128]{2,1,0:T(8,128)(2,1)S(1)} %get-tuple-element.53), channel_id=1, source_target_pairs={{0,16},{16,0},{1,17},{17,1},{2,18},{18,2},{3,19},{19,3},{4,20},{20... | collective-permute-start | bytes 1671176 | tf_op jit(solution)/shard_map/ppermute | solution.py:442
  20.6 9.9 %collective-permute-done.10.refs_5_ = bf16[512,128]{1,0:T(8,128)(2,1)S(1)} collective-permute-done((bf16[512,128]{1,0:T(8,128)(2,1)}, bf16[512,128]{1,0:T(8,128)(2,1)S(1)}, u32[]{:S(2)}, u32[]{:S(2)}) %collective-permute-start.10) | collective-permute-done | bytes 131104 | tf_op jit(solution)/shard_map/ppermute | solution.py:442
  30.5 0.1 stack_chunks.1.refs_4_
  30.5 0.1 collective-permute-start.13
  30.6 0.8 collective-permute-done.refs_1_
  31.4 0.1 merge_fact.1
  31.5 1.8 %collective-permute-start.3 = (bf16[528,128]{1,0:T(8,128)(2,1)S(1)}, bf16[528,128]{1,0:T(8,128)(2,1)S(1)}, u32[]{:S(2)}, u32[]{:S(2)}) collective-permute-start(bf16[528,128]{1,0:T(8,128)(2,1)S(1)} %get-tuple-element.57), channel_id=1, source_target_pairs={{0,1},{1,0},{2,3},{3,2},{4,5},{5,4},{6,7},{7,6},{8,9},{9,8},{10,11... | collective-permute-start | bytes 405512 | tf_op jit(solution)/shard_map/ppermute | solution.py:442
  33.3 2.8 %collective-permute-start.4 = (bf16[528,128]{1,0:T(8,128)(2,1)S(1)}, bf16[528,128]{1,0:T(8,128)(2,1)S(1)}, u32[]{:S(2)}, u32[]{:S(2)}) collective-permute-start(bf16[528,128]{1,0:T(8,128)(2,1)S(1)} %get-tuple-element.58), channel_id=1, source_target_pairs={{0,2},{1,3},{2,0},{3,1},{4,6},{5,7},{6,4},{7,5},{8,10},{9,11},{10,... | collective-permute-start | bytes 405512 | tf_op jit(solution)/shard_map/ppermute | solution.py:442
  36.2 1.1 collective-permute-start.5
  37.3 3.5 %collective-permute-start.14 = (bf16[528,128]{1,0:T(8,128)(2,1)S(1)}, bf16[528,128]{1,0:T(8,128)(2,1)S(1)}, u32[]{:S(2)}, u32[]{:S(2)}) collective-permute-start(bf16[528,128]{1,0:T(8,128)(2,1)S(1)} %get-tuple-element.69), channel_id=1, source_target_pairs={{0,4},{1,5},{2,6},{3,7},{4,0},{5,1},{6,2},{7,3},{8,12},{9,13},{10,... | collective-permute-start | bytes 405512 | tf_op jit(solution)/shard_map/ppermute | solution.py:442
  40.8 2.5 %collective-permute-start.15 = (bf16[528,128]{1,0:T(8,128)(2,1)S(1)}, bf16[528,128]{1,0:T(8,128)(2,1)S(1)}, u32[]{:S(2)}, u32[]{:S(2)}) collective-permute-start(bf16[528,128]{1,0:T(8,128)(2,1)S(1)} %get-tuple-element.70), channel_id=1, source_target_pairs={{0,5},{1,4},{2,7},{3,6},{4,1},{5,0},{6,3},{7,2},{8,13},{9,12},{10,... | collective-permute-start | bytes 405512 | tf_op jit(solution)/shard_map/ppermute | solution.py:442
  43.3 0.6 collective-permute-start.1
  43.9 4.9 %collective-permute-done.5.refs_3_ = bf16[528,128]{1,0:T(8,128)(2,1)S(1)} collective-permute-done((bf16[528,128]{1,0:T(8,128)(2,1)S(1)}, bf16[528,128]{1,0:T(8,128)(2,1)S(1)}, u32[]{:S(2)}, u32[]{:S(2)}) %collective-permute-start.5) | collective-permute-done | bytes 135200 | tf_op jit(solution)/shard_map/ppermute | solution.py:442
  48.8 1.2 collective-permute-start.2
  50.0 9.7 %attend.3 = (bf16[4,256,128]{2,1,0:T(8,128)(2,1)S(1)}, bf16[4,256,128]{2,1,0:T(8,128)(2,1)S(1)}, f32[8192,128]{1,0:T(8,128)S(1)}, bf16[8192,128]{1,0:T(8,128)(2,1)S(1)}) custom-call(s32[5]{0:T(128)S(1)} %stack.23.place, bf16[528,128]{1,0:T(8,128)(2,1)S(1)} %get-tuple-element.56.refs_0_, bf16[528,128]{1,0:T(8,128)(2,1)S(1)} %collective-permute-done.3.refs_1_, ...), custom_call_target="tpu_custom_call" | custom-call | tf_op jit(solution)/shard_map/attend/pallas_call | solution.py:345
  59.8 0.9 collective-permute-done.15.refs_1_
  60.7 4.2 %attend.4 = (bf16[4,256,128]{2,1,0:T(8,128)(2,1)S(1)}, f32[8192,128]{1,0:T(8,128)S(1)}) custom-call(s32[5]{0:T(128)S(1)} %stack.23.place, bf16[528,128]{1,0:T(8,128)(2,1)S(1)} %collective-permute-done.14.refs_0_, bf16[528,128]{1,0:T(8,128)(2,1)S(1)} %collective-permute-done.15.refs_1_, bf16[8192,128]{1,0:T(8,128)(2,1)S(1)} %get-tuple-element.68.refs_2_, ...), custom_call_target="tpu_custom_call" | custom-call | tf_op jit(solution)/shard_map/attend/pallas_call | solution.py:345
  65.0 5.8 %attend.5 = (bf16[4,256,128]{2,1,0:T(8,128)(2,1)S(1)}, f32[4096,128]{1,0:T(8,128)S(1)}, bf16[4096,128]{1,0:T(8,128)(2,1)S(1)}) custom-call(s32[5]{0:T(128)S(1)} %stack.23.place, bf16[528,128]{1,0:T(8,128)(2,1)S(1)} %collective-permute-done.1.refs_0_, bf16[528,128]{1,0:T(8,128)(2,1)S(1)} %collective-permute-done.2.refs_1_, ...), custom_call_target="tpu_custom_call" | custom-call | flops 69000003584 | tf_op jit(solution)/shard_map/attend/pallas_call | solution.py:345
  70.7 0.1 collective-permute-start.19
  70.8 3.3 %collective-permute-start.16 = (bf16[4,256,128]{2,1,0:T(8,128)(2,1)S(1)}, bf16[4,256,128]{2,1,0:T(8,128)(2,1)S(1)}, u32[]{:S(2)}, u32[]{:S(2)}) collective-permute-start(bf16[4,256,128]{2,1,0:T(8,128)(2,1)S(1)} %get-tuple-element.73), channel_id=1, source_target_pairs={{0,6},{2,4},{4,2},{6,0},{1,7},{3,5},{5,3},{7,1},{8,14},{10,12},{12... | collective-permute-start | bytes 786440 | tf_op jit(solution)/shard_map/ppermute | solution.py:442
  74.1 1.2 collective-permute-start.18
  75.3 0.8 sum_shares.1
  76.1 4.2 %collective-permute-start.20 = (bf16[512,128]{1,0:T(8,128)(2,1)S(1)}, bf16[512,128]{1,0:T(8,128)(2,1)S(1)}, u32[]{:S(2)}, u32[]{:S(2)}) collective-permute-start(bf16[512,128]{1,0:T(8,128)(2,1)S(1)} %get-tuple-element.90), channel_id=1, source_target_pairs={{0,7},{1,6},{2,5},{3,4},{4,11},{5,10},{6,9},{7,8},{8,3},{9,2},{10,... | collective-permute-start | bytes 393224 | tf_op jit(solution)/shard_map/ppermute | solution.py:468
  80.3 1.7 %collective-permute-done.16.refs_0_ = bf16[4,256,128]{2,1,0:T(8,128)(2,1)S(1)} collective-permute-done((bf16[4,256,128]{2,1,0:T(8,128)(2,1)S(1)}, bf16[4,256,128]{2,1,0:T(8,128)(2,1)S(1)}, u32[]{:S(2)}, u32[]{:S(2)}) %collective-permute-start.16) | collective-permute-done | bytes 262176 | tf_op jit(solution)/shard_map/ppermute | solution.py:442
  81.9 11.7 %collective-permute-start.22 = (bf16[512,128]{1,0:T(8,128)(2,1)S(1)}, bf16[512,128]{1,0:T(8,128)(2,1)S(1)}, u32[]{:S(2)}, u32[]{:S(2)}) collective-permute-start(bf16[512,128]{1,0:T(8,128)(2,1)S(1)} %get-tuple-element.92), channel_id=1, source_target_pairs={{0,5},{1,4},{2,7},{3,6},{4,9},{5,8},{6,11},{7,10},{8,1},{9,0},{10,... | collective-permute-start | bytes 393224 | tf_op jit(solution)/shard_map/ppermute | solution.py:468
  93.7 6.7 %collective-permute-done.17.refs_1_ = bf16[4,256,128]{2,1,0:T(8,128)(2,1)S(1)} collective-permute-done((bf16[4,256,128]{2,1,0:T(8,128)(2,1)S(1)}, bf16[4,256,128]{2,1,0:T(8,128)(2,1)S(1)}, u32[]{:S(2)}, u32[]{:S(2)}) %collective-permute-start.17) | collective-permute-done | bytes 262176 | tf_op jit(solution)/shard_map/ppermute | solution.py:442
  100.4 1.6 %join_planes.1 = bf16[4,4,256,128]{3,2,1,0:T(8,128)(2,1)} custom-call(s32[5]{0:T(128)S(1)} %stack.23.place, bf16[4,256,128]{2,1,0:T(8,128)(2,1)S(1)} %collective-permute-done.16.refs_0_, bf16[4,256,128]{2,1,0:T(8,128)(2,1)S(1)} %collective-permute-done.17.refs_1_, bf16[4,256,128]{2,1,0:T(8,128)(2,1)S(1)} %collective-permute-done.18.refs_2_, ...), custom_call_target="tpu_custom_call" | custom-call | tf_op jit(solution)/shard_map/join_planes/pallas_call | solution.py:376
  102.0 3.7 %all-to-all-start = ((bf16[4,4,256,128]{3,2,1,0:T(8,128)(2,1)}), bf16[4,4,256,128]{3,2,1,0:T(8,128)(2,1)S(1)}, u32[]{:S(2)}, u32[]{:S(2)}) async-start(bf16[4,4,256,128]{3,2,1,0:T(8,128)(2,1)} %join_planes.1), calls=%async_computation | async-start | bytes 2097152 | tf_op jit(solution)/shard_map/all_to_all | solution.py:507
  105.7 1.9 %collective-permute-start.23 = (bf16[512,128]{1,0:T(8,128)(2,1)S(1)}, bf16[512,128]{1,0:T(8,128)(2,1)S(1)}, u32[]{:S(2)}, u32[]{:S(2)}) collective-permute-start(bf16[512,128]{1,0:T(8,128)(2,1)S(1)} %get-tuple-element.93), channel_id=1, source_target_pairs={{0,4},{1,5},{2,6},{3,7},{4,8},{5,9},{6,10},{7,11},{8,0},{9,1},{10,... | collective-permute-start | bytes 393224 | tf_op jit(solution)/shard_map/ppermute | solution.py:468
  107.6 4.7 %collective-permute-start.24 = (bf16[512,128]{1,0:T(8,128)(2,1)S(1)}, bf16[512,128]{1,0:T(8,128)(2,1)S(1)}, u32[]{:S(2)}, u32[]{:S(2)}) collective-permute-start(bf16[512,128]{1,0:T(8,128)(2,1)S(1)} %get-tuple-element.94), channel_id=1, source_target_pairs={{0,3},{1,2},{2,1},{3,0},{4,15},{5,14},{6,13},{7,12},{8,7},{9,6},{1... | collective-permute-start | bytes 393224 | tf_op jit(solution)/shard_map/ppermute | solution.py:468
  112.3 0.6 collective-permute-start.26
  113.0 0.7 collective-permute-start.27
  113.6 5.0 %collective-permute-done.24.refs_4_ = bf16[512,128]{1,0:T(8,128)(2,1)S(1)} collective-permute-done((bf16[512,128]{1,0:T(8,128)(2,1)S(1)}, bf16[512,128]{1,0:T(8,128)(2,1)S(1)}, u32[]{:S(2)}, u32[]{:S(2)}) %collective-permute-start.24) | collective-permute-done | bytes 131104 | tf_op jit(solution)/shard_map/ppermute | solution.py:468
  118.7 1.4 %collective-permute-done.25.refs_5_ = bf16[512,128]{1,0:T(8,128)(2,1)S(1)} collective-permute-done((bf16[512,128]{1,0:T(8,128)(2,1)S(1)}, bf16[512,128]{1,0:T(8,128)(2,1)S(1)}, u32[]{:S(2)}, u32[]{:S(2)}) %collective-permute-start.25) | collective-permute-done | bytes 131104 | tf_op jit(solution)/shard_map/ppermute | solution.py:468
  120.0 5.0 %collective-permute-done.26.refs_6_ = bf16[512,128]{1,0:T(8,128)(2,1)S(1)} collective-permute-done((bf16[512,128]{1,0:T(8,128)(2,1)S(1)}, bf16[512,128]{1,0:T(8,128)(2,1)S(1)}, u32[]{:S(2)}, u32[]{:S(2)}) %collective-permute-start.26) | collective-permute-done | bytes 131104 | tf_op jit(solution)/shard_map/ppermute | solution.py:468
  125.0 1.7 %unpack_dimension.1 = (bf16[1024,256]{1,0:T(8,128)(2,1)}, bf16[1024,256]{1,0:T(8,128)(2,1)}) custom-call(s32[5]{0:T(128)S(1)} %stack.23.place, bf16[512,128]{1,0:T(8,128)(2,1)S(1)} %collective-permute-done.20.refs_0_, bf16[512,128]{1,0:T(8,128)(2,1)S(1)} %collective-permute-done.21.refs_1_, bf16[512,128]{1,0:T(8,128)(2,1)S(1)} %collective-permute-done.22.refs_2_, ...), custom_call_target="tpu_custom_call" | custom-call | flops 5750000128 | tf_op jit(solution)/shard_map/unpack_dimension/pallas_call | solution.py:430
  126.7 1.1 unpack_fact.1
  (33 shorter events, 0.1 us)
Async XLA Ops:
  0.6 17.2 %copy-start.4 = (s32[2]{0:T(128)S(1)}, s32[2]{0:T(128)}, u32[]{:S(2)}) copy-start(s32[2]{0:T(128)} %param.11) | copy-start | bytes 28
  0.6 17.4 %copy-start.3 = (s32[2,8]{1,0:T(2,128)S(1)}, s32[2,8]{1,0:T(2,128)}, u32[]{:S(2)}) copy-start(s32[2,8]{1,0:T(2,128)} %block_lists.1) | copy-start | bytes 196
  0.7 17.4 %copy-start.1 = (bf16[256,1024]{1,0:T(8,128)(2,1)S(1)}, bf16[256,1024]{1,0:T(8,128)(2,1)}, u32[]{:S(2)}) copy-start(bf16[256,1024]{1,0:T(8,128)(2,1)} %cotangent.1) | copy-start | bytes 1572868
  0.7 17.4 %copy-start = (bf16[256,1024]{1,0:T(8,128)(2,1)S(1)}, bf16[256,1024]{1,0:T(8,128)(2,1)}, u32[]{:S(2)}) copy-start(bf16[256,1024]{1,0:T(8,128)(2,1)} %queries.1) | copy-start | bytes 1572868
  3.2 8.9 %collective-permute-start.6 = (bf16[512,128]{1,0:T(8,128)(2,1)}, bf16[512,128]{1,0:T(8,128)(2,1)S(1)}, u32[]{:S(2)}, u32[]{:S(2)}) collective-permute-start(bf16[512,128]{1,0:T(8,128)(2,1)} %get-tuple-element.61), channel_id=1, source_target_pairs={{0,1},{1,0},{2,3},{3,2},{4,5},{5,4},{6,7},{7,6},{8,9},{9,8},{10,11... | collective-permute-start | bytes 393224 | tf_op jit(solution)/shard_map/ppermute | solution.py:442
  6.2 10.9 %collective-permute-start.7 = (bf16[512,128]{1,0:T(8,128)(2,1)}, bf16[512,128]{1,0:T(8,128)(2,1)S(1)}, u32[]{:S(2)}, u32[]{:S(2)}) collective-permute-start(bf16[512,128]{1,0:T(8,128)(2,1)} %get-tuple-element.62), channel_id=1, source_target_pairs={{0,2},{1,3},{2,0},{3,1},{4,6},{5,7},{6,4},{7,5},{8,10},{9,11},{10,... | collective-permute-start | bytes 393224 | tf_op jit(solution)/shard_map/ppermute | solution.py:442
  7.8 11.2 %collective-permute-start.8 = (bf16[512,128]{1,0:T(8,128)(2,1)}, bf16[512,128]{1,0:T(8,128)(2,1)S(1)}, u32[]{:S(2)}, u32[]{:S(2)}) collective-permute-start(bf16[512,128]{1,0:T(8,128)(2,1)} %get-tuple-element.63), channel_id=1, source_target_pairs={{0,3},{1,2},{2,1},{3,0},{4,7},{5,6},{6,5},{7,4},{8,11},{9,10},{10,... | collective-permute-start | bytes 393224 | tf_op jit(solution)/shard_map/ppermute | solution.py:442
  7.8 12.8 %collective-permute-start.9 = (bf16[512,128]{1,0:T(8,128)(2,1)}, bf16[512,128]{1,0:T(8,128)(2,1)S(1)}, u32[]{:S(2)}, u32[]{:S(2)}) collective-permute-start(bf16[512,128]{1,0:T(8,128)(2,1)} %get-tuple-element.64), channel_id=1, source_target_pairs={{0,4},{1,5},{2,6},{3,7},{4,0},{5,1},{6,2},{7,3},{8,12},{9,13},{10,... | collective-permute-start | bytes 393224 | tf_op jit(solution)/shard_map/ppermute | solution.py:442
  10.8 19.7 %collective-permute-start.10 = (bf16[512,128]{1,0:T(8,128)(2,1)}, bf16[512,128]{1,0:T(8,128)(2,1)S(1)}, u32[]{:S(2)}, u32[]{:S(2)}) collective-permute-start(bf16[512,128]{1,0:T(8,128)(2,1)} %get-tuple-element.65), channel_id=1, source_target_pairs={{0,5},{1,4},{2,7},{3,6},{4,1},{5,0},{6,3},{7,2},{8,13},{9,12},{10,... | collective-permute-start | bytes 393224 | tf_op jit(solution)/shard_map/ppermute | solution.py:442
  12.1 18.4 %collective-permute-start.11 = (bf16[512,128]{1,0:T(8,128)(2,1)}, bf16[512,128]{1,0:T(8,128)(2,1)S(1)}, u32[]{:S(2)}, u32[]{:S(2)}) collective-permute-start(bf16[512,128]{1,0:T(8,128)(2,1)} %get-tuple-element.66), channel_id=1, source_target_pairs={{0,6},{1,7},{2,4},{3,5},{4,2},{5,3},{6,0},{7,1},{8,14},{9,15},{10,... | collective-permute-start | bytes 393224 | tf_op jit(solution)/shard_map/ppermute | solution.py:442
  17.2 13.3 %collective-permute-start.12 = (bf16[512,128]{1,0:T(8,128)(2,1)}, bf16[512,128]{1,0:T(8,128)(2,1)S(1)}, u32[]{:S(2)}, u32[]{:S(2)}) collective-permute-start(bf16[512,128]{1,0:T(8,128)(2,1)} %get-tuple-element.67), channel_id=1, source_target_pairs={{0,7},{1,6},{2,5},{3,4},{4,3},{5,2},{6,1},{7,0},{8,15},{9,14},{10,... | collective-permute-start | bytes 393224 | tf_op jit(solution)/shard_map/ppermute | solution.py:442
  18.0 12.4 %copy-start.2 = (bf16[512,128]{1,0:T(8,128)(2,1)S(1)}, bf16[512,128]{1,0:T(8,128)(2,1)}, u32[]{:S(2)}) copy-start(bf16[512,128]{1,0:T(8,128)(2,1)} %get-tuple-element.60.refs_0_) | copy-start | bytes 393220
  19.0 12.4 %collective-permute-start = (bf16[8,272,128]{2,1,0:T(8,128)(2,1)S(1)}, bf16[8,272,128]{2,1,0:T(8,128)(2,1)S(1)}, u32[]{:S(2)}, u32[]{:S(2)}) collective-permute-start(bf16[8,272,128]{2,1,0:T(8,128)(2,1)S(1)} %get-tuple-element.53), channel_id=1, source_target_pairs={{0,16},{16,0},{1,17},{17,1},{2,18},{18,2},{3,19},{19,3},{4,20},{20... | collective-permute-start | bytes 1671176 | tf_op jit(solution)/shard_map/ppermute | solution.py:442
  30.5 19.5 %collective-permute-start.13 = (bf16[4096,128]{1,0:T(8,128)(2,1)S(1)}, bf16[4096,128]{1,0:T(8,128)(2,1)S(1)}, u32[]{:S(2)}, u32[]{:S(2)}) collective-permute-start(bf16[4096,128]{1,0:T(8,128)(2,1)S(1)} %stack_chunks.1.refs_4_), channel_id=1, source_target_pairs={{0,8},{8,0},{1,9},{9,1},{2,10},{10,2},{3,11},{11,3},{4,12},{12,4},... | collective-permute-start | bytes 3145736 | tf_op jit(solution)/shard_map/ppermute | solution.py:442
  31.5 9.3 %collective-permute-start.3 = (bf16[528,128]{1,0:T(8,128)(2,1)S(1)}, bf16[528,128]{1,0:T(8,128)(2,1)S(1)}, u32[]{:S(2)}, u32[]{:S(2)}) collective-permute-start(bf16[528,128]{1,0:T(8,128)(2,1)S(1)} %get-tuple-element.57), channel_id=1, source_target_pairs={{0,1},{1,0},{2,3},{3,2},{4,5},{5,4},{6,7},{7,6},{8,9},{9,8},{10,11... | collective-permute-start | bytes 405512 | tf_op jit(solution)/shard_map/ppermute | solution.py:442
  33.3 10.0 %collective-permute-start.4 = (bf16[528,128]{1,0:T(8,128)(2,1)S(1)}, bf16[528,128]{1,0:T(8,128)(2,1)S(1)}, u32[]{:S(2)}, u32[]{:S(2)}) collective-permute-start(bf16[528,128]{1,0:T(8,128)(2,1)S(1)} %get-tuple-element.58), channel_id=1, source_target_pairs={{0,2},{1,3},{2,0},{3,1},{4,6},{5,7},{6,4},{7,5},{8,10},{9,11},{10,... | collective-permute-start | bytes 405512 | tf_op jit(solution)/shard_map/ppermute | solution.py:442
  36.2 12.7 %collective-permute-start.5 = (bf16[528,128]{1,0:T(8,128)(2,1)S(1)}, bf16[528,128]{1,0:T(8,128)(2,1)S(1)}, u32[]{:S(2)}, u32[]{:S(2)}) collective-permute-start(bf16[528,128]{1,0:T(8,128)(2,1)S(1)} %get-tuple-element.59), channel_id=1, source_target_pairs={{0,3},{1,2},{2,1},{3,0},{4,7},{5,6},{6,5},{7,4},{8,11},{9,10},{10,... | collective-permute-start | bytes 405512 | tf_op jit(solution)/shard_map/ppermute | solution.py:442
  37.3 22.5 %collective-permute-start.14 = (bf16[528,128]{1,0:T(8,128)(2,1)S(1)}, bf16[528,128]{1,0:T(8,128)(2,1)S(1)}, u32[]{:S(2)}, u32[]{:S(2)}) collective-permute-start(bf16[528,128]{1,0:T(8,128)(2,1)S(1)} %get-tuple-element.69), channel_id=1, source_target_pairs={{0,4},{1,5},{2,6},{3,7},{4,0},{5,1},{6,2},{7,3},{8,12},{9,13},{10,... | collective-permute-start | bytes 405512 | tf_op jit(solution)/shard_map/ppermute | solution.py:442
  40.8 19.9 %collective-permute-start.15 = (bf16[528,128]{1,0:T(8,128)(2,1)S(1)}, bf16[528,128]{1,0:T(8,128)(2,1)S(1)}, u32[]{:S(2)}, u32[]{:S(2)}) collective-permute-start(bf16[528,128]{1,0:T(8,128)(2,1)S(1)} %get-tuple-element.70), channel_id=1, source_target_pairs={{0,5},{1,4},{2,7},{3,6},{4,1},{5,0},{6,3},{7,2},{8,13},{9,12},{10,... | collective-permute-start | bytes 405512 | tf_op jit(solution)/shard_map/ppermute | solution.py:442
  43.3 21.6 %collective-permute-start.1 = (bf16[528,128]{1,0:T(8,128)(2,1)S(1)}, bf16[528,128]{1,0:T(8,128)(2,1)S(1)}, u32[]{:S(2)}, u32[]{:S(2)}) collective-permute-start(bf16[528,128]{1,0:T(8,128)(2,1)S(1)} %get-tuple-element.54), channel_id=1, source_target_pairs={{0,6},{1,7},{2,4},{3,5},{4,2},{5,3},{6,0},{7,1},{8,14},{9,15},{10,... | collective-permute-start | bytes 405512 | tf_op jit(solution)/shard_map/ppermute | solution.py:442
  48.8 16.1 %collective-permute-start.2 = (bf16[528,128]{1,0:T(8,128)(2,1)S(1)}, bf16[528,128]{1,0:T(8,128)(2,1)S(1)}, u32[]{:S(2)}, u32[]{:S(2)}) collective-permute-start(bf16[528,128]{1,0:T(8,128)(2,1)S(1)} %get-tuple-element.55), channel_id=1, source_target_pairs={{0,7},{1,6},{2,5},{3,4},{4,3},{5,2},{6,1},{7,0},{8,15},{9,14},{10,... | collective-permute-start | bytes 405512 | tf_op jit(solution)/shard_map/ppermute | solution.py:442
  70.7 4.5 %collective-permute-start.19 = (bf16[4096,128]{1,0:T(8,128)(2,1)S(1)}, bf16[4096,128]{1,0:T(8,128)(2,1)S(1)}, u32[]{:S(2)}, u32[]{:S(2)}) collective-permute-start(bf16[4096,128]{1,0:T(8,128)(2,1)S(1)} %get-tuple-element.78), channel_id=1, source_target_pairs={{0,8},{8,0},{1,9},{9,1},{2,10},{10,2},{3,11},{11,3},{4,12},{12,4},... | collective-permute-start | bytes 3145736 | tf_op jit(solution)/shard_map/ppermute | solution.py:442
  70.8 11.1 %collective-permute-start.16 = (bf16[4,256,128]{2,1,0:T(8,128)(2,1)S(1)}, bf16[4,256,128]{2,1,0:T(8,128)(2,1)S(1)}, u32[]{:S(2)}, u32[]{:S(2)}) collective-permute-start(bf16[4,256,128]{2,1,0:T(8,128)(2,1)S(1)} %get-tuple-element.73), channel_id=1, source_target_pairs={{0,6},{2,4},{4,2},{6,0},{1,7},{3,5},{5,3},{7,1},{8,14},{10,12},{12... | collective-permute-start | bytes 786440 | tf_op jit(solution)/shard_map/ppermute | solution.py:442
  74.1 26.3 %collective-permute-start.17 = (bf16[4,256,128]{2,1,0:T(8,128)(2,1)S(1)}, bf16[4,256,128]{2,1,0:T(8,128)(2,1)S(1)}, u32[]{:S(2)}, u32[]{:S(2)}) collective-permute-start(bf16[4,256,128]{2,1,0:T(8,128)(2,1)S(1)} %get-tuple-element.74), channel_id=1, source_target_pairs={{0,4},{2,6},{4,0},{6,2},{1,5},{3,7},{5,1},{7,3},{8,12},{10,14},{12... | collective-permute-start | bytes 786440 | tf_op jit(solution)/shard_map/ppermute | solution.py:442
  74.1 26.3 %collective-permute-start.18 = (bf16[4,256,128]{2,1,0:T(8,128)(2,1)S(1)}, bf16[4,256,128]{2,1,0:T(8,128)(2,1)S(1)}, u32[]{:S(2)}, u32[]{:S(2)}) collective-permute-start(bf16[4,256,128]{2,1,0:T(8,128)(2,1)S(1)} %get-tuple-element.75), channel_id=1, source_target_pairs={{0,2},{2,0},{4,6},{6,4},{1,3},{3,1},{5,7},{7,5},{8,10},{10,8},{12,... | collective-permute-start | bytes 786440 | tf_op jit(solution)/shard_map/ppermute | solution.py:442
  76.1 36.3 %collective-permute-start.20 = (bf16[512,128]{1,0:T(8,128)(2,1)S(1)}, bf16[512,128]{1,0:T(8,128)(2,1)S(1)}, u32[]{:S(2)}, u32[]{:S(2)}) collective-permute-start(bf16[512,128]{1,0:T(8,128)(2,1)S(1)} %get-tuple-element.90), channel_id=1, source_target_pairs={{0,7},{1,6},{2,5},{3,4},{4,11},{5,10},{6,9},{7,8},{8,3},{9,2},{10,... | collective-permute-start | bytes 393224 | tf_op jit(solution)/shard_map/ppermute | solution.py:468
  80.2 32.1 %collective-permute-start.21 = (bf16[512,128]{1,0:T(8,128)(2,1)S(1)}, bf16[512,128]{1,0:T(8,128)(2,1)S(1)}, u32[]{:S(2)}, u32[]{:S(2)}) collective-permute-start(bf16[512,128]{1,0:T(8,128)(2,1)S(1)} %get-tuple-element.91), channel_id=1, source_target_pairs={{0,6},{1,7},{2,4},{3,5},{4,10},{5,11},{6,8},{7,9},{8,2},{9,3},{10,... | collective-permute-start | bytes 393224 | tf_op jit(solution)/shard_map/ppermute | solution.py:468
  81.9 31.0 %collective-permute-start.22 = (bf16[512,128]{1,0:T(8,128)(2,1)S(1)}, bf16[512,128]{1,0:T(8,128)(2,1)S(1)}, u32[]{:S(2)}, u32[]{:S(2)}) collective-permute-start(bf16[512,128]{1,0:T(8,128)(2,1)S(1)} %get-tuple-element.92), channel_id=1, source_target_pairs={{0,5},{1,4},{2,7},{3,6},{4,9},{5,8},{6,11},{7,10},{8,1},{9,0},{10,... | collective-permute-start | bytes 393224 | tf_op jit(solution)/shard_map/ppermute | solution.py:468
  102.0 24.7 %all-to-all-start = ((bf16[4,4,256,128]{3,2,1,0:T(8,128)(2,1)}), bf16[4,4,256,128]{3,2,1,0:T(8,128)(2,1)S(1)}, u32[]{:S(2)}, u32[]{:S(2)}) async-start(bf16[4,4,256,128]{3,2,1,0:T(8,128)(2,1)} %join_planes.1), calls=%async_computation | async-start | bytes 2097152 | tf_op jit(solution)/shard_map/all_to_all | solution.py:507
  105.7 7.9 %collective-permute-start.23 = (bf16[512,128]{1,0:T(8,128)(2,1)S(1)}, bf16[512,128]{1,0:T(8,128)(2,1)S(1)}, u32[]{:S(2)}, u32[]{:S(2)}) collective-permute-start(bf16[512,128]{1,0:T(8,128)(2,1)S(1)} %get-tuple-element.93), channel_id=1, source_target_pairs={{0,4},{1,5},{2,6},{3,7},{4,8},{5,9},{6,10},{7,11},{8,0},{9,1},{10,... | collective-permute-start | bytes 393224 | tf_op jit(solution)/shard_map/ppermute | solution.py:468
  107.6 11.1 %collective-permute-start.24 = (bf16[512,128]{1,0:T(8,128)(2,1)S(1)}, bf16[512,128]{1,0:T(8,128)(2,1)S(1)}, u32[]{:S(2)}, u32[]{:S(2)}) collective-permute-start(bf16[512,128]{1,0:T(8,128)(2,1)S(1)} %get-tuple-element.94), channel_id=1, source_target_pairs={{0,3},{1,2},{2,1},{3,0},{4,15},{5,14},{6,13},{7,12},{8,7},{9,6},{1... | collective-permute-start | bytes 393224 | tf_op jit(solution)/shard_map/ppermute | solution.py:468
  112.3 7.7 %collective-permute-start.25 = (bf16[512,128]{1,0:T(8,128)(2,1)S(1)}, bf16[512,128]{1,0:T(8,128)(2,1)S(1)}, u32[]{:S(2)}, u32[]{:S(2)}) collective-permute-start(bf16[512,128]{1,0:T(8,128)(2,1)S(1)} %get-tuple-element.95), channel_id=1, source_target_pairs={{0,2},{1,3},{2,0},{3,1},{4,14},{5,15},{6,12},{7,13},{8,6},{9,7},{1... | collective-permute-start | bytes 393224 | tf_op jit(solution)/shard_map/ppermute | solution.py:468
  112.3 12.7 %collective-permute-start.26 = (bf16[512,128]{1,0:T(8,128)(2,1)S(1)}, bf16[512,128]{1,0:T(8,128)(2,1)S(1)}, u32[]{:S(2)}, u32[]{:S(2)}) collective-permute-start(bf16[512,128]{1,0:T(8,128)(2,1)S(1)} %get-tuple-element.96), channel_id=1, source_target_pairs={{0,1},{1,0},{2,3},{3,2},{4,13},{5,12},{6,15},{7,14},{8,5},{9,4},{1... | collective-permute-start | bytes 393224 | tf_op jit(solution)/shard_map/ppermute | solution.py:468
  113.0 12.1 %collective-permute-start.27 = (bf16[512,128]{1,0:T(8,128)(2,1)S(1)}, bf16[512,128]{1,0:T(8,128)(2,1)S(1)}, u32[]{:S(2)}, u32[]{:S(2)}) collective-permute-start(bf16[512,128]{1,0:T(8,128)(2,1)S(1)} %get-tuple-element.97), channel_id=1, source_target_pairs={{0,0},{1,1},{2,2},{3,3},{4,12},{5,13},{6,14},{7,15},{8,4},{9,5},{1... | collective-permute-start | bytes 393224 | tf_op jit(solution)/shard_map/ppermute | solution.py:468
